TPU v7x, 128 devices: a whole 4x4x4 slice. The times are simulated.
128 devices in a mesh: dp: 64 (over y, z_lo, x, core), mp: 2 (over z_hi).
Axes of the slice: x: 4, y: 4, z: 4 (z_hi: 2, z_lo: 2; z = z_hi * 2 + z_lo), core: 2. Of those that a mesh axis runs over, the one named last changes fastest.
Arguments:
- tokens: bfloat16 [8192, 2560], P('dp'), may hold values from -6 to 6
- attn_gain: bfloat16 [2560], P('dp'), may hold values from 0.099609375 to 1.8984375
- query_weight: bfloat16 [2560, 2560], P('dp', 'mp'), may hold values from -0.125 to 0.125
- kv_weight: bfloat16 [2560, 512], P('dp'), may hold values from -0.125 to 0.125
- out_weight: bfloat16 [2560, 2560], P('mp', 'dp'), may hold values from -0.625 to 0.625
- mlp_gain: bfloat16 [2560], P('dp'), may hold values from 0.099609375 to 1.8984375
- gate_weight: bfloat16 [2560, 7680], P('dp', 'mp'), may hold values from -0.125 to 0.125
- up_weight: bfloat16 [2560, 7680], P('dp', 'mp'), may hold values from -0.125 to 0.125
- down_weight: bfloat16 [7680, 2560], P('mp', 'dp'), may hold values from -0.0625 to 0.0625
- cotangent: bfloat16 [8192, 2560], P('dp'), may hold values from -16 to 16
Outputs:
- block_out: bfloat16 [8192, 2560], P('dp')
- tokens_grad: bfloat16 [8192, 2560], P('dp')
- attn_gain_grad: float32 [2560], P('dp')
- query_weight_grad: float32 [2560, 2560], P('dp', 'mp')
- kv_weight_grad: float32 [2560, 512], P('dp')
- out_weight_grad: float32 [2560, 2560], P('mp', 'dp')
- mlp_gain_grad: float32 [2560], P('dp')
- gate_weight_grad: float32 [2560, 7680], P('dp', 'mp')
- up_weight_grad: float32 [2560, 7680], P('dp', 'mp')
- down_weight_grad: float32 [7680, 2560], P('mp', 'dp')
All inputs are finite; a program needn't handle non-finite values.
Results may differ from a plain program's by a relative error of at most 0.017.
Values may be sent and summed in bfloat16 or wider, within the bound.
A program may use at most 448 MiB of HBM per device.

v0:
```python
import math

import jax
import jax.numpy as jnp
from jax import lax
from jax.sharding import PartitionSpec as P

HEAD_DIM = 256
WINDOW = 2048
SEQ_LEN = 128
ROT = 128


norm_eps = 1e-06


def turned_gather(arrays, axis, dims):
    turned = [jnp.moveaxis(a, dim, 0) for a, dim in zip(arrays, dims)]
    widths = [t[0].size for t in turned]
    both = jnp.concatenate([t.reshape(-1, w) for t, w in zip(turned, widths)], axis=1)
    filled = lax.all_gather(both, axis, axis=0, tiled=True)
    pieces = jnp.split(filled, [sum(widths[:k]) for k in range(1, len(widths))], axis=1)
    return tuple(
        (
            jnp.moveaxis(b.reshape(-1, *t.shape[1:]), 0, dim)
            for b, t, dim in zip(pieces, turned, dims)
        )
    )


def copy_for_each(value, axis):
    copies = jnp.broadcast_to(value, (lax.axis_size(axis), *value.shape))
    return lax.all_to_all(copies, axis, split_axis=0, concat_axis=0, tiled=True)


def taken_together(value, axis):
    return copy_for_each(value, axis).astype(jnp.float32).sum(axis=0)


def sent_together(arrays, axis, dim, along):
    columns = [a.reshape(*a.shape[:along], -1) for a in arrays]
    both = jnp.concatenate(columns, axis=along)
    filled, at, gathered = (lax.psum_scatter(both, axis, scatter_dimension=dim, tiled=True), 0, [])
    for a, column in zip(arrays, columns):
        piece = filled[..., at : at + column.shape[along]]
        gathered.append(piece.reshape(*piece.shape[:along], *a.shape[along:]))
        at += column.shape[along]
    return tuple(gathered)


def in_blocks(value, dim, size):
    lengths = value.shape
    pieces = value.reshape(*lengths[:dim], size, lengths[dim] // size, *lengths[dim + 1 :])
    return jnp.moveaxis(pieces, dim, 0)


def sum_together(arrays, axis, dims):
    size = lax.axis_size(axis)
    pieces = [in_blocks(a, dim, size) for a, dim in zip(arrays, dims)]
    lines = jnp.concatenate([b.reshape(size, -1) for b in pieces], axis=1)
    span = max(16, -(-lines.shape[1] // 1024) * 8)
    lines = jnp.pad(lines, ((0, 0), (0, span * 128 - lines.shape[1]))).reshape(-1, 128)
    flat, at, gathered = (lax.psum_scatter(lines, axis, tiled=True).reshape(-1), 0, [])
    for b in pieces:
        part = b[0]
        gathered.append(flat[at : at + part.size].reshape(part.shape))
        at += part.size
    return tuple(gathered)


def rms_norm(values, gain_row):
    return (
        values * lax.rsqrt(jnp.mean(values * values, axis=-1, keepdims=True) + norm_eps) * gain_row
    )


def geglu(gate_part, up_part):
    return jax.nn.gelu(gate_part) * up_part


def tables():
    half_rot = ROT // 2
    rates = jnp.exp(jnp.arange(half_rot, dtype=jnp.float32) * (-2.0 * math.log(10000.0) / ROT))
    angles = jnp.arange(SEQ_LEN, dtype=jnp.float32)[:, None] * rates[None, :]
    return (jnp.cos(angles), jnp.sin(angles))


def rotate(field, cosine, sine):
    half_rot = ROT // 2
    first = field[..., :half_rot]
    second = field[..., half_rot:ROT]
    return jnp.concatenate(
        [first * cosine - second * sine, second * cosine + first * sine, field[..., ROT:]], axis=-1
    )


def contract(left, right, left_dim, right_dim):
    return lax.dot_general(
        left, right, (((left_dim,), (right_dim,)), ((), ())), preferred_element_type=jnp.float32
    )


def local(
    tokens,
    attn_gain,
    query_weight,
    kv_weight,
    out_weight,
    mlp_gain,
    gate_weight,
    up_weight,
    down_weight,
    cotangent,
):
    rows = tokens.shape[0]
    seqs = rows // SEQ_LEN
    heads_here = query_weight.shape[1] // HEAD_DIM
    scale = HEAD_DIM ** (-0.5)
    cosine, sine = tables()
    positions = jnp.arange(SEQ_LEN)
    keep_mask = (positions[:, None] >= positions[None, :]) & (
        positions[:, None] - positions[None, :] < WINDOW
    )
    gain_one, w_query, w_kv, w_out = turned_gather(
        (attn_gain, query_weight, kv_weight, out_weight), "dp", (0, 0, 0, 1)
    )
    x_in = tokens.astype(jnp.float32)
    xn_one = rms_norm(x_in, gain_one.astype(jnp.float32)).astype(jnp.bfloat16)
    q_pre = jnp.dot(xn_one, w_query, preferred_element_type=jnp.float32)
    kv_pre = jnp.dot(xn_one, w_kv, preferred_element_type=jnp.float32)
    queries = rotate(
        q_pre.reshape(seqs, SEQ_LEN, heads_here, HEAD_DIM), cosine[:, None, :], sine[:, None, :]
    ).astype(jnp.bfloat16)
    key_rot = rotate(kv_pre[:, :HEAD_DIM].reshape(seqs, SEQ_LEN, HEAD_DIM), cosine, sine).astype(
        jnp.bfloat16
    )
    value_rows = kv_pre[:, HEAD_DIM:].reshape(seqs, SEQ_LEN, HEAD_DIM).astype(jnp.bfloat16)

    def score_rows():
        raw = (
            jnp.einsum("sqhd,skd->shqk", queries, key_rot, preferred_element_type=jnp.float32)
            * scale
        )
        return jnp.where(keep_mask, raw, -1e30)

    scores = score_rows()
    row_max = jnp.max(scores, axis=-1, keepdims=True)
    log_total = row_max + jnp.log(jnp.sum(jnp.exp(scores - row_max), axis=-1, keepdims=True))
    attn_probs = jnp.exp(scores - log_total).astype(jnp.bfloat16)
    mixed_heads = jnp.einsum(
        "shqk,skd->sqhd", attn_probs, value_rows, preferred_element_type=jnp.float32
    )
    mixed_heads = mixed_heads.reshape(rows, heads_here * HEAD_DIM).astype(jnp.bfloat16)
    attn_branch = taken_together(
        jnp.dot(mixed_heads, w_out, preferred_element_type=jnp.float32).astype(jnp.bfloat16), "mp"
    ).astype(jnp.float32)
    x_mid = x_in + attn_branch
    gain_two, w_gate, w_up, w_down = turned_gather(
        (mlp_gain, gate_weight, up_weight, down_weight), "dp", (0, 0, 0, 1)
    )
    xn_two = rms_norm(x_mid, gain_two.astype(jnp.float32)).astype(jnp.bfloat16)
    gate_pre = jnp.dot(xn_two, w_gate, preferred_element_type=jnp.float32)
    up_pre = jnp.dot(xn_two, w_up, preferred_element_type=jnp.float32)
    hidden = geglu(gate_pre, up_pre).astype(jnp.bfloat16)
    down_branch = taken_together(
        jnp.dot(hidden, w_down, preferred_element_type=jnp.float32).astype(jnp.bfloat16), "mp"
    ).astype(jnp.float32)
    block_out = (x_mid + down_branch).astype(jnp.bfloat16)
    d_down = contract(hidden, cotangent, 0, 0)
    d_hidden = contract(cotangent, w_down, 1, 1)
    geglu_pull = jax.vjp(geglu, gate_pre, up_pre)[1]
    d_gate_pre, d_up_pre = geglu_pull(d_hidden)
    d_gate_low = d_gate_pre.astype(jnp.bfloat16)
    d_up_low = d_up_pre.astype(jnp.bfloat16)
    d_gate_w = contract(xn_two, d_gate_low, 0, 0)
    d_up_w = contract(xn_two, d_up_low, 0, 0)
    d_xn_two_part = contract(d_gate_low, w_gate, 1, 1) + contract(d_up_low, w_up, 1, 1)
    d_xn_two = taken_together(d_xn_two_part.astype(jnp.bfloat16), "mp").astype(jnp.float32)
    norm_two_pull = jax.vjp(rms_norm, x_mid, gain_two.astype(jnp.float32))[1]
    d_mid_norm, d_gain_two = norm_two_pull(d_xn_two)
    mlp_parts = (
        *sent_together((d_gain_two, d_gate_w, d_up_w), "dp", 0, 1),
        lax.psum_scatter(d_down, "dp", scatter_dimension=1, tiled=True),
    )
    d_mid = cotangent.astype(jnp.float32) + d_mid_norm
    d_mid_low = d_mid.astype(jnp.bfloat16)
    d_out_w = contract(mixed_heads, d_mid_low, 0, 0)
    d_mixed = (
        contract(d_mid_low, w_out, 1, 1)
        .astype(jnp.bfloat16)
        .reshape(seqs, SEQ_LEN, heads_here, HEAD_DIM)
    )
    soft_rows = jnp.exp(score_rows() - log_total)
    d_probs = jnp.einsum("sqhd,skd->shqk", d_mixed, value_rows, preferred_element_type=jnp.float32)
    d_scores = (
        soft_rows * (d_probs - jnp.sum(soft_rows * d_probs, axis=-1, keepdims=True))
    ).astype(jnp.bfloat16)
    d_queries = (
        jnp.einsum("shqk,skd->sqhd", d_scores, key_rot, preferred_element_type=jnp.float32) * scale
    )
    d_keys = (
        jnp.einsum("shqk,sqhd->skd", d_scores, queries, preferred_element_type=jnp.float32) * scale
    )
    d_values = jnp.einsum("shqk,sqhd->skd", attn_probs, d_mixed, preferred_element_type=jnp.float32)
    d_q_pre = (
        rotate(d_queries, cosine[:, None, :], -sine[:, None, :])
        .reshape(rows, heads_here * HEAD_DIM)
        .astype(jnp.bfloat16)
    )
    d_k_pre = rotate(d_keys, cosine, -sine).reshape(rows, HEAD_DIM)
    d_kv_part = jnp.concatenate([d_k_pre, d_values.reshape(rows, HEAD_DIM)], axis=-1)
    d_query_w = contract(xn_one, d_q_pre, 0, 0)
    d_xn_one_part = contract(d_q_pre, w_query, 1, 1)
    d_xn_one_q, d_kv_full = (
        taken_together(d_xn_one_part.astype(jnp.bfloat16), "mp").astype(jnp.float32),
        taken_together(d_kv_part.astype(jnp.bfloat16), "mp").astype(jnp.float32),
    )
    d_kv_low = d_kv_full.astype(jnp.bfloat16)
    d_kv_w = contract(xn_one, d_kv_low, 0, 0)
    d_xn_one = d_xn_one_q + contract(d_kv_low, w_kv, 1, 1)
    norm_one_pull = jax.vjp(rms_norm, x_in, gain_one.astype(jnp.float32))[1]
    d_in_norm, d_gain_one = norm_one_pull(d_xn_one)
    tokens_grad = (d_mid + d_in_norm).astype(jnp.bfloat16)
    attn_parts = sum_together((d_gain_one, d_query_w, d_kv_w, d_out_w), "dp", (0, 0, 0, 1))
    return (
        block_out,
        tokens_grad,
        attn_parts[0],
        attn_parts[1],
        attn_parts[2],
        attn_parts[3],
        mlp_parts[0],
        mlp_parts[1],
        mlp_parts[2],
        mlp_parts[3],
    )


def solution(mesh):
    in_specs = (
        P("dp", None),
        P("dp"),
        P("dp", "mp"),
        P("dp", None),
        P("mp", "dp"),
        P("dp"),
        P("dp", "mp"),
        P("dp", "mp"),
        P("mp", "dp"),
        P("dp", None),
    )
    out_specs = (
        P("dp", None),
        P("dp", None),
        P("dp"),
        P("dp", "mp"),
        P("dp", None),
        P("mp", "dp"),
        P("dp"),
        P("dp", "mp"),
        P("dp", "mp"),
        P("mp", "dp"),
    )
    return jax.shard_map(local, mesh=mesh, in_specs=in_specs, out_specs=out_specs, check_vma=False)
```

profile of v0, /device:TPU:1, one launch (start us, length us, event | category | flops | bytes accessed | tf_op | source)
XLA Modules:
  0.0 2412.4 jit_solution(15309965692565526293)
XLA Ops:
  7.2 0.8 copy.112
  8.0 1.9 concatenate.52
  10.0 0.8 copy.119
  10.8 3.4 concatenate.61
  14.7 122.0 %all-gather.3.cloned.1.call-done = bf16[2560,3073]{1,0:T(8,128)(2,1)} async-done(((bf16[40,3073]{1,0:T(8,128)(2,1)}), bf16[2560,3073]{1,0:T(8,128)(2,1)}) %all-gather.3.cloned.1.call-update) | async-done | bytes 15733776 | tf_op jit(solution)/shard_map/all_gather | solution.py:21
  136.7 1.3 convert_reduce_fusion.5
  138.0 8.5 fusion.18
  147.1 3.0 fusion.42
  152.0 6.5 fusion.35
  158.6 36.1 %all_to_all.25 = bf16[2,128,2560]{2,1,0:T(8,128)(2,1)S(1)} all-to-all(bf16[2,128,2560]{2,1,0:T(8,128)(2,1)S(1)} %broadcast_in_dim.26), channel_id=1, replica_groups=mesh['dp'=64,'mp'=2] {'mp'}, dimensions={0} | all-to-all | bytes 2621440 | tf_op jit(solution)/shard_map/all_to_all | solution.py:33
  195.3 279.0 %all-gather.5.cloned.1.call-done = bf16[2560,11521]{1,0:T(8,128)(2,1)} async-done(((bf16[40,11521]{1,0:T(8,128)(2,1)}), bf16[2560,11521]{1,0:T(8,128)(2,1)}) %all-gather.5.cloned.1.call-update) | async-done | bytes 58987536 | tf_op jit(solution)/shard_map/all_gather | solution.py:21
  474.2 1.3 convert_reduce_fusion.4
  475.8 10.7 fusion.20
  486.5 10.4 fusion.6
  496.9 12.8 fusion.50
  509.7 11.9 fusion.4
  521.6 11.3 fusion.29
  532.9 1.2 broadcast_in_dim.28
  534.1 3.8 all-to-all-start.2
  538.0 12.2 fusion.26
  550.2 5.3 all-to-all-done.2
  555.5 2.7 broadcast_in_dim.27
  558.2 4.7 all-to-all-start.1
  562.8 1.6 convert_reduce_fusion.1
  564.5 1.0 multiply_reduce_fusion
  565.5 14.0 all-to-all-done.1
  579.5 1.7 convert_reduce_fusion.2
  581.2 1.7 convert_bitcast_fusion
  582.9 1.1 copy-done.7
  584.0 5.2 fusion.38
  591.8 0.7 broadcast_in_dim.31
  592.5 3.4 all-to-all-start.4
  596.0 6.7 fusion.96
  602.7 7.1 fusion.32
  610.2 2.3 broadcast_in_dim.30
  612.4 4.2 all-to-all-start.3
  616.9 6.6 convolution_bitcast_fusion
  623.5 23.4 copy.131
  646.9 12.2 reshape_reshape.6
  659.1 18.8 copy.133
  677.9 3.3 fusion.94
  681.2 5.6 reshape_reshape.7
  686.8 8.4 copy.134
  695.5 4.9 fusion.54
  700.6 52.9 %pad_maximum_fusion = f32[64,122920]{0,1:T(8,128)} fusion(f32[64,51200]{0,1:T(8,128)} %bitcast.109, f32[64,20480]{0,1:T(8,128)} %copy.134, f32[64,51200]{0,1:T(8,128)} %copy.133, f32[64,40]{0,1:T(8,128)S(1)} %copy.132), kind=kLoop, calls=%fused_computation | loop fusion | flops 23600640 | bytes 62935040 | tf_op jit(solution)/shard_map/concatenate | solution.py:60
  753.5 46.7 %copy.151 = f32[64,122920]{1,0:T(8,128)} copy(f32[64,122920]{0,1:T(8,128)} %pad_maximum_fusion) | data formatting | bytes 62935040
  800.2 21.6 pad.4.clone
  821.8 22.7 reshape.404
  844.8 0.7 copy-done.3
  845.9 15.8 fusion.105
  861.7 15.7 fusion.106
  877.8 90.4 %concatenate.66 = f32[2560,7681]{1,0:T(8,128)} concatenate(f32[2560,1]{1,0:T(8,128)S(1)} %reshape.420, f32[2560,3840]{1,0:T(8,128)} %fusion.105, f32[2560,3840]{1,0:T(8,128)} %fusion.106), dimensions={1} | concatenate | bytes 157306880 | tf_op jit(solution)/shard_map/concatenate | solution.py:42
  968.3 1.0 copy-done.13
  969.6 15.6 fusion.107
  987.3 1.3 fusion.57
  988.6 188.2 %reduce-scatter.8.cloned.1.call-done = f32[968,128]{1,0:T(8,128)} async-done(((f32[61952,128]{1,0:T(8,128)}), f32[968,128]{1,0:T(8,128)}) %reduce-scatter.8.cloned.1.call-update) | async-done | bytes 495632
  1176.7 1.2 slice.103
  1177.9 1.0 slice.105
  1178.9 1.2 fusion.103
  1181.9 0.9 copy.137
  1182.8 871.4 %all-reduce.5.cloned.1.call-done = f32[2560,7681]{1,0:T(8,128)} async-done(((f32[2560,7681]{1,0:T(8,128)}), f32[2560,7681]{1,0:T(8,128)}) %all-reduce.5.cloned.1.call-update) | async-done | bytes 78653456
  2054.2 1.4 dynamic-slice_reduce_fusion
  2055.6 2.7 fusion.101
  2058.3 347.2 %reduce-scatter.6.cloned.1.call-done = f32[3840,40]{0,1:T(8,128)} async-done(((f32[3840,2560]{0,1:T(8,128)}), f32[3840,40]{0,1:T(8,128)}) %reduce-scatter.6.cloned.1.call-update) | async-done | bytes 614416 | tf_op jit(solution)/shard_map/reduce_scatter | solution.py:183
  (134 shorter events, 11.6 us)
Async XLA Ops:
  7.2 7.0 copy-start
  7.2 129.5 %all-gather.3.cloned.1.call-start = ((), (), s32[]{:S(2)}) async-start(), calls=%async_computation.7 | async-start | bytes 16640000 | tf_op jit(solution)/shard_map/all_gather | solution.py:21
  10.0 464.3 %all-gather.5.cloned.1.call-start = ((), (), s32[]{:S(2)}) async-start(), calls=%async_computation.8 | async-start | bytes 60569600 | tf_op jit(solution)/shard_map/all_gather | solution.py:21
  14.4 132.1 %copy-start.35 = (f32[128]{0:T(128)}, f32[128]{0:T(128)S(1)}, u32[]{:S(2)}) copy-start(f32[128]{0:T(128)S(1)} %fusion.58) | copy-start | bytes 1540
  14.4 681.1 %copy-start.32 = (f32[128]{0:T(128)}, f32[128]{0:T(128)S(1)}, u32[]{:S(2)}) copy-start(f32[128]{0:T(128)S(1)} %fusion.89) | copy-start | bytes 1540
  138.0 557.5 %copy-start.23 = (f32[2560]{0:T(1024)}, f32[2560]{0:T(1024)S(1)}, u32[]{:S(2)}) copy-start(f32[2560]{0:T(1024)S(1)} %convert_reduce_fusion.5) | copy-start | bytes 30724
  146.7 3.9 copy-start.29
  150.1 1.8 copy-start.21
  150.6 7.9 copy-start.25
  150.6 7.9 copy-start.27
  150.9 0.7 copy-start.4
  152.0 6.5 copy-start.15
  195.2 280.5 %copy-start.11 = (bf16[128,2560]{1,0:T(8,128)(2,1)S(1)}, bf16[128,2560]{1,0:T(8,128)(2,1)}, u32[]{:S(2)}) copy-start(bf16[128,2560]{1,0:T(8,128)(2,1)} %param.19) | copy-start | bytes 1966084
  475.8 21.1 copy-start.2
  509.7 11.9 copy-start.17
  509.7 11.9 copy-start.19
  534.1 21.3 all-to-all-start.2
  555.5 2.7 copy-start.9
  558.2 21.3 all-to-all-start.1
  579.5 1.7 copy-start.12
  582.9 1.1 copy-start.7
  584.0 5.5 copy-start.5
  584.0 5.5 copy-start.22
  589.2 1.2 copy-start.26
  589.2 1.2 copy-start.28
  589.3 1.2 copy-start.30
  592.5 17.6 all-to-all-start.4
  602.7 7.1 copy-start.10
  610.1 6.7 copy-start.16
  612.4 82.8 %all-to-all-start.3 = ((bf16[2,128,2560]{2,1,0:T(8,128)(2,1)}), bf16[2,128,2560]{2,1,0:T(8,128)(2,1)S(1)}, u32[]{:S(2)}, u32[]{:S(2)}) async-start(bf16[2,128,2560]{2,1,0:T(8,128)(2,1)} %broadcast_in_dim.30), calls=%async_computation.3 | async-start | bytes 2621440 | tf_op jit(solution)/shard_map/all_to_all | solution.py:33
  616.7 560.1 %reduce-scatter.8.cloned.1.call-start = ((), (), s32[]{:S(2)}) async-start(), calls=%async_computation.11 | async-start | bytes 32215040
  844.5 1.1 copy-start.3
  844.5 1.4 copy-start.20
  844.5 17.2 copy-start.18
  844.5 1209.7 %all-reduce.5.cloned.1.call-start = ((), (), s32[]{:S(2)}) async-start(), calls=%async_computation.10 | async-start | bytes 159907840
  861.7 15.7 copy-start.31
  968.2 1.1 copy-start.13
  968.2 1.4 copy-start.14
  968.2 1437.3 %reduce-scatter.6.cloned.1.call-start = ((), (), s32[]{:S(2)}) async-start(), calls=%async_computation.9 | async-start | bytes 39936000 | tf_op jit(solution)/shard_map/reduce_scatter | solution.py:183
  985.3 0.7 copy-start.37
  985.3 1.9 copy-start.34
  985.3 1.9 copy-start.36
  985.3 1.9 copy-start.1
  985.3 1.9 copy-start.6
  985.3 2.0 copy-start.8
  985.3 2.0 copy-start.24
  985.3 2.0 copy-start.33
Sparse Core Ops, SparseCore 0:
  10.3 126.2 all-gather.2
  138.4 335.8 all-gather.4
  844.7 332.0 reduce-scatter.7
  1179.3 874.9 all-reduce.4
  2057.2 348.2 reduce-scatter.5
where the time goes:
time: 2430 us; the launch traced here: 2410 us
  waiting for transfers between devices  1830 us (75%)
  local copies, waits for them, and re-layouts  281 us (12%)
  matrix products  170 us (7%)
  other arithmetic  65.7 us (3%)
  blocking collectives  36.1 us (1%)
    unnamed x7, waiting for transfers between devices  1060 us
    all_gather x2, waiting for transfers between devices, turned_gather(): filled = lax.all_gather(both, axis, axis=0, tiled=True)  401 us
    reduce_scatter x1, waiting for transfers between devices, local(): lax.psum_scatter(d_down, 'dp', scatter_dimension=1, tiled=True)  347 us
    dot_general x12, matrix products, contract(): lax.dot_general(left, right, (((left_dim,), (right_dim,)), ((), ())), pre...  115 us
    concatenate x1, local copies, waits for them, and re-layouts, sent_together(): both = jnp.concatenate(columns, axis=along)  90.4 us
    unnamed x82, local copies, waits for them, and re-layouts  53.6 us
    concatenate x1, other arithmetic, sum_together(): lines = jnp.concatenate([b.reshape(size, -1) for b in pieces], axis=1)  52.9 us
  transfers between devices with their start and end apart: 9, of which 7 were waited for; matrix products, arithmetic and copies ran while one was open for 12% of the time, Pallas kernels for 0%

commit v1 on v0

v1 whole, which is shorter than its diff:
```python
import math

import jax
import jax.numpy as jnp
from jax import lax
from jax.experimental import pallas as pl
from jax.experimental.pallas import tpu as pltpu
from jax.sharding import Mesh
from jax.sharding import PartitionSpec as P

HEAD_DIM = 256
WINDOW = 2048
SEQ_LEN = 128
ROT = 128
AXES = ("y", "zl", "x", "c", "zh")
PLANE = ("y", "x")
GROUP = ("zl", "c")
OWNERS = ("y", "x", "zl", "c")
MESH = pl.DeviceIdType.MESH

norm_eps = 1e-06


def permuted(v):
    n = v.shape[0]
    return v.reshape(n, 4, 2, 4, 80).transpose(0, 1, 3, 2, 4).reshape(n, 2560)


def restored(v):
    n = v.shape[0]
    return v.reshape(n, 4, 4, 2, 80).transpose(0, 1, 3, 2, 4).reshape(n, 2560)


def greet(peers):
    barrier = pltpu.get_barrier_semaphore()
    for peer in peers:
        pl.semaphore_signal(barrier, inc=1, device_id=peer, device_id_type=MESH)
    pl.semaphore_wait(barrier, len(peers))


def remote(src, dst, send, recv, peer):
    return pltpu.make_async_remote_copy(
        src_ref=src, dst_ref=dst, send_sem=send, recv_sem=recv, device_id=peer, device_id_type=MESH
    )


def gather_kernel(x_ref, o_ref, local_sem, send, recv):
    zl, c, zh = lax.axis_index("zl"), lax.axis_index("c"), lax.axis_index("zh")
    half = x_ref.shape[0] // 2
    core = {"c": 1 - c}
    chips = [{"zl": 1 - zl, "zh": k} for k in range(2)]
    greet([core, *chips])
    mine, other = zl * 2 + c, (1 - zl) * 2 + c
    part = pl.ds(pl.multiple_of(zh * half, half), half)
    away = [
        remote(x_ref.at[part], o_ref.at[mine, part], send.at[k], recv.at[zh], chips[k])
        for k in range(2)
    ]
    for copy in away:
        copy.start()
    keep = pltpu.make_async_copy(x_ref, o_ref.at[mine], local_sem)
    keep.start()
    across = remote(x_ref, o_ref.at[mine], send.at[2], recv.at[2], core)
    across.start()
    passed = []
    for k in range(2):
        rows = pl.ds(k * half, half)
        arrived = remote(x_ref.at[rows], o_ref.at[other, rows], send.at[k], recv.at[k], chips[k])
        arrived.wait_recv()
        on = remote(o_ref.at[other, rows], o_ref.at[other, rows], send.at[3 + k], recv.at[3 + k], core)
        on.start()
        passed.append(on)
    for copy in away:
        copy.wait_send()
    across.wait()
    for copy in passed:
        copy.wait()
    keep.wait()


def token_gather(x, cid):
    return pl.pallas_call(
        gather_kernel,
        out_shape=jax.ShapeDtypeStruct((4, *x.shape), x.dtype),
        in_specs=[pl.BlockSpec(memory_space=pltpu.VMEM)],
        out_specs=pl.BlockSpec(memory_space=pltpu.VMEM),
        scratch_shapes=[
            pltpu.SemaphoreType.DMA,
            pltpu.SemaphoreType.DMA((5,)),
            pltpu.SemaphoreType.DMA((5,)),
        ],
        compiler_params=pltpu.CompilerParams(
            collective_id=cid, has_side_effects=True, vmem_limit_bytes=32 * 2**20
        ),
    )(x)


def sum_kernel(p_ref, o_ref, from_core, other, from_chips, own, own_low, from_far, send, recv):
    zl, c, zh = lax.axis_index("zl"), lax.axis_index("c"), lax.axis_index("zh")
    rows = p_ref.shape[1]
    half = rows // 2
    core, far = {"c": 1 - c}, {"zh": 1 - zh}
    chips = [{"zl": 1 - zl, "zh": k} for k in range(2)]
    greet([core, far, *chips])
    order = [1 - zl, zl]
    cores = [
        remote(p_ref.at[z * 2 + 1 - c], from_core.at[i], send.at[i], recv.at[i], core)
        for i, z in enumerate(order)
    ]
    for copy in cores:
        copy.start()
    step = 16
    cores[0].wait_recv()
    aways = []
    for k in range(2):

        @pl.loop(0, half // step)
        def _(j, k=k):
            at = pl.ds(pl.multiple_of(k * half + j * step, step), step)
            total = p_ref[(1 - zl) * 2 + c, at].astype(jnp.float32) + from_core[0, at].astype(jnp.float32)
            other[at] = total.astype(jnp.bfloat16)

        away = remote(
            other.at[pl.ds(k * half, half)], from_chips.at[zh], send.at[2 + k], recv.at[2 + zh], chips[k]
        )
        away.start()
        aways.append(away)
    cores[1].wait_recv()
    fars = []
    for k in range(2):
        piece = (1 - zh) if k == 0 else zh
        if k == 1:
            for i in range(2):
                remote(
                    other.at[pl.ds(0, half)], from_chips.at[i], send.at[2 + i], recv.at[2 + i], chips[i]
                ).wait_recv()

        @pl.loop(0, half // step)
        def _(j, k=k, piece=piece):
            at = pl.ds(pl.multiple_of(piece * half + j * step, step), step)
            total = p_ref[zl * 2 + c, at].astype(jnp.float32) + from_core[1, at].astype(jnp.float32)
            if k == 1:
                here = pl.ds(pl.multiple_of(j * step, step), step)
                total += from_chips[0, here].astype(jnp.float32) + from_chips[1, here].astype(jnp.float32)
            own[at] = total.astype(jnp.bfloat16)

        at = pl.ds(pl.multiple_of(piece * half, half), half)
        copy = remote(own.at[at], from_far.at[at], send.at[4 + k], recv.at[4 + k], far)
        copy.start()
        fars.append(copy)
    for k in range(2):
        fars[k].wait_recv()
        piece = zh if k == 0 else (1 - zh)

        @pl.loop(0, half // step)
        def _(j, piece=piece):
            at = pl.ds(pl.multiple_of(piece * half + j * step, step), step)
            o_ref[at] = own[at].astype(jnp.float32) + from_far[at].astype(jnp.float32)

    for copy in (*cores, *aways, *fars):
        copy.wait_send()


def token_sum(p, cid):
    rows, width = p.shape[1:]
    low = jnp.bfloat16
    return pl.pallas_call(
        sum_kernel,
        out_shape=jax.ShapeDtypeStruct((rows, width), jnp.float32),
        in_specs=[pl.BlockSpec(memory_space=pltpu.VMEM)],
        out_specs=pl.BlockSpec(memory_space=pltpu.VMEM),
        scratch_shapes=[
            pltpu.VMEM((2, rows, width), low),
            pltpu.VMEM((rows, width), low),
            pltpu.VMEM((2, rows // 2, width), low),
            pltpu.VMEM((rows, width), low),
            pltpu.VMEM((rows, width), low),
            pltpu.VMEM((rows, width), low),
            pltpu.SemaphoreType.DMA((6,)),
            pltpu.SemaphoreType.DMA((6,)),
        ],
        compiler_params=pltpu.CompilerParams(
            collective_id=cid, has_side_effects=True, vmem_limit_bytes=32 * 2**20
        ),
    )(p)


def pair_kernel(p_ref, o_ref, landed, send, recv):
    far = {"zh": 1 - lax.axis_index("zh")}
    rows = p_ref.shape[0]
    greet([far])
    copy = remote(p_ref, landed, send, recv, far)
    copy.start()
    copy.wait()
    step = 16

    @pl.loop(0, rows // step)
    def _(j):
        at = pl.ds(pl.multiple_of(j * step, step), step)
        o_ref[at] = p_ref[at].astype(jnp.float32) + landed[at].astype(jnp.float32)


def pair_sum(p, cid):
    return pl.pallas_call(
        pair_kernel,
        out_shape=jax.ShapeDtypeStruct(p.shape, jnp.float32),
        in_specs=[pl.BlockSpec(memory_space=pltpu.VMEM)],
        out_specs=pl.BlockSpec(memory_space=pltpu.VMEM),
        scratch_shapes=[
            pltpu.VMEM(p.shape, p.dtype),
            pltpu.SemaphoreType.DMA,
            pltpu.SemaphoreType.DMA,
        ],
        compiler_params=pltpu.CompilerParams(
            collective_id=cid, has_side_effects=True, vmem_limit_bytes=32 * 2**20
        ),
    )(p)


def ring_of(axis, at):
    return {axis: lax.rem(at + 3, 4)}, {axis: lax.rem(at + 1, 4)}


def block_rows(row, column, start=0, size=160):
    return pl.ds(pl.multiple_of((row * 4 + column) * 160 + start, 16), size)


def exchange_kernel(*refs):
    n = (len(refs) - 3) // 2
    ins, outs, (here, send, recv) = refs[:n], refs[n : 2 * n], refs[2 * n :]
    zl, c = lax.axis_index("zl"), lax.axis_index("c")
    mine = zl * 2 + c
    peers = [({"zl": 1 - zl, "c": k}, (1 - zl) * 2 + k) for k in range(2)]
    peers.append(({"c": 1 - c}, zl * 2 + 1 - c))
    greet([p for p, _ in peers])
    copies = []
    for i in range(n):
        for k, (peer, block) in enumerate(peers):
            slot = i * 3 + k
            landing = i * 3 + (c if k < 2 else 2)
            copies.append(
                remote(ins[i].at[block], outs[i].at[mine], send.at[slot], recv.at[landing], peer)
            )
            copies[-1].start()
    keeps = [pltpu.make_async_copy(ins[i].at[mine], outs[i].at[mine], here.at[i]) for i in range(n)]
    for keep in keeps:
        keep.start()
    for keep in keeps:
        keep.wait()
    for i in range(n):
        for k, (peer, block) in enumerate(peers):
            remote(
                ins[i].at[block], outs[i].at[block], send.at[i * 3 + k], recv.at[i * 3 + k], peer
            ).wait_recv()
    for copy in copies:
        copy.wait_send()


def group_exchange(arrays, cid):
    n = len(arrays)
    return pl.pallas_call(
        exchange_kernel,
        out_shape=[jax.ShapeDtypeStruct(a.shape, a.dtype) for a in arrays],
        in_specs=[pl.BlockSpec(memory_space=pl.ANY)] * n,
        out_specs=[pl.BlockSpec(memory_space=pl.ANY)] * n,
        scratch_shapes=[
            pltpu.SemaphoreType.DMA((n,)),
            pltpu.SemaphoreType.DMA((3 * n,)),
            pltpu.SemaphoreType.DMA((3 * n,)),
        ],
        compiler_params=pltpu.CompilerParams(collective_id=cid, has_side_effects=True),
    )(*arrays)


ATTN, FEED = 768, 512


def plane_gather_kernel(in_ref, dy_ref, a_ref, f_ref, o_ref, here, send, recv, csend, crecv, dsend, drecv):
    y, x, c = lax.axis_index("y"), lax.axis_index("x"), lax.axis_index("c")
    zl, zh = lax.axis_index("zl"), lax.axis_index("zh")
    core = {"c": 1 - c}
    chips = [{"zl": 1 - zl, "zh": k} for k in range(2)]
    greet([*ring_of("x", x), *ring_of("y", y), core, *chips])

    half = dy_ref.shape[0] // 2
    mine, other = zl * 2 + c, (1 - zl) * 2 + c
    part = pl.ds(pl.multiple_of(zh * half, half), half)
    dy_copies = [
        remote(dy_ref.at[part], o_ref.at[mine, part], dsend.at[k], drecv.at[zh], chips[k])
        for k in range(2)
    ]
    dy_copies.append(remote(dy_ref, o_ref.at[mine], dsend.at[2], drecv.at[2], core))
    for copy in dy_copies:
        copy.start()
    keeps = [pltpu.make_async_copy(dy_ref, o_ref.at[mine], here.at[0])]

    def spot(h, kind, start=0, size=160):
        def at(i1, i2):
            row, column = (i2, i1) if h == 0 else (i1, i2)
            rows = block_rows(row, column, start, size)
            if kind == 0:
                return a_ref.at[rows, pl.ds(pl.multiple_of((c * 2 + h) * ATTN, 128), ATTN)]
            return f_ref.at[rows, pl.ds(h * FEED, FEED)]

        return at

    def own(h, kind, start=0, size=160):
        columns = pl.ds(0, ATTN) if kind == 0 else pl.ds(ATTN, FEED)
        return in_ref.at[h, pl.ds(start, size), columns]

    pieces = [(h, kind) for kind in range(2) for h in range(2)]
    for n, (h, kind) in enumerate(pieces):
        i1, i2 = (x, y) if h == 0 else (y, x)
        keeps.append(
            pltpu.make_async_copy(own(h, kind), spot(h, kind)(i1, i2), here.at[1 + n])
        )
    for keep in keeps:
        keep.start()
    started = []

    def go(src, dst, n, ring, slot, peer):
        k = (n * 5 + ring) * 4 + slot
        copy = remote(src, dst, send.at[k], recv.at[k], peer)
        copy.start()
        started.append(copy)

    def arrived(dst, n, ring, slot):
        k = (n * 5 + ring) * 4 + slot
        remote(dst, dst, send.at[k], recv.at[k], core).wait_recv()

    crossed = []

    def cross(n, ref):
        if pieces[n][1] == 0:
            k = len(crossed)
            copy = remote(ref, ref, csend.at[k], crecv.at[k], core)
            copy.start()
            crossed.append(copy)

    def cross_own(n, src, dst):
        if pieces[n][1] == 0:
            k = len(crossed)
            copy = remote(src, dst, csend.at[k], crecv.at[k], core)
            copy.start()
            crossed.append(copy)

    def around(h):
        if h == 0:
            return x, ring_of("x", x), y, ring_of("y", y)
        return y, ring_of("y", y), x, ring_of("x", x)

    def shift(i, by):
        return lax.rem(i + by, 4)

    for n, (h, kind) in enumerate(pieces):
        i1, (back1, ahead1), i2, (back2, ahead2) = around(h)
        place = spot(h, kind)(i1, i2)
        go(own(h, kind), place, n, 0, 0, ahead1)
        go(own(h, kind), place, n, 0, 1, back1)
    for n, (h, kind) in enumerate(pieces):
        i1, (back1, ahead1), i2, (back2, ahead2) = around(h)
        place = spot(h, kind)(i1, i2)
        go(own(h, kind), place, n, 1, 0, ahead2)
        go(own(h, kind), place, n, 1, 1, back2)
        cross_own(n, own(h, kind), place)
    for n, (h, kind) in enumerate(pieces):
        i1, (back1, ahead1), i2, (back2, ahead2) = around(h)
        left, right = spot(h, kind)(shift(i1, 3), i2), spot(h, kind)(shift(i1, 1), i2)
        arrived(left, n, 0, 0)
        low_half = spot(h, kind, 0, 80)(shift(i1, 3), i2)
        go(low_half, low_half, n, 0, 2, ahead1)
        arrived(right, n, 0, 1)
        high_half = spot(h, kind, 80, 80)(shift(i1, 1), i2)
        go(high_half, high_half, n, 0, 3, back1)
        for ring, ref in ((2, left), (3, right)):
            go(ref, ref, n, ring, 0, ahead2)
            go(ref, ref, n, ring, 1, back2)
            cross(n, ref)
    for n, (h, kind) in enumerate(pieces):
        i1, (back1, ahead1), i2, (back2, ahead2) = around(h)
        far = shift(i1, 2)
        arrived(spot(h, kind, 0, 80)(far, i2), n, 0, 2)
        arrived(spot(h, kind, 80, 80)(far, i2), n, 0, 3)
        ref = spot(h, kind)(far, i2)
        go(ref, ref, n, 4, 0, ahead2)
        go(ref, ref, n, 4, 1, back2)
        cross(n, ref)
    firsts = ((1, 0), (2, 3), (3, 1), (4, 2))
    for ring, by in firsts:
        for n, (h, kind) in enumerate(pieces):
            i1, (back1, ahead1), i2, (back2, ahead2) = around(h)
            j = shift(i1, by)
            left, right = spot(h, kind)(j, shift(i2, 3)), spot(h, kind)(j, shift(i2, 1))
            arrived(left, n, ring, 0)
            low_half = spot(h, kind, 0, 80)(j, shift(i2, 3))
            go(low_half, low_half, n, ring, 2, ahead2)
            cross(n, left)
            arrived(right, n, ring, 1)
            high_half = spot(h, kind, 80, 80)(j, shift(i2, 1))
            go(high_half, high_half, n, ring, 3, back2)
            cross(n, right)
    passed = []
    for k in range(2):
        rows = pl.ds(k * half, half)
        remote(dy_ref.at[rows], o_ref.at[other, rows], dsend.at[k], drecv.at[k], chips[k]).wait_recv()
        on = remote(o_ref.at[other, rows], o_ref.at[other, rows], dsend.at[3 + k], drecv.at[3 + k], core)
        on.start()
        passed.append(on)
    for ring, by in firsts:
        for n, (h, kind) in enumerate(pieces):
            i1, (back1, ahead1), i2, (back2, ahead2) = around(h)
            j, far = shift(i1, by), shift(i2, 2)
            arrived(spot(h, kind, 0, 80)(j, far), n, ring, 2)
            arrived(spot(h, kind, 80, 80)(j, far), n, ring, 3)
            cross(n, spot(h, kind)(j, far))
    for copy in crossed:
        copy.wait()
    for copy in passed:
        copy.wait()
    dy_copies[2].wait()
    for copy in (*started, *dy_copies[:2]):
        copy.wait_send()
    for keep in keeps:
        keep.wait()


def plane_gather(own, dy, cid):
    return pl.pallas_call(
        plane_gather_kernel,
        out_shape=[
            jax.ShapeDtypeStruct((2560, 4 * ATTN), own.dtype),
            jax.ShapeDtypeStruct((2560, 2 * FEED), own.dtype),
            jax.ShapeDtypeStruct((4, *dy.shape), dy.dtype),
        ],
        in_specs=[pl.BlockSpec(memory_space=pl.ANY)] * 2,
        out_specs=[pl.BlockSpec(memory_space=pl.ANY)] * 3,
        scratch_shapes=[
            pltpu.SemaphoreType.DMA((5,)),
            pltpu.SemaphoreType.DMA((80,)),
            pltpu.SemaphoreType.DMA((80,)),
            pltpu.SemaphoreType.DMA((32,)),
            pltpu.SemaphoreType.DMA((32,)),
            pltpu.SemaphoreType.DMA((5,)),
            pltpu.SemaphoreType.DMA((5,)),
        ],
        compiler_params=pltpu.CompilerParams(collective_id=cid, has_side_effects=True),
    )(own, dy)


WIDE = ATTN + FEED
SEGMENTS = ((0, 0, 256), (256, 256, 512), (WIDE, 768, 768))


def plane_sum_kernel(
    a_ref, o_ref, f_ref, attn_ref, feed_ref,
    sums, from_core, via, main, from_chip, attn_low, feed_low,
    here, csend, crecv, send, recv, esend, erecv,
):
    y, x, c, zl = (lax.axis_index(k) for k in ("y", "x", "c", "zl"))
    core, chip = {"c": 1 - c}, {"zl": 1 - zl}
    greet([*ring_of("x", x), *ring_of("y", y), core, chip])
    step = 16
    f32, low = jnp.float32, jnp.bfloat16

    def shift(i, by):
        return lax.rem(i + by, 4)

    order = (2, 1, 3, 0)

    def chunk(q):
        return pl.ds(pl.multiple_of(shift(y, order[q]) * 640, 640), 640)

    def load(q, side, remote_side):
        rows = chunk(q)
        if side == 0:
            parts = [a_ref.at[rows, pl.ds(0, 256)], a_ref.at[rows, pl.ds(256, 512)], a_ref.at[rows, pl.ds(768, 768)]]
        else:
            parts = [a_ref.at[rows, pl.ds(1536, 256)], o_ref.at[rows, pl.ds(0, 512)], o_ref.at[rows, pl.ds(512, 768)]]
        out = []
        for s, (at, landing, width) in enumerate(SEGMENTS):
            k = q * 3 + s
            if remote_side:
                out.append(
                    remote(parts[s], from_core.at[rows, pl.ds(landing, width)], csend.at[k], crecv.at[k], core)
                )
            else:
                out.append(pltpu.make_async_copy(parts[s], sums.at[rows, pl.ds(at, width)], here.at[k]))
        return out

    def feed_load(q):
        rows = chunk(q)
        return [
            pltpu.make_async_copy(
                f_ref.at[rows, pl.ds(h * FEED, FEED)],
                sums.at[rows, pl.ds(h * WIDE + ATTN, FEED)],
                here.at[12 + q * 2 + h],
            )
            for h in range(2)
        ]

    for side in range(2):

        @pl.when(c == side)
        def _(side=side):
            for q in range(4):
                for copy in load(q, 1 - side, True):
                    copy.start()
                for copy in load(q, side, False):
                    copy.start()

    for q in range(4):
        for copy in feed_load(q):
            copy.start()

    def columns(h):
        return pl.ds(h * WIDE, WIDE)

    def rows_at(h, i1, i2, start=0, size=160):
        row, column = (i2, i1) if h == 0 else (i1, i2)
        return block_rows(row, column, start, size)

    def around(h):
        if h == 0:
            return x, ring_of("x", x), y, ring_of("y", y)
        return y, ring_of("y", y), x, ring_of("x", x)

    def add(h, first, size, terms):
        @pl.loop(0, size // step)
        def _(i):
            at = pl.ds(pl.multiple_of(first + i * step, step), step)
            total = sums[at, columns(h)].astype(f32)
            for ref, index, start in terms:
                total += ref[(*index, pl.ds(pl.multiple_of(start + i * step, step), step))].astype(f32)
            sums[at, columns(h)] = total.astype(low)

    started = []

    def go(h, ring, slot, src, dst, peer):
        k = (h * 5 + ring) * 4 + slot
        copy = remote(src, dst, send.at[k], recv.at[k], peer)
        copy.start()
        started.append(copy)

    def arrived(h, ring, slot, dst):
        k = (h * 5 + ring) * 4 + slot
        remote(dst, dst, send.at[k], recv.at[k], core).wait_recv()

    def first_row(h, i1, i2):
        row, column = (i2, i1) if h == 0 else (i1, i2)
        return (row * 4 + column) * 160

    def out_via(h, ring, place, at, ring_peers):
        back, ahead = ring_peers
        far = shift(at, 2)
        go(h, ring, 0, sums.at[place(far, 0, 80), columns(h)], via.at[h, ring, 0], ahead)
        go(h, ring, 1, sums.at[place(far, 80, 80), columns(h)], via.at[h, ring, 1], back)

    def out_main(h, ring, place, first, at, ring_peers):
        back, ahead = ring_peers
        arrived(h, ring, 0, via.at[h, ring, 0])
        add(h, first(shift(at, 1)), 80, [(via, (h, ring, 0), 0)])
        go(h, ring, 2, sums.at[place(shift(at, 1), 0, 160), columns(h)], main.at[h, ring, 0], ahead)
        arrived(h, ring, 1, via.at[h, ring, 1])
        add(h, first(shift(at, 3)) + 80, 80, [(via, (h, ring, 1), 0)])
        go(h, ring, 3, sums.at[place(shift(at, 3), 0, 160), columns(h)], main.at[h, ring, 1], back)

    def take(h, ring, first, at):
        arrived(h, ring, 2, main.at[h, ring, 0])
        arrived(h, ring, 3, main.at[h, ring, 1])
        add(h, first(at), 160, [(main, (h, ring, 0), 0), (main, (h, ring, 1), 0)])

    def along_second(h, j):
        i1, _, i2, peers = around(h)
        fixed = shift(i1, order[j])
        return (
            lambda k, start, size: rows_at(h, fixed, k, start, size),
            lambda k: first_row(h, fixed, k),
            i2,
            peers,
        )

    def along_first(h):
        i1, peers, i2, _ = around(h)
        return (
            lambda k, start, size: rows_at(h, k, i2, start, size),
            lambda k: first_row(h, k, i2),
            i1,
            peers,
        )

    for q in range(4):
        for copy in load(q, 0, False):
            copy.wait()
        for copy in feed_load(q):
            copy.wait()
        for copy in load(q, 0, True):
            copy.wait_recv()
        top = shift(y, order[q]) * 640

        @pl.loop(0, 640 // step)
        def _(i, top=top):
            at = pl.ds(pl.multiple_of(top + i * step, step), step)
            for place, landing, width in SEGMENTS:
                total = sums[at, pl.ds(place, width)].astype(f32) + from_core[
                    at, pl.ds(landing, width)
                ].astype(f32)
                sums[at, pl.ds(place, width)] = total.astype(low)

        if q == 0:
            for j in range(4):
                place, first, at, peers = along_second(0, j)
                out_via(0, j, place, at, peers)
        place, first, at, peers = along_second(1, q)
        out_via(1, q, place, at, peers)
        if q > 0:
            place, first, at, peers = along_second(1, q - 1)
            out_main(1, q - 1, place, first, at, peers)
    for j in range(4):
        place, first, at, peers = along_second(0, j)
        out_main(0, j, place, first, at, peers)
        if j == 0:
            place, first, at, peers = along_second(1, 3)
            out_main(1, 3, place, first, at, peers)
    for j in range(4):
        for h in (1, 0):
            place, first, at, peers = along_second(h, j)
            take(h, j, first, at)
            if j == 0:
                place, first, at, peers = along_first(h)
                out_via(h, 4, place, at, peers)
    for h in (1, 0):
        place, first, at, peers = along_first(h)
        out_main(h, 4, place, first, at, peers)
    for h in (1, 0):
        place, first, at, peers = along_first(h)
        take(h, 4, first, at)
    home = (y * 4 + x) * 160
    theirs = pl.ds(pl.multiple_of(home + (1 - zl) * 80, 16), 80)
    away = remote(sums.at[theirs], from_chip, esend.at[0], erecv.at[0], chip)
    away.start()
    away.wait()

    @pl.loop(0, 80 // step)
    def _(i):
        here_at = pl.ds(pl.multiple_of(home + zl * 80 + i * step, step), step)
        at = pl.ds(pl.multiple_of(i * step, step), step)
        for h in range(2):
            a = pl.ds(h * WIDE, ATTN)
            attn_low[at, pl.ds(h * ATTN, ATTN)] = sums[here_at, a].astype(f32) + from_chip[at, a].astype(f32)
            f = pl.ds(h * WIDE + ATTN, FEED)
            feed_low[0, at, pl.ds(h * FEED, FEED)] = sums[here_at, f].astype(f32)
            feed_low[1, at, pl.ds(h * FEED, FEED)] = from_chip[at, f].astype(f32)

    ours = pl.ds(pl.multiple_of(c * 40, 8), 40)
    for_core = pl.ds(pl.multiple_of((1 - c) * 40, 8), 40)
    half = pl.ds(pl.multiple_of(c * 2 * ATTN, 128), 2 * ATTN)
    last = [remote(attn_low.at[for_core], attn_ref.at[:, half], esend.at[1], erecv.at[1], core)]
    keep = [pltpu.make_async_copy(attn_low.at[ours], attn_ref.at[:, half], here.at[0])]
    for k, source in enumerate((zl * 2 + c, (1 - zl) * 2 + c)):
        last.append(
            remote(feed_low.at[k, for_core], feed_ref.at[source], esend.at[2 + k], erecv.at[2 + k], core)
        )
        keep.append(pltpu.make_async_copy(feed_low.at[k, ours], feed_ref.at[source], here.at[1 + k]))
    for copy in (*last, *keep):
        copy.start()
    for copy in (*last, *keep):
        copy.wait()
    for copy in started:
        copy.wait_send()
    for q in range(4):
        for copy in load(q, 0, True):
            copy.wait_send()


def plane_sum(a, o, f, cid):
    low, dma = jnp.bfloat16, pltpu.SemaphoreType.DMA
    return pl.pallas_call(
        plane_sum_kernel,
        out_shape=[
            jax.ShapeDtypeStruct((40, 4 * ATTN), jnp.float32),
            jax.ShapeDtypeStruct((4, 40, 2 * FEED), jnp.float32),
        ],
        in_specs=[pl.BlockSpec(memory_space=pl.ANY)] * 3,
        out_specs=[pl.BlockSpec(memory_space=pltpu.VMEM)] * 2,
        scratch_shapes=[
            pltpu.VMEM((2560, 2 * WIDE), low),
            pltpu.VMEM((2560, 2 * ATTN), low),
            pltpu.VMEM((2, 5, 2, 80, WIDE), low),
            pltpu.VMEM((2, 5, 2, 160, WIDE), low),
            pltpu.VMEM((80, 2 * WIDE), low),
            pltpu.VMEM((80, 2 * ATTN), jnp.float32),
            pltpu.VMEM((2, 80, 2 * FEED), jnp.float32),
            dma((20,)),
            dma((12,)),
            dma((12,)),
            dma((40,)),
            dma((40,)),
            dma((4,)),
            dma((4,)),
        ],
        compiler_params=pltpu.CompilerParams(
            collective_id=cid, has_side_effects=True, vmem_limit_bytes=48 * 2**20
        ),
    )(a, o, f)


def rms_norm(values, gain_row):
    return (
        values * lax.rsqrt(jnp.mean(values * values, axis=-1, keepdims=True) + norm_eps) * gain_row
    )


def geglu(gate_part, up_part):
    return jax.nn.gelu(gate_part) * up_part


def tables():
    half_rot = ROT // 2
    rates = jnp.exp(jnp.arange(half_rot, dtype=jnp.float32) * (-2.0 * math.log(10000.0) / ROT))
    angles = jnp.arange(SEQ_LEN, dtype=jnp.float32)[:, None] * rates[None, :]
    return (jnp.cos(angles), jnp.sin(angles))


def rotate(field, cosine, sine):
    half_rot = ROT // 2
    first = field[..., :half_rot]
    second = field[..., half_rot:ROT]
    return jnp.concatenate(
        [first * cosine - second * sine, second * cosine + first * sine, field[..., ROT:]], axis=-1
    )


def contract(left, right, left_dim, right_dim):
    return lax.dot_general(
        left, right, (((left_dim,), (right_dim,)), ((), ())), preferred_element_type=jnp.float32
    )


def padded(weight):
    return jnp.pad(weight.reshape(40, 4, 960), ((0, 0), (0, 0), (0, 64)))


def scattered(value):
    return lax.psum_scatter(value.astype(jnp.bfloat16), PLANE, scatter_dimension=0, tiled=True)


def joined(slices):
    return slices[:, :, :960].transpose(1, 0, 2).reshape(40, 3840).astype(jnp.float32)


def local(
    tokens,
    attn_gain,
    query_weight,
    kv_weight,
    out_weight,
    mlp_gain,
    gate_weight,
    up_weight,
    down_weight,
    cotangent,
):
    low = jnp.bfloat16
    rows = tokens.shape[0]
    seqs = rows // SEQ_LEN
    heads_here = query_weight.shape[1] // HEAD_DIM
    wide = heads_here * HEAD_DIM
    scale = HEAD_DIM ** (-0.5)
    cosine, sine = tables()
    positions = jnp.arange(SEQ_LEN)
    keep_mask = (positions[:, None] >= positions[None, :]) & (
        positions[:, None] - positions[None, :] < WINDOW
    )
    attn = jnp.concatenate([query_weight, kv_weight, out_weight.T], axis=1)
    attn = attn.reshape(40, 2, 2, ATTN).transpose(1, 2, 0, 3)
    attn = jnp.broadcast_to(attn, (2, *attn.shape)).reshape(4, 2, 40, ATTN)
    gains = jnp.stack([attn_gain, mlp_gain], axis=1)[:, None, :]
    gains = jnp.pad(jnp.broadcast_to(gains, (40, 4, 2)), ((0, 0), (0, 0), (960, 62)))
    down = (padded(down_weight.T) + gains).reshape(40, 4, 2, FEED).transpose(1, 2, 0, 3)
    first = jnp.concatenate([attn, down], axis=3).reshape(4, 80, WIDE)
    second = jnp.stack([padded(gate_weight), padded(up_weight)], axis=0)
    second = second.transpose(2, 0, 1, 3).reshape(4, 80, 2 * FEED)
    first, second = group_exchange([first, second], 5)
    first = first.reshape(4, 2, 40, WIDE).transpose(1, 0, 2, 3).reshape(2, 160, WIDE)
    second = second.reshape(4, 2, 40, 2 * FEED).transpose(0, 2, 1, 3).reshape(160, 4 * FEED)
    w_gate_up = lax.all_gather(second, PLANE, axis=0, tiled=True)
    dy_here = permuted(cotangent)
    w_attn, w_down_t, dy = plane_gather(first, dy_here, 6)
    dy = dy.reshape(4 * rows, -1)
    w_query, w_kv, w_out_t = (
        w_attn[:, :wide],
        w_attn[:, wide : wide + 2 * HEAD_DIM],
        w_attn[:, wide + 2 * HEAD_DIM :],
    )
    chosen = jnp.zeros((16, 2 * FEED), low).at[0, 960].set(1).at[1, 961].set(1)
    gain_rows = contract(chosen[:, 896:], w_down_t[:, 896:], 1, 1)
    gain_one, gain_two = gain_rows[0], gain_rows[1]

    x_in = permuted(tokens).astype(jnp.float32)
    xn_one = rms_norm(x_in, gain_one).astype(low)
    q_pre = jnp.dot(xn_one, w_query, preferred_element_type=jnp.float32)
    kv_pre = jnp.dot(xn_one, w_kv, preferred_element_type=jnp.float32)
    queries = rotate(
        q_pre.reshape(seqs, SEQ_LEN, heads_here, HEAD_DIM), cosine[:, None, :], sine[:, None, :]
    ).astype(low)
    key_rot = rotate(kv_pre[:, :HEAD_DIM].reshape(seqs, SEQ_LEN, HEAD_DIM), cosine, sine).astype(low)
    value_rows = kv_pre[:, HEAD_DIM:].reshape(seqs, SEQ_LEN, HEAD_DIM).astype(low)

    def score_rows():
        raw = (
            jnp.einsum("sqhd,skd->shqk", queries, key_rot, preferred_element_type=jnp.float32)
            * scale
        )
        return jnp.where(keep_mask, raw, -1e30)

    scores = score_rows()
    row_max = jnp.max(scores, axis=-1, keepdims=True)
    log_total = row_max + jnp.log(jnp.sum(jnp.exp(scores - row_max), axis=-1, keepdims=True))
    attn_probs = jnp.exp(scores - log_total).astype(low)
    mixed_heads = jnp.einsum(
        "shqk,skd->sqhd", attn_probs, value_rows, preferred_element_type=jnp.float32
    )
    mixed_heads = mixed_heads.reshape(rows, wide).astype(low)
    x_mid = x_in + pair_sum(contract(mixed_heads, w_out_t, 1, 1).astype(low), 1)

    xn_two = rms_norm(x_mid, gain_two).astype(low)
    xn_all = token_gather(xn_two, 2).reshape(4 * rows, -1)
    gate_up = jnp.dot(xn_all, w_gate_up, preferred_element_type=jnp.float32)
    gate_pre, up_pre = gate_up[:, : 2 * FEED], gate_up[:, 2 * FEED :]
    hidden = geglu(gate_pre, up_pre).astype(low)
    down_part = contract(hidden, w_down_t, 1, 1).astype(low)
    d_down_t = contract(dy, hidden, 0, 0)
    d_hidden = jnp.dot(dy, w_down_t, preferred_element_type=jnp.float32)
    geglu_pull = jax.vjp(geglu, gate_pre, up_pre)[1]
    d_gate_pre, d_up_pre = geglu_pull(d_hidden)
    d_gate_low = d_gate_pre.astype(low)
    d_up_low = d_up_pre.astype(low)
    d_xn_two_part = contract(jnp.concatenate([d_gate_low, d_up_low], axis=1), w_gate_up, 1, 1)
    d_xn_two = token_sum(d_xn_two_part.astype(low).reshape(4, rows, -1), 3)
    down_branch = token_sum(down_part.reshape(4, rows, -1), 3)
    block_out = restored((x_mid + down_branch).astype(low))
    d_gate_w = contract(xn_all, d_gate_low, 0, 0)
    sent = jnp.stack([scattered(d_down_t), scattered(d_gate_w)], axis=0)

    norm_two_pull = jax.vjp(rms_norm, x_mid, gain_two)[1]
    d_mid_norm, d_gain_two = norm_two_pull(d_xn_two)
    d_mid = dy_here.astype(jnp.float32) + d_mid_norm
    d_mid_low = d_mid.astype(low)
    d_out_t = contract(d_mid_low, mixed_heads, 0, 0)
    d_mixed = (
        jnp.dot(d_mid_low, w_out_t, preferred_element_type=jnp.float32)
        .astype(low)
        .reshape(seqs, SEQ_LEN, heads_here, HEAD_DIM)
    )
    soft_rows = jnp.exp(score_rows() - log_total)
    d_probs = jnp.einsum("sqhd,skd->shqk", d_mixed, value_rows, preferred_element_type=jnp.float32)
    d_scores = (
        soft_rows * (d_probs - jnp.sum(soft_rows * d_probs, axis=-1, keepdims=True))
    ).astype(low)
    d_queries = (
        jnp.einsum("shqk,skd->sqhd", d_scores, key_rot, preferred_element_type=jnp.float32) * scale
    )
    d_keys = (
        jnp.einsum("shqk,sqhd->skd", d_scores, queries, preferred_element_type=jnp.float32) * scale
    )
    d_values = jnp.einsum("shqk,sqhd->skd", attn_probs, d_mixed, preferred_element_type=jnp.float32)
    d_q_pre = (
        rotate(d_queries, cosine[:, None, :], -sine[:, None, :]).reshape(rows, wide).astype(low)
    )
    d_k_pre = rotate(d_keys, cosine, -sine).reshape(rows, HEAD_DIM)
    d_kv_part = jnp.concatenate([d_k_pre, d_values.reshape(rows, HEAD_DIM)], axis=-1)
    d_xn_one_part = contract(d_q_pre, w_query, 1, 1)
    sums = pair_sum(jnp.concatenate([d_xn_one_part.astype(low), d_kv_part.astype(low)], axis=1), 4)
    d_xn_one_q, d_kv_low = sums[:, : x_in.shape[1]], sums[:, x_in.shape[1] :].astype(low)
    d_q_kv_w = contract(xn_one, jnp.concatenate([d_q_pre, d_kv_low], axis=1), 0, 0).astype(low)
    d_xn_one = d_xn_one_q + contract(d_kv_low, w_kv, 1, 1)
    norm_one_pull = jax.vjp(rms_norm, x_in, gain_one)[1]
    d_in_norm, d_gain_one = norm_one_pull(d_xn_one)
    tokens_grad = restored((d_mid + d_in_norm).astype(low))
    d_gains = jnp.pad(jnp.stack([d_gain_one, d_gain_two], axis=0).astype(low), ((0, 14), (0, 0)))
    d_up_w = contract(
        jnp.concatenate([xn_all, d_gains], axis=0),
        jnp.concatenate([d_up_low, chosen], axis=0),
        0,
        0,
    ).astype(low)
    attn_out, up_out = plane_sum(d_q_kv_w, d_out_t.astype(low), d_up_w, 7)
    sent = sent.reshape(2, 4, 40, 2 * FEED).transpose(1, 0, 2, 3).reshape(4, 80, 2 * FEED)
    sent = group_exchange([sent], 8)[0].reshape(4, 2, 40, 2 * FEED)
    gain_out = up_out[:, :, 960:962].sum(axis=0)
    return (
        block_out,
        tokens_grad,
        gain_out[:, 0],
        attn_out[:, :wide],
        attn_out[:, wide : wide + 2 * HEAD_DIM],
        attn_out[:, wide + 2 * HEAD_DIM :].T,
        gain_out[:, 1],
        joined(sent[:, 1]),
        joined(up_out),
        joined(sent[:, 0]).T,
    )


def solution(mesh):
    fine = Mesh(mesh.devices.reshape(4, 2, 4, 2, 2), AXES)
    dp = ("y", "zl", "x", "c")
    in_specs = (
        P(dp, None),
        P(dp),
        P(dp, "zh"),
        P(dp, None),
        P("zh", dp),
        P(dp),
        P(dp, "zh"),
        P(dp, "zh"),
        P("zh", dp),
        P(dp, None),
    )
    out_specs = (
        P(dp, None),
        P(dp, None),
        P(dp),
        P(dp, "zh"),
        P(dp, None),
        P("zh", dp),
        P(dp),
        P(dp, "zh"),
        P(dp, "zh"),
        P("zh", dp),
    )
    return jax.shard_map(local, mesh=fine, in_specs=in_specs, out_specs=out_specs, check_vma=False)
```

time: 2430 us -> 556 us (0.23)
  waiting for transfers between devices: 1830 us -> 0.07 us
  Pallas kernels: 0 us -> 367 us
  local copies, waits for them, and re-layouts: 281 us -> 59.8 us
  matrix products: 170 us -> 91 us
  other arithmetic: 65.7 us -> 14.6 us
  blocking collectives: 36.1 us -> 0 us
    unnamed x7 -> x3, waiting for transfers between devices: 1060 us -> 0.05 us
    all_gather x2 -> x1, waiting for transfers between devices: 401 us -> 0.02 us  [local(): w_gate_up = lax.all_gather(second, PLANE, axis=0, tiled=True)]
    pallas_call x0 -> x9, Pallas kernels: none -> 367 us  [the longest x1 128 us: plane_gather(): pl.pallas_call(plane_gather_kernel, out_shape=[jax.ShapeDtypeStruct((2560...]
    reduce_scatter x1 -> x2, waiting for transfers between devices: 347 us -> 0.01 us  [scattered(): lax.psum_scatter(value.astype(jnp.bfloat16), PLANE, scatter_dimension=0,...]
    concatenate x3 -> x0, local copies, waits for them, and re-layouts: 95.6 us -> none  [the longest x1 90.4 us: sent_together(): both = jnp.concatenate(columns, axis=along)]
    dot_general x12 -> x11, matrix products: 115 us -> 60.1 us  [contract(): lax.dot_general(left, right, (((left_dim,), (right_dim,)), ((), ())), pre...]
    concatenate x2 -> x3, other arithmetic: 53 us -> 1.06 us  [the longest x1 0.97 us: local(): first = jnp.concatenate([attn, down], axis=3).reshape(4, 80, WIDE)]
    another operation x4 -> x3, local copies, waits for them, and re-layouts: 45 us -> 0.76 us  [sum_together(): lines = jnp.concatenate([b.reshape(size, -1) for b in pieces], axis=1)]
  transfers between devices with their start and end apart: 9 -> 3, of which waited for: 7 -> 0; matrix products, arithmetic and copies ran while one was open for 12% -> 23% of each run, Pallas kernels for 0% -> 61%
where the time goes in v1:
time: 556 us; the launch traced here: 549 us
  Pallas kernels  367 us (66%)
  matrix products  91 us (16%)
  local copies, waits for them, and re-layouts  59.8 us (11%)
  between operations  15.7 us (3%)
  other arithmetic  14.6 us (3%)
    pallas_call x1, Pallas kernels, plane_gather(): pl.pallas_call(plane_gather_kernel, out_shape=[jax.ShapeDtypeStruct((2560...  128 us
    pallas_call x1, Pallas kernels, plane_sum(): pl.pallas_call(plane_sum_kernel, out_shape=[jax.ShapeDtypeStruct((40, 4 *...  101 us
    dot_general x11, matrix products, contract(): lax.dot_general(left, right, (((left_dim,), (right_dim,)), ((), ())), pre...  60.1 us
    pallas_call x2, Pallas kernels, token_sum(): pl.pallas_call(sum_kernel, out_shape=jax.ShapeDtypeStruct((rows, width),...  55.9 us
    pallas_call x2, Pallas kernels, pair_sum(): pl.pallas_call(pair_kernel, out_shape=jax.ShapeDtypeStruct(p.shape, jnp.f...  38.7 us
    pallas_call x2, Pallas kernels, group_exchange(): pl.pallas_call(exchange_kernel, out_shape=[jax.ShapeDtypeStruct(a.shape,...  30.2 us
    dot_general x2, local copies, waits for them, and re-layouts, local(): q_pre = jnp.dot(xn_one, w_query, preferred_element_type=jnp.float32)  15.6 us
    pallas_call x1, Pallas kernels, token_gather(): pl.pallas_call(gather_kernel, out_shape=jax.ShapeDtypeStruct((4, *x.shape...  13.8 us
  transfers between devices with their start and end apart: 3, of which 0 were waited for; matrix products, arithmetic and copies ran while one was open for 23% of the time, Pallas kernels for 61%

profile of v1, /device:TPU:1, one launch (start us, length us, event | category | flops | bytes accessed | tf_op | source)
XLA Modules:
  0.0 548.7 jit_solution(6697003767171803068)
XLA Ops:
  7.3 0.7 pad_maximum_fusion.9
  8.1 1.4 reshape.595
  11.7 1.0 pad_maximum_fusion.refs_0_
  12.7 0.9 pad_maximum_fusion.2
  13.6 20.3 %shard_map.177 = (bf16[4,80,1280]{2,1,0:T(8,128)(2,1)}, bf16[4,80,1024]{2,1,0:T(8,128)(2,1)}) custom-call(bf16[4,80,1280]{2,1,0:T(8,128)(2,1)} %pad_maximum_fusion.refs_0_, bf16[4,80,1024]{2,1,0:T(8,128)(2,1)} %bitcast.184), custom_call_target="tpu_custom_call" | custom-call | tf_op jit(solution)/shard_map/pallas_call | solution.py:261
  34.0 1.8 copy.144
  35.7 1.0 copy.178
  37.8 2.6 copy.134
  40.4 2.2 copy.135
  42.5 2.0 copy.136
  44.5 2.2 copy.137.dy_ref
  46.7 127.7 %shard_map.178 = (bf16[2560,3072]{1,0:T(8,128)(2,1)}, bf16[2560,1024]{1,0:T(8,128)(2,1)}, bf16[4,128,2560]{2,1,0:T(8,128)(2,1)}) custom-call(bf16[2,160,1280]{2,1,0:T(8,128)(2,1)} %bitcast.180, bf16[128,2560]{1,0:T(8,128)(2,1)} %copy.137.dy_ref), custom_call_target="tpu_custom_call" | custom-call | tf_op jit(solution)/shard_map/pallas_call | solution.py:428
  174.4 6.1 %slice_bitcast_fusion = bf16[1280,2560]{0,1:T(8,128)(2,1)} fusion(bf16[2560,3072]{1,0:T(8,128)(2,1)} %get-tuple-element.43), kind=kLoop, calls=%fused_computation.8 | loop fusion | bytes 13107200 | tf_op jit(solution)/shard_map/dot_general | solution.py:801
  180.5 9.5 %copy.139 = bf16[1280,2560]{1,0:T(8,128)(2,1)} copy(bf16[1280,2560]{0,1:T(8,128)(2,1)} %slice_bitcast_fusion) | data formatting | bytes 13107200 | tf_op jit(solution)/shard_map/dot_general | solution.py:801
  191.8 1.4 scatter.6
  193.6 1.5 fusion.47
  195.6 2.4 fusion.19
  198.7 2.8 convolution_bitcast_fusion
  202.5 5.2 fusion.9.p_ref
  207.8 17.7 %shard_map.179 = f32[128,2560]{1,0:T(8,128)S(1)} custom-call(bf16[128,2560]{1,0:T(8,128)(2,1)S(1)} %fusion.9.p_ref), custom_call_target="tpu_custom_call" | custom-call | tf_op jit(solution)/shard_map/pallas_call | solution.py:204
  225.8 1.1 copy-done.4
  227.1 13.8 %shard_map.180 = bf16[4,128,2560]{2,1,0:T(8,128)(2,1)S(1)} custom-call(bf16[128,2560]{1,0:T(8,128)(2,1)S(1)} %multiply_convert_fusion.2.x_ref), custom_call_target="tpu_custom_call" | custom-call | tf_op jit(solution)/shard_map/pallas_call | solution.py:82
  241.0 8.4 %fusion.91 = f32[512,2048]{1,0:T(8,128)S(1)} fusion(bf16[512,2560]{1,0:T(8,128)(2,1)S(1)} %bitcast.171, bf16[2560,2048]{1,0:T(8,128)(2,1)} %all-gather.2.cloned.1.call-done), kind=kOutput, calls=%fused_computation.169 | convolution fusion | flops 5368709120 | bytes 17301504 | tf_op jit(solution)/shard_map/dot_general | solution.py:828
  249.4 8.2 %fusion.27 = (bf16[512,1024]{1,0:T(8,128)(2,1)S(1)}, bf16[512,1024]{1,0:T(8,128)(2,1)}, bf16[512,1024]{1,0:T(8,128)(2,1)}) fusion(f32[512,2048]{1,0:T(8,128)S(1)} %fusion.91, bf16[512,2560]{1,0:T(8,128)(2,1)S(1)} %bitcast.210, bf16[2560,1024]{1,0:T(8,128)(2,1)} %get-tuple-element.42), kind=kOutput, calls=%fused_computation.32 | convolution fusion | flops 2697986048 | bytes 15204352 | tf_op jit(solution)/shard_map/dot_general | solution.py:833
  257.5 1.0 copy-done.37
  258.5 4.7 convolution_convert_fusion.3
  263.5 7.2 %convolution_convert_fusion.4 = bf16[2560,1024]{1,0:T(8,128)(2,1)} fusion(bf16[512,2560]{1,0:T(8,128)(2,1)} %bitcast.209, bf16[512,1024]{1,0:T(8,128)(2,1)} %get-tuple-element.90), kind=kOutput, calls=%fused_computation.11 | convolution fusion | flops 2686976000 | bytes 8912896 | tf_op jit(solution)/shard_map/dot_general | solution.py:734
  270.7 9.0 %convolution_convert_fusion.6 = bf16[512,2560]{1,0:T(8,128)(2,1)S(1)} fusion(bf16[2560,2048]{1,0:T(8,128)(2,1)} %all-gather.2.cloned.1.call-done, bf16[512,1024]{1,0:T(8,128)(2,1)} %get-tuple-element.89, bf16[512,1024]{1,0:T(8,128)(2,1)} %copy-done.37), kind=kOutput, calls=%fused_computation.13 | convolution fusion | flops 5374214144 | bytes 15204352 | tf_op jit(solution)/shard_map/dot_general | solution.py:734
  279.7 28.0 %shard_map.182 = f32[128,2560]{1,0:T(8,128)S(1)} custom-call(bf16[4,128,2560]{2,1,0:T(8,128)(2,1)S(1)} %bitcast.174), custom_call_target="tpu_custom_call" | custom-call | tf_op jit(solution)/shard_map/pallas_call | solution.py:167
  307.7 5.7 %convolution_convert_fusion.5 = bf16[512,2560]{1,0:T(8,128)(2,1)S(1)} fusion(bf16[512,1024]{1,0:T(8,128)(2,1)S(1)} %copy-done.36, bf16[2560,1024]{1,0:T(8,128)(2,1)} %get-tuple-element.42), kind=kOutput, calls=%fused_computation.12 | convolution fusion | flops 2685665280 | bytes 8912896 | tf_op jit(solution)/shard_map/dot_general | solution.py:734
  313.5 27.9 %shard_map.181 = f32[128,2560]{1,0:T(8,128)S(1)} custom-call(bf16[4,128,2560]{2,1,0:T(8,128)(2,1)S(1)} %bitcast.175), custom_call_target="tpu_custom_call" | custom-call | tf_op jit(solution)/shard_map/pallas_call | solution.py:167
  341.4 1.1 multiply_reduce_fusion
  342.5 1.8 fusion.31
  344.4 2.2 copy.145
  346.5 2.0 copy.146
  348.5 2.2 copy.165
  350.7 5.3 fusion.15
  356.0 1.2 copy.148
  357.2 1.2 multiply_reduce_fusion.6
  358.4 1.4 fusion.38
  361.0 0.9 pad_maximum_fusion.5
  361.9 1.9 copy.153
  363.8 0.9 subtract_convert_fusion.2
  364.7 0.9 maximum_bitcast_fusion.1
  365.9 5.4 fusion.6
  371.4 20.9 %shard_map.183 = f32[128,3072]{1,0:T(8,128)S(1)} custom-call(bf16[128,3072]{1,0:T(8,128)(2,1)S(1)} %pad_maximum_fusion.1.p_ref), custom_call_target="tpu_custom_call" | custom-call | tf_op jit(solution)/shard_map/pallas_call | solution.py:204
  392.4 3.0 multiply_reduce_fusion.1
  395.4 1.3 fusion.33
  396.7 1.4 copy.157
  398.2 1.0 copy.158
  399.1 2.2 copy.166
  401.5 6.2 %convolution_convert_fusion.o_ref = bf16[2560,1280]{1,0:T(8,128)(2,1)} fusion(bf16[128,1280]{0,1:T(8,128)(2,1)} %bitcast.198, f32[128,2560]{1,0:T(8,128)} %get-tuple-element.91), kind=kOutput, calls=%fused_computation | convolution fusion | flops 842465280 | bytes 8192000 | tf_op jit(solution)/shard_map/dot_general | solution.py:734
  407.7 6.2 %convolution_convert_fusion.1.a_ref = bf16[2560,1792]{1,0:T(8,128)(2,1)} fusion(bf16[128,512]{0,1:T(8,128)(2,1)S(1)} %copy.159, bf16[128,1280]{0,1:T(8,128)(2,1)S(1)} %bitcast.200, f32[128,2560]{1,0:T(8,128)S(1)} %copy-done.2, f32[2560]{0:T(1024)S(1)} %get-tuple-element.83, f32[128]{0:T(128)S(1)} %copy-done.30), kind=kOutput, calls=%fused_computation.1 | convolution fusion | flops 1180893184 | bytes 10955264 | tf_op jit(solution)/shard_map/dot_general | solution.py:734
  413.9 6.0 %convolution_convert_fusion.2.f_ref = bf16[2560,1024]{1,0:T(8,128)(2,1)} fusion(bf16[16,2560]{1,0:T(8,128)(2,1)S(1)} %fusion.62, bf16[512,2560]{1,0:T(8,128)(2,1)S(1)} %bitcast.173, bf16[16,1024]{1,0:T(8,128)(2,1)S(1)} %copy-done.26, bf16[512,1024]{1,0:T(8,128)(2,1)S(1)} %copy-done.38), kind=kOutput, calls=%fused_computation.9 | convolution fusion | flops 2778431488 | bytes 9027584 | tf_op jit(solution)/shard_map/dot_general | solution.py:734
  419.9 101.0 %shard_map.184 = (f32[40,3072]{1,0:T(8,128)S(1)}, f32[4,40,1024]{2,1,0:T(8,128)S(1)}) custom-call(bf16[2560,1792]{1,0:T(8,128)(2,1)} %convolution_convert_fusion.1.a_ref, bf16[2560,1280]{1,0:T(8,128)(2,1)} %convolution_convert_fusion.o_ref, bf16[2560,1024]{1,0:T(8,128)(2,1)} %convolution_convert_fusion.2.f_ref), custom_call_target="tpu_custom_call" | custom-call | tf_op jit(solution)/shard_map/pallas_call | solution.py:677
  520.9 0.6 slice.185
  522.1 1.4 reshape.623
  523.6 0.7 slice_reduce_fusion.1
  524.3 0.8 slice_bitcast_fusion.4
  525.1 2.0 pad_maximum_fusion.3
  527.0 9.9 %shard_map.185 = bf16[4,80,1024]{2,1,0:T(8,128)(2,1)} custom-call(bf16[4,80,1024]{2,1,0:T(8,128)(2,1)} %bitcast.186), custom_call_target="tpu_custom_call" | custom-call | tf_op jit(solution)/shard_map/pallas_call | solution.py:261
  536.9 1.1 slice_bitcast_fusion.2
  538.6 1.4 reshape.626
  540.5 1.4 reshape.627
  (148 shorter events, 10.8 us)
Async XLA Ops:
  7.2 2.8 copy-start.23
  7.2 2.8 copy-start.27
  7.2 2.8 copy-start.24
  7.2 233.7 %all-gather.2.cloned.1.call-start = ((), (), s32[]{:S(2)}) async-start(), calls=%async_computation.2 | async-start | bytes 11141120 | tf_op jit(solution)/shard_map/all_gather | solution.py:786
  9.5 1.0 copy-start.12
  9.7 1.3 copy-start.13
  13.6 23.2 %copy-start.10 = (bf16[128,2560]{1,0:T(8,128)(2,1)S(1)}, bf16[128,2560]{1,0:T(8,128)(2,1)}, u32[]{:S(2)}) copy-start(bf16[128,2560]{1,0:T(8,128)(2,1)} %param.14) | copy-start | bytes 1966084
  36.8 488.3 %reduce-scatter.5.cloned.1.call-start = ((), (), s32[]{:S(2)}) async-start(), calls=%async_computation.4 | async-start | bytes 5570560 | tf_op jit(solution)/shard_map/reduce_scatter | solution.py:744
  37.8 187.7 %copy-start = (f32[128,2560]{1,0:T(8,128)}, f32[128,2560]{1,0:T(8,128)S(1)}, u32[]{:S(2)}) copy-start(f32[128,2560]{1,0:T(8,128)S(1)} %copy.143) | copy-start | bytes 3932164
  180.5 9.5 %copy-start.35 = (s32[2]{0:T(128)S(1)}, s32[2]{0:T(128)}, u32[]{:S(2)}) copy-start(s32[2]{0:T(128)} %constant.83.clone.1) | copy-start | bytes 28
  193.6 4.5 copy-start.25
  193.6 4.8 copy-start.31
  193.6 5.1 copy-start.3
  195.6 2.5 copy-start.32
  195.6 3.1 copy-start.29
  198.0 4.2 copy-start.11
  198.1 3.7 copy-start.17
  198.4 3.4 copy-start.19
  198.4 3.4 copy-start.21
  201.5 1.0 copy-start.16
  201.7 0.8 copy-start.14
  201.7 0.8 copy-start.15
  202.5 5.3 copy-start.8
  225.8 1.1 copy-start.4
  240.9 8.4 %copy-start.34 = (bf16[4,128,2560]{2,1,0:T(8,128)(2,1)S(1)}, bf16[4,128,2560]{2,1,0:T(8,128)(2,1)}, u32[]{:S(2)}) copy-start(bf16[4,128,2560]{2,1,0:T(8,128)(2,1)} %get-tuple-element.45) | copy-start | bytes 7864324
  257.5 1.0 copy-start.37
  263.2 261.8 %reduce-scatter.3.cloned.1.call-start = ((), (), s32[]{:S(2)}) async-start(), calls=%async_computation.3 | async-start | bytes 5570560 | tf_op jit(solution)/shard_map/reduce_scatter | solution.py:744
  279.7 28.0 %copy-start.36 = (bf16[512,1024]{1,0:T(8,128)(2,1)S(1)}, bf16[512,1024]{1,0:T(8,128)(2,1)}, u32[]{:S(2)}) copy-start(bf16[512,1024]{1,0:T(8,128)(2,1)} %get-tuple-element.90) | copy-start | bytes 3145732
  313.4 27.9 %copy-start.5 = (f32[128,2560]{1,0:T(8,128)S(1)}, f32[128,2560]{1,0:T(8,128)}, u32[]{:S(2)}) copy-start(f32[128,2560]{1,0:T(8,128)} %copy-done.4) | copy-start | bytes 3932164
  341.4 1.2 copy-start.7
  357.1 3.3 copy-start.18
  357.1 3.3 copy-start.20
  357.2 3.3 copy-start.22
  371.3 21.1 %copy-start.1 = (f32[128,2560]{1,0:T(8,128)S(1)}, f32[128,2560]{1,0:T(8,128)}, u32[]{:S(2)}) copy-start(f32[128,2560]{1,0:T(8,128)} %copy-done) | copy-start | bytes 3932164
  371.3 21.1 %copy-start.30 = (f32[128]{0:T(128)S(1)}, f32[128]{0:T(128)}, u32[]{:S(2)}) copy-start(f32[128]{0:T(128)} %copy-done.29) | copy-start | bytes 1540
  392.4 3.0 copy-start.33
  392.4 3.1 copy-start.6
  396.7 4.7 copy-start.28
  401.5 6.2 %copy-start.2 = (f32[128,2560]{1,0:T(8,128)S(1)}, f32[128,2560]{1,0:T(8,128)}, u32[]{:S(2)}) copy-start(f32[128,2560]{1,0:T(8,128)} %copy-done) | copy-start | bytes 3932164
  401.5 6.2 %copy-start.9 = (bf16[1,128,5,256]{1,3,2,0:T(8,128)(2,1)S(1)}, bf16[1,128,5,256]{1,3,2,0:T(8,128)(2,1)}, u32[]{:S(2)}) copy-start(bf16[1,128,5,256]{1,3,2,0:T(8,128)(2,1)} %copy.153) | copy-start | bytes 983044
  407.7 6.2 %copy-start.26 = (bf16[16,1024]{1,0:T(8,128)(2,1)S(1)}, bf16[16,1024]{1,0:T(8,128)(2,1)}, u32[]{:S(2)}) copy-start(bf16[16,1024]{1,0:T(8,128)(2,1)} %copy-done.25) | copy-start | bytes 98308
  407.7 6.2 %copy-start.38 = (bf16[512,1024]{1,0:T(8,128)(2,1)S(1)}, bf16[512,1024]{1,0:T(8,128)(2,1)}, u32[]{:S(2)}) copy-start(bf16[512,1024]{1,0:T(8,128)(2,1)} %get-tuple-element.89) | copy-start | bytes 3145732
Sparse Core Ops, SparseCore 0:
  36.9 133.5 all-gather.1
  263.4 75.2 reduce-scatter.4
  342.0 78.0 reduce-scatter.2

commit v2 on v1

v2 whole, which is shorter than its diff:
```python
import math

import jax
import jax.numpy as jnp
import numpy as np
from jax import lax
from jax.experimental import pallas as pl
from jax.experimental.pallas import tpu as pltpu
from jax.sharding import Mesh
from jax.sharding import PartitionSpec as P

HEAD_DIM = 256
WINDOW = 2048
SEQ_LEN = 128
ROT = 128
AXES = ("y", "zl", "x", "c", "zh")
PLANE = ("y", "x")
GROUP = ("zl", "c")
OWNERS = ("y", "x", "zl", "c")
MESH = pl.DeviceIdType.MESH

norm_eps = 1e-06


def feature_order():
    place = np.arange(640).reshape(2, 4, 80).transpose(1, 0, 2).reshape(640)
    return (np.arange(640)[:, None] == place[None, :]).astype(np.float32)


def reorder(src, order, dst, back):
    for k in range(4):
        group = pl.ds(k * 640, 640)
        dst[:, group] = lax.dot_general(
            src[:, group],
            order[...],
            (((1,), (1 if back else 0,)), ((), ())),
            preferred_element_type=jnp.float32,
        ).astype(dst.dtype)


def greet(peers):
    barrier = pltpu.get_barrier_semaphore()
    for peer in peers:
        pl.semaphore_signal(barrier, inc=1, device_id=peer, device_id_type=MESH)
    pl.semaphore_wait(barrier, len(peers))


def remote(src, dst, send, recv, peer):
    return pltpu.make_async_remote_copy(
        src_ref=src, dst_ref=dst, send_sem=send, recv_sem=recv, device_id=peer, device_id_type=MESH
    )


def sum_kernel(p_ref, o_ref, from_core, other, from_chips, own, own_low, from_far, send, recv):
    zl, c, zh = lax.axis_index("zl"), lax.axis_index("c"), lax.axis_index("zh")
    rows = p_ref.shape[1]
    half = rows // 2
    core, far = {"c": 1 - c}, {"zh": 1 - zh}
    chips = [{"zl": 1 - zl, "zh": k} for k in range(2)]
    greet([core, far, *chips])
    order = [1 - zl, zl]
    cores = [
        remote(p_ref.at[z * 2 + 1 - c], from_core.at[i], send.at[i], recv.at[i], core)
        for i, z in enumerate(order)
    ]
    for copy in cores:
        copy.start()
    step = 16
    cores[0].wait_recv()
    aways = []
    for k in range(2):

        @pl.loop(0, half // step)
        def _(j, k=k):
            at = pl.ds(pl.multiple_of(k * half + j * step, step), step)
            total = p_ref[(1 - zl) * 2 + c, at].astype(jnp.float32) + from_core[0, at].astype(jnp.float32)
            other[at] = total.astype(jnp.bfloat16)

        away = remote(
            other.at[pl.ds(k * half, half)], from_chips.at[zh], send.at[2 + k], recv.at[2 + zh], chips[k]
        )
        away.start()
        aways.append(away)
    cores[1].wait_recv()
    fars = []
    for k in range(2):
        piece = (1 - zh) if k == 0 else zh
        if k == 1:
            for i in range(2):
                remote(
                    other.at[pl.ds(0, half)], from_chips.at[i], send.at[2 + i], recv.at[2 + i], chips[i]
                ).wait_recv()

        @pl.loop(0, half // step)
        def _(j, k=k, piece=piece):
            at = pl.ds(pl.multiple_of(piece * half + j * step, step), step)
            total = p_ref[zl * 2 + c, at].astype(jnp.float32) + from_core[1, at].astype(jnp.float32)
            if k == 1:
                here = pl.ds(pl.multiple_of(j * step, step), step)
                total += from_chips[0, here].astype(jnp.float32) + from_chips[1, here].astype(jnp.float32)
            own[at] = total.astype(jnp.bfloat16)

        at = pl.ds(pl.multiple_of(piece * half, half), half)
        copy = remote(own.at[at], from_far.at[at], send.at[4 + k], recv.at[4 + k], far)
        copy.start()
        fars.append(copy)
    for k in range(2):
        fars[k].wait_recv()
        piece = zh if k == 0 else (1 - zh)

        @pl.loop(0, half // step)
        def _(j, piece=piece):
            at = pl.ds(pl.multiple_of(piece * half + j * step, step), step)
            o_ref[at] = own[at].astype(jnp.float32) + from_far[at].astype(jnp.float32)

    for copy in (*cores, *aways, *fars):
        copy.wait_send()


def token_sum(p, cid):
    rows, width = p.shape[1:]
    low = jnp.bfloat16
    return pl.pallas_call(
        sum_kernel,
        out_shape=jax.ShapeDtypeStruct((rows, width), jnp.float32),
        in_specs=[pl.BlockSpec(memory_space=pltpu.VMEM)],
        out_specs=pl.BlockSpec(memory_space=pltpu.VMEM),
        scratch_shapes=[
            pltpu.VMEM((2, rows, width), low),
            pltpu.VMEM((rows, width), low),
            pltpu.VMEM((2, rows // 2, width), low),
            pltpu.VMEM((rows, width), low),
            pltpu.VMEM((rows, width), low),
            pltpu.VMEM((rows, width), low),
            pltpu.SemaphoreType.DMA((6,)),
            pltpu.SemaphoreType.DMA((6,)),
        ],
        compiler_params=pltpu.CompilerParams(
            collective_id=cid, has_side_effects=True, vmem_limit_bytes=32 * 2**20
        ),
    )(p)


def pair_kernel(p_ref, o_ref, landed, send, recv):
    far = {"zh": 1 - lax.axis_index("zh")}
    rows = p_ref.shape[0]
    greet([far])
    copy = remote(p_ref, landed, send, recv, far)
    copy.start()
    copy.wait()
    step = 16

    @pl.loop(0, rows // step)
    def _(j):
        at = pl.ds(pl.multiple_of(j * step, step), step)
        o_ref[at] = p_ref[at].astype(jnp.float32) + landed[at].astype(jnp.float32)


def pair_sum(p, cid):
    return pl.pallas_call(
        pair_kernel,
        out_shape=jax.ShapeDtypeStruct(p.shape, jnp.float32),
        in_specs=[pl.BlockSpec(memory_space=pltpu.VMEM)],
        out_specs=pl.BlockSpec(memory_space=pltpu.VMEM),
        scratch_shapes=[
            pltpu.VMEM(p.shape, p.dtype),
            pltpu.SemaphoreType.DMA,
            pltpu.SemaphoreType.DMA,
        ],
        compiler_params=pltpu.CompilerParams(
            collective_id=cid, has_side_effects=True, vmem_limit_bytes=32 * 2**20
        ),
    )(p)


def ring_of(axis, at):
    return {axis: lax.rem(at + 3, 4)}, {axis: lax.rem(at + 1, 4)}


def block_rows(row, column, start=0, size=160):
    return pl.ds(pl.multiple_of((row * 4 + column) * 160 + start, 16), size)


def send_blocks(ins, outs, here, send, recv):
    zl, c = lax.axis_index("zl"), lax.axis_index("c")
    mine = zl * 2 + c
    peers = [({"zl": 1 - zl, "c": k}, (1 - zl) * 2 + k) for k in range(2)]
    peers.append(({"c": 1 - c}, zl * 2 + 1 - c))
    n = len(ins)
    copies, keeps = [], []
    for i in range(n):
        for k, (peer, block) in enumerate(peers):
            landing = i * 3 + (c if k < 2 else 2)
            copy = remote(ins[i].at[block], outs[i].at[mine], send.at[i * 3 + k], recv.at[landing], peer)
            copy.start()
            copies.append(copy)
    for i in range(n):
        keep = pltpu.make_async_copy(ins[i].at[mine], outs[i].at[mine], here.at[i])
        keep.start()
        keeps.append(keep)

    def finish():
        for keep in keeps:
            keep.wait()
        for i in range(n):
            for k, (peer, block) in enumerate(peers):
                remote(
                    ins[i].at[block], outs[i].at[block], send.at[i * 3 + k], recv.at[i * 3 + k], peer
                ).wait_recv()
        for copy in copies:
            copy.wait_send()

    return finish


def group_peers():
    zl, c = lax.axis_index("zl"), lax.axis_index("c")
    return [{"c": 1 - c}, {"zl": 1 - zl, "c": 0}, {"zl": 1 - zl, "c": 1}]


def exchange_kernel(
    a_ref, g_ref, s_ref, tok_ref, cot_ref, order_ref, ao_ref, go_ref, so_ref, x_ref, dy_ref, here, send, recv
):
    greet(group_peers())
    finish = send_blocks([a_ref, g_ref, s_ref], [ao_ref, go_ref, so_ref], here, send, recv)
    reorder(tok_ref, order_ref, x_ref, False)
    reorder(cot_ref, order_ref, dy_ref, False)
    finish()


def group_exchange(arrays, tokens, cotangent, order, cid):
    n = len(arrays)
    like = lambda a, kind: jax.ShapeDtypeStruct(a.shape, kind)
    anywhere, vmem = pl.BlockSpec(memory_space=pl.ANY), pl.BlockSpec(memory_space=pltpu.VMEM)
    return pl.pallas_call(
        exchange_kernel,
        out_shape=[
            *(like(a, a.dtype) for a in arrays),
            like(tokens, jnp.float32),
            like(cotangent, jnp.bfloat16),
        ],
        in_specs=[anywhere] * n + [vmem] * 3,
        out_specs=[anywhere] * n + [vmem] * 2,
        scratch_shapes=[
            pltpu.SemaphoreType.DMA((n,)),
            pltpu.SemaphoreType.DMA((3 * n,)),
            pltpu.SemaphoreType.DMA((3 * n,)),
        ],
        compiler_params=pltpu.CompilerParams(
            collective_id=cid, has_side_effects=True, vmem_limit_bytes=32 * 2**20
        ),
    )(*arrays, tokens, cotangent, order)


ATTN, FEED = 768, 512
WIDE = ATTN + FEED


def shift(i, by):
    return lax.rem(i + by, 4)


def around(h, y, x):
    if h == 0:
        return x, ring_of("x", x), y, ring_of("y", y)
    return y, ring_of("y", y), x, ring_of("x", x)


class Piece:
    def __init__(self, h, source, target, columns, rows=160):
        self.h, self.source, self.target, self.columns, self.rows = h, source, target, columns, rows

    def own(self):
        return self.source

    def at(self, i1, i2, part=None):
        row, column = (i2, i1) if self.h == 0 else (i1, i2)
        size = self.rows if part is None else self.rows // 2
        first = (row * 4 + column) * self.rows + (0 if part is None else part * size)
        return self.target.at[pl.ds(pl.multiple_of(first, 16), size), self.columns]


def gather_steps(y, x, pieces, send, recv, cross):
    started = []

    def go(src, dst, n, ring, slot, peer):
        k = (n * 5 + ring) * 4 + slot
        copy = remote(src, dst, send.at[k], recv.at[k], peer)
        copy.start()
        started.append(copy)

    def arrived(dst, n, ring, slot):
        k = (n * 5 + ring) * 4 + slot
        remote(dst, dst, send.at[k], recv.at[k], {"c": 1 - lax.axis_index("c")}).wait_recv()

    each = [(n, p, *around(p.h, y, x)) for n, p in enumerate(pieces)]
    firsts = ((1, 0), (2, 3), (3, 1), (4, 2))

    def own_blocks():
        for n, p, i1, (back1, ahead1), i2, _ in each:
            go(p.own(), p.at(i1, i2), n, 0, 0, ahead1)
            go(p.own(), p.at(i1, i2), n, 0, 1, back1)
        for n, p, i1, _, i2, (back2, ahead2) in each:
            go(p.own(), p.at(i1, i2), n, 1, 0, ahead2)
            go(p.own(), p.at(i1, i2), n, 1, 1, back2)
            cross(n, p.own(), p.at(i1, i2))

    def first_axis():
        for n, p, i1, (back1, ahead1), i2, (back2, ahead2) in each:
            left, right = p.at(shift(i1, 3), i2), p.at(shift(i1, 1), i2)
            arrived(left, n, 0, 0)
            low = p.at(shift(i1, 3), i2, 0)
            go(low, low, n, 0, 2, ahead1)
            arrived(right, n, 0, 1)
            high = p.at(shift(i1, 1), i2, 1)
            go(high, high, n, 0, 3, back1)
            for ring, ref in ((2, left), (3, right)):
                go(ref, ref, n, ring, 0, ahead2)
                go(ref, ref, n, ring, 1, back2)
                cross(n, ref, ref)
        for n, p, i1, _, i2, (back2, ahead2) in each:
            far = shift(i1, 2)
            arrived(p.at(far, i2, 0), n, 0, 2)
            arrived(p.at(far, i2, 1), n, 0, 3)
            ref = p.at(far, i2)
            go(ref, ref, n, 4, 0, ahead2)
            go(ref, ref, n, 4, 1, back2)
            cross(n, ref, ref)

    def second_axis():
        for ring, by in firsts:
            for n, p, i1, _, i2, (back2, ahead2) in each:
                j = shift(i1, by)
                left, right = p.at(j, shift(i2, 3)), p.at(j, shift(i2, 1))
                arrived(left, n, ring, 0)
                low = p.at(j, shift(i2, 3), 0)
                go(low, low, n, ring, 2, ahead2)
                cross(n, left, left)
                arrived(right, n, ring, 1)
                high = p.at(j, shift(i2, 1), 1)
                go(high, high, n, ring, 3, back2)
                cross(n, right, right)

    def last():
        for ring, by in firsts:
            for n, p, i1, _, i2, _ in each:
                j, far = shift(i1, by), shift(i2, 2)
                arrived(p.at(j, far, 0), n, ring, 2)
                arrived(p.at(j, far, 1), n, ring, 3)
                cross(n, p.at(j, far), p.at(j, far))
        for copy in started:
            copy.wait_send()

    return own_blocks, first_axis, second_axis, last


def attention_gather_kernel(
    in_ref, g_ref, dy_ref, d_ref, a_ref, o_ref, go_ref, all_ref, do_ref,
    here, send, recv, csend, crecv, dsend, drecv, xhere, xsend, xrecv,
):
    y, x, c = lax.axis_index("y"), lax.axis_index("x"), lax.axis_index("c")
    zl, zh = lax.axis_index("zl"), lax.axis_index("zh")
    core = {"c": 1 - c}
    chips = [{"zl": 1 - zl, "zh": k} for k in range(2)]
    greet([*ring_of("x", x), *ring_of("y", y), core, *chips, {"zl": 1 - zl, "c": 1 - c}])
    whole = pl.ds(0, 160)

    for side in range(2):

        @pl.when(c == side)
        def _(side=side):
            sources = [
                in_ref.at[0, whole, pl.ds(0, 256)],
                in_ref.at[0, whole, pl.ds(256, 512)],
                in_ref.at[1, whole, pl.ds(0, 768)],
                g_ref,
            ]
            if side == 0:
                targets = [(a_ref, 0, 256), (a_ref, 256, 512), (a_ref, 768, 768)]
            else:
                targets = [(a_ref, 1536, 256), (o_ref, 0, 512), (o_ref, 512, 768)]
            targets.append((go_ref, 0, 128))
            pieces = [
                Piece(h, source, ref, pl.ds(first, width), rows)
                for h, source, (ref, first, width), rows in zip((0, 0, 1, 0), sources, targets, (160, 160, 160, 64))
            ]
            crossed = []

            def cross(n, src, dst):
                if n < 3:
                    k = len(crossed)
                    copy = remote(src, dst, csend.at[k], crecv.at[k], core)
                    copy.start()
                    crossed.append(copy)

            own_blocks, first_axis, second_axis, last = gather_steps(y, x, pieces, send, recv, cross)
            own_blocks()
            keeps = []
            for n, p in enumerate(pieces):
                i1, _, i2, _ = around(p.h, y, x)
                keeps.append(pltpu.make_async_copy(p.own(), p.at(i1, i2), here.at[n]))
                keeps[-1].start()
            finish = send_blocks([d_ref], [do_ref], xhere, xsend, xrecv)
            half = dy_ref.shape[0] // 2
            mine, other = zl * 2 + c, (1 - zl) * 2 + c
            part = pl.ds(pl.multiple_of(zh * half, half), half)
            away = [
                remote(dy_ref.at[part], all_ref.at[mine, part], dsend.at[k], drecv.at[zh], chips[k])
                for k in range(2)
            ]
            across = remote(dy_ref, all_ref.at[mine], dsend.at[2], drecv.at[2], core)
            for copy in (*away, across):
                copy.start()
            keeps.append(pltpu.make_async_copy(dy_ref, all_ref.at[mine], here.at[4]))
            keeps[-1].start()
            first_axis()
            second_axis()
            passed = []
            for k in range(2):
                rows = pl.ds(k * half, half)
                there = all_ref.at[other, rows]
                remote(dy_ref.at[rows], there, dsend.at[k], drecv.at[k], chips[k]).wait_recv()
                passed.append(remote(there, there, dsend.at[3 + k], drecv.at[3 + k], core))
                passed[-1].start()
            last()
            for copy in (*crossed, *passed, across):
                copy.wait()
            for copy in away:
                copy.wait_send()
            for keep in keeps:
                keep.wait()
            finish()


def attention_gather(own, gains, dy, down, cid):
    kind, dma = jnp.bfloat16, pltpu.SemaphoreType.DMA
    return pl.pallas_call(
        attention_gather_kernel,
        out_shape=[
            jax.ShapeDtypeStruct((2560, 1792), kind),
            jax.ShapeDtypeStruct((2560, 1280), kind),
            jax.ShapeDtypeStruct((1024, 128), kind),
            jax.ShapeDtypeStruct((4, *dy.shape), kind),
            jax.ShapeDtypeStruct(down.shape, kind),
        ],
        in_specs=[pl.BlockSpec(memory_space=pl.ANY)] * 4,
        out_specs=[pl.BlockSpec(memory_space=pl.ANY)] * 5,
        scratch_shapes=[
            dma((5,)),
            dma((80,)),
            dma((80,)),
            dma((48,)),
            dma((48,)),
            dma((5,)),
            dma((5,)),
            dma((1,)),
            dma((3,)),
            dma((3,)),
        ],
        compiler_params=pltpu.CompilerParams(collective_id=cid, has_side_effects=True),
    )(own, gains, dy, down)


def middle_kernel(
    p_ref, x_ref, g_ref, d_ref, mid_ref, all_ref, w_ref, landed, here, psend, precv, gsend, grecv, send, recv
):
    y, x, c = lax.axis_index("y"), lax.axis_index("x"), lax.axis_index("c")
    zl, zh = lax.axis_index("zl"), lax.axis_index("zh")
    core, far = {"c": 1 - c}, {"zh": 1 - zh}
    chips = [{"zl": 1 - zl, "zh": k} for k in range(2)]
    greet([*ring_of("x", x), *ring_of("y", y), core, far, *chips])
    half, step = p_ref.shape[0] // 2, 16
    mine, other = zl * 2 + c, (1 - zl) * 2 + c
    parts = [pl.ds(pl.multiple_of(k * half, half), half) for k in (1 - zh, zh)]
    pair = [
        remote(p_ref.at[part], landed.at[part], psend.at[k], precv.at[k], far)
        for k, part in enumerate(parts)
    ]
    for copy in pair:
        copy.start()
    pieces = [
        Piece(h, d_ref.at[h, pl.ds(0, 160)], w_ref, pl.ds(h * FEED, FEED)) for h in range(2)
    ]
    own_blocks, first_axis, second_axis, last = gather_steps(
        y, x, pieces, send, recv, lambda n, src, dst: None
    )
    own_blocks()
    keeps = []
    for n, p in enumerate(pieces):
        i1, _, i2, _ = around(p.h, y, x)
        keeps.append(pltpu.make_async_copy(p.own(), p.at(i1, i2), here.at[n]))
        keeps[-1].start()
    away, across = [], []
    for k in range(2):
        part = parts[1 - k]
        pair[k].wait_recv()
        first = (zh if k == 0 else 1 - zh) * half

        @pl.loop(0, half // step)
        def _(i, first=first):
            at = pl.ds(pl.multiple_of(first + i * step, step), step)
            branch = p_ref[at].astype(jnp.float32) + landed[at].astype(jnp.float32)
            v = x_ref[at] + branch
            mid_ref[at] = v
            r = lax.rsqrt(jnp.mean(v * v, axis=-1, keepdims=True) + norm_eps)
            all_ref[mine, at] = (v * r * g_ref[...]).astype(jnp.bfloat16)

        rows = all_ref.at[mine, part]
        if k == 0:
            for i in range(2):
                away.append(remote(rows, rows, gsend.at[i], grecv.at[zh], chips[i]))
                away[-1].start()
        across.append(remote(rows, rows, gsend.at[2 + k], grecv.at[2 + k], core))
        across[-1].start()
        if k == 0:
            first_axis()
    second_axis()
    passed = []
    for k in range(2):
        there = all_ref.at[other, pl.ds(k * half, half)]
        remote(there, there, gsend.at[k], grecv.at[k], chips[k]).wait_recv()
        passed.append(remote(there, there, gsend.at[4 + k], grecv.at[4 + k], core))
        passed[-1].start()
    last()
    for copy in (*across, *passed):
        copy.wait()
    for copy in (*away, *pair):
        copy.wait_send()
    for keep in keeps:
        keep.wait()


def middle(p, x, gain, down, cid):
    dma = pltpu.SemaphoreType.DMA
    anywhere, vmem = pl.BlockSpec(memory_space=pl.ANY), pl.BlockSpec(memory_space=pltpu.VMEM)
    return pl.pallas_call(
        middle_kernel,
        out_shape=[
            jax.ShapeDtypeStruct(x.shape, jnp.float32),
            jax.ShapeDtypeStruct((4, *x.shape), jnp.bfloat16),
            jax.ShapeDtypeStruct((2560, 2 * FEED), jnp.bfloat16),
        ],
        in_specs=[vmem, vmem, vmem, anywhere],
        out_specs=[vmem, vmem, anywhere],
        scratch_shapes=[
            pltpu.VMEM(p.shape, p.dtype),
            dma((2,)),
            dma((2,)),
            dma((2,)),
            dma((6,)),
            dma((6,)),
            dma((40,)),
            dma((40,)),
        ],
        compiler_params=pltpu.CompilerParams(
            collective_id=cid, has_side_effects=True, vmem_limit_bytes=32 * 2**20
        ),
    )(p, x, gain, down)


SEGMENTS = ((0, 0, 256), (256, 256, 512), (WIDE, 768, 768))


def plane_sum_kernel(
    a_ref, o_ref, f_ref, s_ref, p_ref, t_ref, x_ref, mid_ref, dmid_ref, g_ref, order_ref,
    attn_ref, feed_ref, so_ref, block_ref, grad_ref,
    sums, from_core, via, main, from_chip, attn_low, feed_low, gains,
    t_core, t_other, t_chips, t_own, t_far, landed, block_low, grad_low,
    here, csend, crecv, send, recv, esend, erecv, tsend, trecv, shere, ssend, srecv,
):
    y, x, c, zl, zh = (lax.axis_index(k) for k in ("y", "x", "c", "zl", "zh"))
    core, chip, far_peer = {"c": 1 - c}, {"zl": 1 - zl}, {"zh": 1 - zh}
    diagonal = {"zl": 1 - zl, "zh": 1 - zh}
    chips = [{"zl": 1 - zl, "zh": k} for k in range(2)]
    greet(
        [
            *ring_of("x", x), *ring_of("y", y), core, chip, far_peer, diagonal,
            {"zl": 1 - zl, "c": 1 - c},
        ]
    )
    step = 16
    f32, low = jnp.float32, jnp.bfloat16

    order = (2, 1, 3, 0)

    def chunk(q):
        return pl.ds(pl.multiple_of(shift(y, order[q]) * 640, 640), 640)

    def load(q, side, remote_side):
        rows = chunk(q)
        if side == 0:
            parts = [a_ref.at[rows, pl.ds(0, 256)], a_ref.at[rows, pl.ds(256, 512)], a_ref.at[rows, pl.ds(768, 768)]]
        else:
            parts = [a_ref.at[rows, pl.ds(1536, 256)], o_ref.at[rows, pl.ds(0, 512)], o_ref.at[rows, pl.ds(512, 768)]]
        out = []
        for s, (at, landing, width) in enumerate(SEGMENTS):
            k = q * 3 + s
            if remote_side:
                out.append(
                    remote(parts[s], from_core.at[rows, pl.ds(landing, width)], csend.at[k], crecv.at[k], core)
                )
            else:
                out.append(pltpu.make_async_copy(parts[s], sums.at[rows, pl.ds(at, width)], here.at[k]))
        return out

    def feed_load(q):
        rows = chunk(q)
        return [
            pltpu.make_async_copy(
                f_ref.at[rows, pl.ds(h * FEED, FEED)],
                sums.at[rows, pl.ds(h * WIDE + ATTN, FEED)],
                here.at[12 + q * 2 + h],
            )
            for h in range(2)
        ]

    for side in range(2):

        @pl.when(c == side)
        def _(side=side):
            for q in range(4):
                for copy in load(q, 1 - side, True):
                    copy.start()
                for copy in load(q, side, False):
                    copy.start()

    for q in range(4):
        for copy in feed_load(q):
            copy.start()
    finish = send_blocks([s_ref], [so_ref], shere, ssend, srecv)
    pair = remote(t_ref, landed, tsend.at[6], trecv.at[6], far_peer)
    pair.start()
    tokens = p_ref.shape[1]
    half = tokens // 2
    t_cores = [
        remote(p_ref.at[z * 2 + 1 - c], t_core.at[i], tsend.at[i], trecv.at[i], core)
        for i, z in enumerate((1 - zl, zl))
    ]
    for copy in t_cores:
        copy.start()
    t_sent = []

    def tokens_to_chips():
        t_cores[0].wait_recv()

        @pl.loop(0, tokens // step)
        def _(i):
            at = pl.ds(pl.multiple_of(i * step, step), step)
            total = p_ref[(1 - zl) * 2 + c, at].astype(f32) + t_core[0, at].astype(f32)
            t_other[at] = total.astype(low)

        for k in range(2):
            t_sent.append(
                remote(t_other.at[pl.ds(k * half, half)], t_chips.at[zh], tsend.at[2 + k], trecv.at[2 + zh], chips[k])
            )
            t_sent[-1].start()

    def tokens_to_far(k):
        piece = (1 - zh) if k == 0 else zh
        if k == 0:
            t_cores[1].wait_recv()
        else:
            for i in range(2):
                remote(
                    t_other.at[pl.ds(0, half)], t_chips.at[i], tsend.at[2 + i], trecv.at[2 + i], chips[i]
                ).wait_recv()

        @pl.loop(0, half // step)
        def _(i):
            at = pl.ds(pl.multiple_of(piece * half + i * step, step), step)
            total = p_ref[zl * 2 + c, at].astype(f32) + t_core[1, at].astype(f32)
            if k == 1:
                there = pl.ds(pl.multiple_of(i * step, step), step)
                total += t_chips[0, there].astype(f32) + t_chips[1, there].astype(f32)
            t_own[at] = total.astype(low)

        at = pl.ds(pl.multiple_of(piece * half, half), half)
        t_sent.append(remote(t_own.at[at], t_far.at[at], tsend.at[4 + k], trecv.at[4 + k], far_peer))
        t_sent[-1].start()

    def tokens_gradient():
        pair.wait_recv()

        @pl.loop(0, tokens // step)
        def _(i):
            at = pl.ds(pl.multiple_of(i * step, step), step)
            d = (t_ref[at].astype(f32) + landed[at].astype(f32)) * g_ref[...]
            v = x_ref[at]
            r = lax.rsqrt(jnp.mean(v * v, axis=-1, keepdims=True) + norm_eps)
            n = v * r
            d = r * (d - n * jnp.mean(d * n, axis=-1, keepdims=True))
            grad_low[at] = (dmid_ref[at] + d).astype(low)

        reorder(grad_low, order_ref, grad_ref, True)

    def tokens_output():
        for k in range(2):
            t_sent[2 + k].wait_recv()

        @pl.loop(0, tokens // step)
        def _(i):
            at = pl.ds(pl.multiple_of(i * step, step), step)
            branch = t_own[at].astype(f32) + t_far[at].astype(f32)
            block_low[at] = (mid_ref[at] + branch).astype(low)

        reorder(block_low, order_ref, block_ref, True)

    def columns(h):
        return pl.ds(h * WIDE, WIDE)

    def rows_at(h, i1, i2, start=0, size=160):
        row, column = (i2, i1) if h == 0 else (i1, i2)
        return block_rows(row, column, start, size)

    def add(h, first, size, terms):
        @pl.loop(0, size // step)
        def _(i):
            at = pl.ds(pl.multiple_of(first + i * step, step), step)
            total = sums[at, columns(h)].astype(f32)
            for ref, index, start in terms:
                total += ref[(*index, pl.ds(pl.multiple_of(start + i * step, step), step))].astype(f32)
            sums[at, columns(h)] = total.astype(low)

    started = []

    def go(h, ring, slot, src, dst, peer):
        k = (h * 5 + ring) * 4 + slot
        copy = remote(src, dst, send.at[k], recv.at[k], peer)
        copy.start()
        started.append(copy)

    def arrived(h, ring, slot, dst):
        k = (h * 5 + ring) * 4 + slot
        remote(dst, dst, send.at[k], recv.at[k], core).wait_recv()

    def first_row(h, i1, i2):
        row, column = (i2, i1) if h == 0 else (i1, i2)
        return (row * 4 + column) * 160

    def out_via(h, ring, place, at, ring_peers):
        back, ahead = ring_peers
        far = shift(at, 2)
        go(h, ring, 0, sums.at[place(far, 0, 80), columns(h)], via.at[h, ring, 0], ahead)
        go(h, ring, 1, sums.at[place(far, 80, 80), columns(h)], via.at[h, ring, 1], back)

    def out_main(h, ring, place, first, at, ring_peers):
        back, ahead = ring_peers
        arrived(h, ring, 0, via.at[h, ring, 0])
        add(h, first(shift(at, 1)), 80, [(via, (h, ring, 0), 0)])
        go(h, ring, 2, sums.at[place(shift(at, 1), 0, 160), columns(h)], main.at[h, ring, 0], ahead)
        arrived(h, ring, 1, via.at[h, ring, 1])
        add(h, first(shift(at, 3)) + 80, 80, [(via, (h, ring, 1), 0)])
        go(h, ring, 3, sums.at[place(shift(at, 3), 0, 160), columns(h)], main.at[h, ring, 1], back)

    def take(h, ring, first, at):
        arrived(h, ring, 2, main.at[h, ring, 0])
        arrived(h, ring, 3, main.at[h, ring, 1])
        add(h, first(at), 160, [(main, (h, ring, 0), 0), (main, (h, ring, 1), 0)])

    def along_second(h, j):
        i1, _, i2, peers = around(h, y, x)
        fixed = shift(i1, order[j])
        return (
            lambda k, start, size: rows_at(h, fixed, k, start, size),
            lambda k: first_row(h, fixed, k),
            i2,
            peers,
        )

    def along_first(h):
        i1, peers, i2, _ = around(h, y, x)
        return (
            lambda k, start, size: rows_at(h, k, i2, start, size),
            lambda k: first_row(h, k, i2),
            i1,
            peers,
        )

    for q in range(4):
        for copy in load(q, 0, False):
            copy.wait()
        for copy in feed_load(q):
            copy.wait()
        for copy in load(q, 0, True):
            copy.wait_recv()
        top = shift(y, order[q]) * 640

        @pl.loop(0, 640 // step)
        def _(i, top=top):
            at = pl.ds(pl.multiple_of(top + i * step, step), step)
            for place, landing, width in SEGMENTS:
                total = sums[at, pl.ds(place, width)].astype(f32) + from_core[
                    at, pl.ds(landing, width)
                ].astype(f32)
                sums[at, pl.ds(place, width)] = total.astype(low)

        if q == 0:
            for j in range(4):
                place, first, at, peers = along_second(0, j)
                out_via(0, j, place, at, peers)
        place, first, at, peers = along_second(1, q)
        out_via(1, q, place, at, peers)
        if q > 0:
            place, first, at, peers = along_second(1, q - 1)
            out_main(1, q - 1, place, first, at, peers)
        if q == 1:
            tokens_to_chips()
        if q == 2:
            tokens_to_far(0)
    for j in range(4):
        place, first, at, peers = along_second(0, j)
        out_main(0, j, place, first, at, peers)
        if j == 0:
            place, first, at, peers = along_second(1, 3)
            out_main(1, 3, place, first, at, peers)
        if j == 1:
            tokens_to_far(1)
        if j == 3:
            tokens_gradient()
    for j in range(4):
        for h in (1, 0):
            place, first, at, peers = along_second(h, j)
            take(h, j, first, at)
            if j == 0:
                place, first, at, peers = along_first(h)
                out_via(h, 4, place, at, peers)
    for h in (1, 0):
        place, first, at, peers = along_first(h)
        out_main(h, 4, place, first, at, peers)
    tokens_output()
    for h in (1, 0):
        place, first, at, peers = along_first(h)
        take(h, 4, first, at)
    home = (y * 4 + x) * 160
    theirs = pl.ds(pl.multiple_of(home + (1 - zl) * 80, 16), 80)
    yours = pl.ds(pl.multiple_of(home + zl * 80, 16), 80)
    tile = pl.ds(2 * WIDE - 128, 128)
    away = [
        remote(sums.at[theirs], from_chip, esend.at[0], erecv.at[0], chip),
        remote(sums.at[yours, tile], gains.at[0], esend.at[4], erecv.at[4], far_peer),
        remote(sums.at[theirs, tile], gains.at[1], esend.at[5], erecv.at[5], diagonal),
    ]
    for copy in away:
        copy.start()
    finish()
    for copy in away:
        copy.wait()
    is_gain = lax.broadcasted_iota(jnp.int32, (step, 128), 1) >= 64

    @pl.loop(0, 80 // step)
    def _(i):
        here_at = pl.ds(pl.multiple_of(home + zl * 80 + i * step, step), step)
        at = pl.ds(pl.multiple_of(i * step, step), step)
        for h in range(2):
            a = pl.ds(h * WIDE, ATTN)
            attn_low[at, pl.ds(h * ATTN, ATTN)] = sums[here_at, a].astype(f32) + from_chip[at, a].astype(f32)
            f = pl.ds(h * WIDE + ATTN, FEED)
            feed_low[0, at, pl.ds(h * FEED, FEED)] = sums[here_at, f].astype(f32)
            feed_low[1, at, pl.ds(h * FEED, FEED)] = from_chip[at, f].astype(f32)
        end = pl.ds(2 * FEED - 128, 128)
        for k in range(2):
            v = feed_low[k, at, end]
            feed_low[k, at, end] = jnp.where(is_gain, v + gains[k, at].astype(f32), v)

    ours = pl.ds(pl.multiple_of(c * 40, 8), 40)
    for_core = pl.ds(pl.multiple_of((1 - c) * 40, 8), 40)
    half = pl.ds(pl.multiple_of(c * 2 * ATTN, 128), 2 * ATTN)
    last = [remote(attn_low.at[for_core], attn_ref.at[:, half], esend.at[1], erecv.at[1], core)]
    keep = [pltpu.make_async_copy(attn_low.at[ours], attn_ref.at[:, half], here.at[0])]
    for k, source in enumerate((zl * 2 + c, (1 - zl) * 2 + c)):
        last.append(
            remote(feed_low.at[k, for_core], feed_ref.at[source], esend.at[2 + k], erecv.at[2 + k], core)
        )
        keep.append(pltpu.make_async_copy(feed_low.at[k, ours], feed_ref.at[source], here.at[1 + k]))
    for copy in (*last, *keep):
        copy.start()
    for copy in (*last, *keep):
        copy.wait()
    for copy in (*started, pair, *t_cores, *t_sent):
        copy.wait_send()
    for q in range(4):
        for copy in load(q, 0, True):
            copy.wait_send()


def plane_sum(a, o, f, sent, down, d_xn, x, mid, d_mid, gain, order, cid):
    low, dma, f32 = jnp.bfloat16, pltpu.SemaphoreType.DMA, jnp.float32
    rows, width = x.shape
    anywhere, vmem = pl.BlockSpec(memory_space=pl.ANY), pl.BlockSpec(memory_space=pltpu.VMEM)
    return pl.pallas_call(
        plane_sum_kernel,
        out_shape=[
            jax.ShapeDtypeStruct((40, 4 * ATTN), f32),
            jax.ShapeDtypeStruct((4, 40, 2 * FEED), f32),
            jax.ShapeDtypeStruct(sent.shape, low),
            jax.ShapeDtypeStruct(x.shape, low),
            jax.ShapeDtypeStruct(x.shape, low),
        ],
        in_specs=[anywhere] * 4 + [vmem] * 7,
        out_specs=[vmem, vmem, anywhere, vmem, vmem],
        scratch_shapes=[
            pltpu.VMEM((2560, 2 * WIDE), low),
            pltpu.VMEM((2560, 2 * ATTN), low),
            pltpu.VMEM((2, 5, 2, 80, WIDE), low),
            pltpu.VMEM((2, 5, 2, 160, WIDE), low),
            pltpu.VMEM((80, 2 * WIDE), low),
            pltpu.VMEM((80, 2 * ATTN), f32),
            pltpu.VMEM((2, 80, 2 * FEED), f32),
            pltpu.VMEM((2, 80, 128), low),
            pltpu.VMEM((2, rows, width), low),
            pltpu.VMEM((rows, width), low),
            pltpu.VMEM((2, rows // 2, width), low),
            pltpu.VMEM((rows, width), low),
            pltpu.VMEM((rows, width), low),
            pltpu.VMEM((rows, width), low),
            pltpu.VMEM((rows, width), low),
            pltpu.VMEM((rows, width), low),
            dma((20,)),
            dma((12,)),
            dma((12,)),
            dma((40,)),
            dma((40,)),
            dma((6,)),
            dma((6,)),
            dma((7,)),
            dma((7,)),
            dma((1,)),
            dma((3,)),
            dma((3,)),
        ],
        compiler_params=pltpu.CompilerParams(
            collective_id=cid, has_side_effects=True, vmem_limit_bytes=56 * 2**20
        ),
    )(a, o, f, sent, down, d_xn, x, mid, d_mid, gain, order)


def grads_kernel(l_ref, r_ref, o_ref):
    o_ref[...] = lax.dot_general(
        l_ref[0], r_ref[0], (((0,), (0,)), ((), ())), preferred_element_type=jnp.float32
    ).astype(o_ref.dtype)


def pair_of_grads(left, right):
    n, depth, rows = left.shape
    columns, tile = right.shape[2], 256
    per = columns // tile
    return pl.pallas_call(
        grads_kernel,
        grid=(n, per),
        out_shape=jax.ShapeDtypeStruct((rows, n * columns), jnp.bfloat16),
        in_specs=[
            pl.BlockSpec((1, depth, rows), lambda b, j: (b, 0, 0)),
            pl.BlockSpec((1, depth, tile), lambda b, j: (b, 0, j)),
        ],
        out_specs=pl.BlockSpec((rows, tile), lambda b, j: (0, b * per + j)),
        compiler_params=pltpu.CompilerParams(vmem_limit_bytes=40 * 2**20),
        cost_estimate=pl.CostEstimate(
            flops=2 * n * depth * rows * columns,
            bytes_accessed=2 * n * (depth * rows + depth * columns + rows * columns),
            transcendentals=0,
        ),
    )(left, right)


def rms_norm(values, gain_row):
    return (
        values * lax.rsqrt(jnp.mean(values * values, axis=-1, keepdims=True) + norm_eps) * gain_row
    )


def geglu(gate_part, up_part):
    return jax.nn.gelu(gate_part) * up_part


def tables():
    half_rot = ROT // 2
    rates = jnp.exp(jnp.arange(half_rot, dtype=jnp.float32) * (-2.0 * math.log(10000.0) / ROT))
    angles = jnp.arange(SEQ_LEN, dtype=jnp.float32)[:, None] * rates[None, :]
    return (jnp.cos(angles), jnp.sin(angles))


def rotate(field, cosine, sine):
    half_rot = ROT // 2
    first = field[..., :half_rot]
    second = field[..., half_rot:ROT]
    return jnp.concatenate(
        [first * cosine - second * sine, second * cosine + first * sine, field[..., ROT:]], axis=-1
    )


def contract(left, right, left_dim, right_dim):
    return lax.dot_general(
        left, right, (((left_dim,), (right_dim,)), ((), ())), preferred_element_type=jnp.float32
    )


def padded(weight):
    return jnp.pad(weight.reshape(40, 4, 960), ((0, 0), (0, 0), (0, 64)))


def joined(slices):
    return slices[:, :, :960].transpose(1, 0, 2).reshape(40, 3840).astype(jnp.float32)


def local(
    tokens,
    attn_gain,
    query_weight,
    kv_weight,
    out_weight,
    mlp_gain,
    gate_weight,
    up_weight,
    down_weight,
    cotangent,
):
    low = jnp.bfloat16
    rows = tokens.shape[0]
    seqs = rows // SEQ_LEN
    heads_here = query_weight.shape[1] // HEAD_DIM
    wide = heads_here * HEAD_DIM
    scale = HEAD_DIM ** (-0.5)
    cosine, sine = tables()
    positions = jnp.arange(SEQ_LEN)
    keep_mask = (positions[:, None] >= positions[None, :]) & (
        positions[:, None] - positions[None, :] < WINDOW
    )
    attn = jnp.concatenate([query_weight, kv_weight, out_weight.T], axis=1)
    attn = attn.reshape(40, 2, 2, ATTN).transpose(1, 2, 0, 3)
    attn = jnp.broadcast_to(attn, (2, *attn.shape)).reshape(4, 2, 40, ATTN)
    first = attn.reshape(4, 80, ATTN)
    gains = jnp.pad(jnp.stack([attn_gain, mlp_gain], axis=0), ((0, 14), (0, 88)))
    gains = jnp.broadcast_to(gains, (4, 16, 128))
    down = padded(down_weight.T).reshape(40, 4, 2, FEED).transpose(1, 2, 0, 3).reshape(4, 80, FEED)
    second = jnp.stack([padded(gate_weight), padded(up_weight)], axis=0)
    second = second.transpose(2, 0, 1, 3).reshape(4, 80, 2 * FEED)
    order = jnp.asarray(feature_order(), low)
    first, gains, second, x_in, dy_here = group_exchange(
        [first, gains, second], tokens, cotangent, order, 5
    )
    second = second.reshape(4, 2, 40, 2 * FEED).transpose(0, 2, 1, 3).reshape(160, 4 * FEED)
    w_gate_up = lax.all_gather(second, PLANE, axis=0, tiled=True)
    first = first.reshape(4, 2, 40, ATTN).transpose(1, 0, 2, 3).reshape(2, 160, ATTN)
    w_q_kv, w_out_t, gains, dy, down = attention_gather(first, gains.reshape(64, 128), dy_here, down, 6)
    gains = gains.reshape(64, 16, 128)[:, :2, :40].transpose(1, 0, 2).reshape(2, 2560).astype(jnp.float32)
    down = down.reshape(4, 2, 40, FEED).transpose(1, 0, 2, 3).reshape(2, 160, FEED)
    dy = dy.reshape(4 * rows, -1)
    gain_one, gain_two = gains[0], gains[1]

    xn_one = rms_norm(x_in, gain_one).astype(low)
    q_kv_pre = jnp.dot(xn_one, w_q_kv, preferred_element_type=jnp.float32)
    q_pre, kv_pre = q_kv_pre[:, :wide], q_kv_pre[:, wide:]
    queries = rotate(
        q_pre.reshape(seqs, SEQ_LEN, heads_here, HEAD_DIM), cosine[:, None, :], sine[:, None, :]
    ).astype(low)
    key_rot = rotate(kv_pre[:, :HEAD_DIM].reshape(seqs, SEQ_LEN, HEAD_DIM), cosine, sine).astype(low)
    value_rows = kv_pre[:, HEAD_DIM:].reshape(seqs, SEQ_LEN, HEAD_DIM).astype(low)

    def score_rows():
        raw = (
            jnp.einsum("sqhd,skd->shqk", queries, key_rot, preferred_element_type=jnp.float32)
            * scale
        )
        return jnp.where(keep_mask, raw, -1e30)

    scores = score_rows()
    row_max = jnp.max(scores, axis=-1, keepdims=True)
    log_total = row_max + jnp.log(jnp.sum(jnp.exp(scores - row_max), axis=-1, keepdims=True))
    attn_probs = jnp.exp(scores - log_total).astype(low)
    mixed_heads = jnp.einsum(
        "shqk,skd->sqhd", attn_probs, value_rows, preferred_element_type=jnp.float32
    )
    mixed_heads = mixed_heads.reshape(rows, wide).astype(low)
    attn_part = contract(mixed_heads, w_out_t, 1, 1).astype(low)
    x_mid, xn_all, w_down_t = middle(attn_part, x_in, gain_two[None, :], down, 2)
    xn_all = xn_all.reshape(4 * rows, -1)
    gate_up = jnp.dot(xn_all, w_gate_up, preferred_element_type=jnp.float32)
    gate_pre, up_pre = gate_up[:, : 2 * FEED], gate_up[:, 2 * FEED :]
    hidden = geglu(gate_pre, up_pre).astype(low)
    down_part = contract(hidden, w_down_t, 1, 1).astype(low)
    d_hidden = jnp.dot(dy, w_down_t, preferred_element_type=jnp.float32)
    geglu_pull = jax.vjp(geglu, gate_pre, up_pre)[1]
    d_gate_pre, d_up_pre = geglu_pull(d_hidden)
    d_gate_low = d_gate_pre.astype(low)
    d_up_low = d_up_pre.astype(low)
    d_xn_two_part = contract(jnp.concatenate([d_gate_low, d_up_low], axis=1), w_gate_up, 1, 1)
    d_xn_two = token_sum(d_xn_two_part.astype(low).reshape(4, rows, -1), 3)
    sent = pair_of_grads(jnp.stack([dy, xn_all]), jnp.stack([hidden, d_gate_low]))
    sent = lax.psum_scatter(sent, PLANE, scatter_dimension=0, tiled=True)
    sent = sent.reshape(4, 40, 2, 2 * FEED).transpose(0, 2, 1, 3).reshape(4, 80, 2 * FEED)

    norm_two_pull = jax.vjp(rms_norm, x_mid, gain_two)[1]
    d_mid_norm, d_gain_two = norm_two_pull(d_xn_two)
    d_mid = dy_here.astype(jnp.float32) + d_mid_norm
    d_mid_low = d_mid.astype(low)
    d_out_t = contract(d_mid_low, mixed_heads, 0, 0)
    d_mixed = (
        jnp.dot(d_mid_low, w_out_t, preferred_element_type=jnp.float32)
        .astype(low)
        .reshape(seqs, SEQ_LEN, heads_here, HEAD_DIM)
    )
    soft_rows = jnp.exp(score_rows() - log_total)
    d_probs = jnp.einsum("sqhd,skd->shqk", d_mixed, value_rows, preferred_element_type=jnp.float32)
    d_scores = (
        soft_rows * (d_probs - jnp.sum(soft_rows * d_probs, axis=-1, keepdims=True))
    ).astype(low)
    d_queries = (
        jnp.einsum("shqk,skd->sqhd", d_scores, key_rot, preferred_element_type=jnp.float32) * scale
    )
    d_keys = (
        jnp.einsum("shqk,sqhd->skd", d_scores, queries, preferred_element_type=jnp.float32) * scale
    )
    d_values = jnp.einsum("shqk,sqhd->skd", attn_probs, d_mixed, preferred_element_type=jnp.float32)
    d_q_pre = (
        rotate(d_queries, cosine[:, None, :], -sine[:, None, :]).reshape(rows, wide).astype(low)
    )
    d_k_pre = rotate(d_keys, cosine, -sine).reshape(rows, HEAD_DIM)
    d_kv_part = jnp.concatenate([d_k_pre, d_values.reshape(rows, HEAD_DIM)], axis=-1)
    d_kv_low = pair_sum(d_kv_part.astype(low), 4).astype(low)
    d_q_kv_w = contract(xn_one, jnp.concatenate([d_q_pre, d_kv_low], axis=1), 0, 0).astype(low)
    d_xn_one = contract(jnp.concatenate([d_q_pre, d_kv_low * 0.5], axis=1), w_q_kv, 1, 1)
    norm_one_pull = jax.vjp(lambda g: rms_norm(x_in, g), gain_one)[1]
    d_gain_one = norm_one_pull(d_xn_one)[0]
    d_gains = jnp.pad(jnp.stack([d_gain_one, 0.5 * d_gain_two], axis=0).astype(low), ((0, 14), (0, 0)))
    chosen = jnp.asarray(np.eye(16, 2 * FEED, 960) * (np.arange(16) < 2)[:, None], low)
    d_up_w = contract(
        jnp.concatenate([xn_all, d_gains], axis=0),
        jnp.concatenate([d_up_low, chosen], axis=0),
        0,
        0,
    ).astype(low)
    attn_out, up_out, sent, block_out, tokens_grad = plane_sum(
        d_q_kv_w,
        d_out_t.astype(low),
        d_up_w,
        sent,
        down_part.reshape(4, rows, -1),
        d_xn_one.astype(low),
        x_in,
        x_mid,
        d_mid,
        gain_one[None, :],
        order,
        7,
    )
    sent = sent.reshape(4, 2, 40, 2 * FEED)
    gain_out = up_out[:, :, 960:962].sum(axis=0)
    return (
        block_out,
        tokens_grad,
        gain_out[:, 0],
        attn_out[:, :wide],
        attn_out[:, wide : wide + 2 * HEAD_DIM],
        attn_out[:, wide + 2 * HEAD_DIM :].T,
        gain_out[:, 1],
        joined(sent[:, 1]),
        joined(up_out),
        joined(sent[:, 0]).T,
    )


def solution(mesh):
    fine = Mesh(mesh.devices.reshape(4, 2, 4, 2, 2), AXES)
    dp = ("y", "zl", "x", "c")
    in_specs = (
        P(dp, None),
        P(dp),
        P(dp, "zh"),
        P(dp, None),
        P("zh", dp),
        P(dp),
        P(dp, "zh"),
        P(dp, "zh"),
        P("zh", dp),
        P(dp, None),
    )
    out_specs = (
        P(dp, None),
        P(dp, None),
        P(dp),
        P(dp, "zh"),
        P(dp, None),
        P("zh", dp),
        P(dp),
        P(dp, "zh"),
        P(dp, "zh"),
        P("zh", dp),
    )
    return jax.shard_map(local, mesh=fine, in_specs=in_specs, out_specs=out_specs, check_vma=False)
```

time: 556 us -> 436 us (0.78)
  Pallas kernels: 367 us -> 291 us
  matrix products: 91 us -> 71 us
  local copies, waits for them, and re-layouts: 59.8 us -> 40.5 us
  other arithmetic: 14.6 us -> 8.04 us
    pallas_call x2 -> x1, Pallas kernels: 38.7 us -> 6.55 us  [pair_sum(): pl.pallas_call(pair_kernel, out_shape=jax.ShapeDtypeStruct(p.shape, jnp.f...]
    pallas_call x4, Pallas kernels: 172 us -> 141 us  [the longest x1 80.7 us: attention_gather(): pl.pallas_call(attention_gather_kernel, out_shape=[jax.ShapeDtypeStruct((...]
    pallas_call x2 -> x1, Pallas kernels: 55.9 us -> 28.4 us  [token_sum(): pl.pallas_call(sum_kernel, out_shape=jax.ShapeDtypeStruct((rows, width),...]
    dot_general x11 -> x7, matrix products: 60.1 us -> 43.5 us  [contract(): lax.dot_general(left, right, (((left_dim,), (right_dim,)), ((), ())), pre...]
    dot_general x2 -> x0, local copies, waits for them, and re-layouts: 15.6 us -> none  [local(): q_pre = jnp.dot(xn_one, w_query, preferred_element_type=jnp.float32)]
    pallas_call x1, Pallas kernels: 101 us -> 115 us  [plane_sum(): pl.pallas_call(plane_sum_kernel, out_shape=[jax.ShapeDtypeStruct((40, 4 *...]
    unnamed x83 -> x96, local copies, waits for them, and re-layouts: 10.3 us -> 14.1 us
  transfers between devices with their start and end apart: 3 -> 2, of which waited for: 0 -> 1; matrix products, arithmetic and copies ran while one was open for 23% -> 17% of each run, Pallas kernels for 61% -> 35%
where the time goes in v2:
time: 436 us; the launch traced here: 428 us
  Pallas kernels  291 us (67%)
  matrix products  71 us (16%)
  local copies, waits for them, and re-layouts  40.5 us (9%)
  between operations  15.2 us (3%)
  other arithmetic  8.04 us (2%)
    pallas_call x1, Pallas kernels, plane_sum(): pl.pallas_call(plane_sum_kernel, out_shape=[jax.ShapeDtypeStruct((40, 4 *...  115 us
    pallas_call x1, Pallas kernels, attention_gather(): pl.pallas_call(attention_gather_kernel, out_shape=[jax.ShapeDtypeStruct((...  80.7 us
    dot_general x7, matrix products, contract(): lax.dot_general(left, right, (((left_dim,), (right_dim,)), ((), ())), pre...  43.5 us
    pallas_call x1, Pallas kernels, middle(): pl.pallas_call(middle_kernel, out_shape=[jax.ShapeDtypeStruct(x.shape, jn...  34.7 us
    pallas_call x1, Pallas kernels, token_sum(): pl.pallas_call(sum_kernel, out_shape=jax.ShapeDtypeStruct((rows, width),...  28.4 us
    pallas_call x1, Pallas kernels, group_exchange(): pl.pallas_call(exchange_kernel, out_shape=[*(like(a, a.dtype) for a in ar...  16.8 us
    unnamed x96, local copies, waits for them, and re-layouts  14.1 us
    dot_general x1, matrix products, local(): gate_up = jnp.dot(xn_all, w_gate_up, preferred_element_type=jnp.float32)  9.22 us
  transfers between devices with their start and end apart: 2, of which 1 were waited for; matrix products, arithmetic and copies ran while one was open for 17% of the time, Pallas kernels for 35%

profile of v2, /device:TPU:1, one launch (start us, length us, event | category | flops | bytes accessed | tf_op | source)
XLA Modules:
  0.0 428.4 jit_solution(10087930428289368947)
XLA Ops:
  7.3 1.0 pad_maximum_fusion.9
  8.5 1.4 reshape.423
  10.0 0.5 reshape.424
  10.9 0.8 copy-done.3
  12.0 16.8 %shard_map.195 = (bf16[4,80,768]{2,1,0:T(8,128)(2,1)S(1)}, bf16[4,16,128]{2,1,0:T(8,128)(2,1)S(1)}, bf16[4,80,1024]{2,1,0:T(8,128)(2,1)S(1)}, f32[128,2560]{1,0:T(8,128)S(1)}, bf16[128,2560]{1,0:T(8,128)(2,1)S(1)}) custom-call(bf16[4,80,768]{2,1,0:T(8,128)(2,1)S(1)} %bitcast.152, bf16[4,16,128]{2,1,0:T(8,128)(2,1)S(1)} %broadcast_in_dim.17.g_ref, ...), custom_call_target="tpu_custom_call" | custom-call | tf_op jit(solution)/shard_map/pallas_call | solution.py:235
  28.8 0.8 copy-done.6
  29.7 0.6 copy-done.10
  30.3 0.7 copy.111
  30.9 1.0 copy.138
  32.0 0.5 reshape.429
  32.9 0.8 copy.102
  33.6 0.8 copy.100
  34.5 80.7 %shard_map.196 = (bf16[2560,1792]{1,0:T(8,128)(2,1)}, bf16[2560,1280]{1,0:T(8,128)(2,1)}, bf16[1024,128]{1,0:T(8,128)(2,1)}, bf16[4,128,2560]{2,1,0:T(8,128)(2,1)}, bf16[4,80,512]{2,1,0:T(8,128)(2,1)}) custom-call(bf16[2,160,768]{2,1,0:T(8,128)(2,1)} %bitcast.173, bf16[64,128]{1,0:T(8,128)(2,1)} %bitcast.156, bf16[128,2560]{1,0:T(8,128)(2,1)} %copy-done.6, ...), custom_call_target="tpu_custom_call" | custom-call | tf_op jit(solution)/shard_map/pallas_call | solution.py:437
  115.2 0.9 slice.140
  116.1 1.0 copy.110
  117.5 5.2 %fusion.66 = f32[128,1792]{1,0:T(8,128)S(1)} fusion(bf16[2560,1792]{1,0:T(8,128)(2,1)} %get-tuple-element.33, f32[128,2560]{1,0:T(8,128)S(1)} %get-tuple-element.28.x_ref, f32[2560]{0:T(1024)S(1)} %mul.457, f32[128]{0:T(128)S(1)} %add_rsqrt_fusion), kind=kOutput, calls=%fused_computation.142 | convolution fusion | flops 1175388160 | bytes 11414016 | tf_op jit(solution)/shard_map/dot_general | solution.py:1051
  122.8 1.1 copy.104
  123.9 1.0 slice.149
  124.9 0.8 copy.137
  125.7 1.0 fusion.68
  127.8 1.4 fusion.70
  129.6 5.3 %convolution_convert_fusion.5.p_ref = bf16[128,2560]{1,0:T(8,128)(2,1)S(1)} fusion(bf16[128,1280]{0,1:T(8,128)(2,1)S(1)} %bitcast.161, bf16[2560,1280]{1,0:T(8,128)(2,1)} %get-tuple-element.35), kind=kOutput, calls=%fused_computation.6 | convolution fusion | flops 839188480 | bytes 7536640 | tf_op jit(solution)/shard_map/dot_general | solution.py:992
  135.0 34.7 %shard_map.197 = (f32[128,2560]{1,0:T(8,128)S(1)}, bf16[4,128,2560]{2,1,0:T(8,128)(2,1)S(1)}, bf16[2560,1024]{1,0:T(8,128)(2,1)S(1)}) custom-call(bf16[128,2560]{1,0:T(8,128)(2,1)S(1)} %convolution_convert_fusion.5.p_ref, f32[128,2560]{1,0:T(8,128)S(1)} %get-tuple-element.28.x_ref, f32[1,2560]{1,0:T(1,128)S(1)} %slice.119.g_ref, ...), custom_call_target="tpu_custom_call" | custom-call | tf_op jit(solution)/shard_map/pallas_call | solution.py:536
  169.7 2.3 copy-done.11
  172.0 1.5 copy-done.4
  173.5 2.8 pad_maximum_fusion.l_ref
  176.3 9.2 %fusion.71 = f32[512,2048]{1,0:T(8,128)S(1)} fusion(bf16[512,2560]{1,0:T(8,128)(2,1)} %bitcast.148, bf16[2560,2048]{1,0:T(8,128)(2,1)} %all-gather.2.cloned.1.call-done), kind=kOutput, calls=%fused_computation.147 | convolution fusion | flops 5368709120 | bytes 17301504 | tf_op jit(solution)/shard_map/dot_general | solution.py:1077
  185.5 5.2 %fusion.9 = (bf16[512,1024]{1,0:T(8,128)(2,1)S(1)}, bf16[512,1024]{1,0:T(8,128)(2,1)}, bf16[512,1024]{1,0:T(8,128)(2,1)S(1)}) fusion(f32[512,2048]{1,0:T(8,128)S(1)} %fusion.71, bf16[512,2560]{1,0:T(8,128)(2,1)S(1)} %bitcast.166, bf16[2560,1024]{1,0:T(8,128)(2,1)S(1)} %copy-done.12), kind=kOutput, calls=%fused_computation.19 | convolution fusion | flops 2697986048 | bytes 15204352 | tf_op jit(solution)/shard_map/dot_general | solution.py:1081
  190.8 1.0 copy-done.20
  191.8 0.3 copy-done.22
  192.3 9.2 %shard_map.200 = bf16[2560,2048]{1,0:T(8,128)(2,1)} custom-call(bf16[2,512,2560]{2,1,0:T(8,128)(2,1)S(1)} %copy-done.2, bf16[2,512,1024]{2,1,0:T(8,128)(2,1)S(1)} %pad_maximum_fusion.1.r_ref), custom_call_target="tpu_custom_call" | custom-call | flops 5368709120 | bytes 17825792 | tf_op jit(solution)/shard_map/pallas_call | solution.py:947
  201.6 0.7 copy-done.33
  202.4 0.7 slice.128.g_ref
  203.3 9.0 %convolution_convert_fusion.4 = bf16[512,2560]{1,0:T(8,128)(2,1)S(1)} fusion(bf16[2560,2048]{1,0:T(8,128)(2,1)} %all-gather.2.cloned.1.call-done, bf16[512,1024]{1,0:T(8,128)(2,1)} %get-tuple-element.53, bf16[512,1024]{1,0:T(8,128)(2,1)} %copy-done.22), kind=kOutput, calls=%fused_computation.5 | convolution fusion | flops 5374214144 | bytes 15204352 | tf_op jit(solution)/shard_map/dot_general | solution.py:992
  212.2 28.4 %shard_map.198 = f32[128,2560]{1,0:T(8,128)S(1)} custom-call(bf16[4,128,2560]{2,1,0:T(8,128)(2,1)S(1)} %bitcast.150), custom_call_target="tpu_custom_call" | custom-call | tf_op jit(solution)/shard_map/pallas_call | solution.py:123
  240.7 0.5 multiply_reduce_fusion
  241.2 0.6 copy-done.7
  241.8 0.4 fusion.13.dmid_ref
  242.2 1.1 copy-done.13
  243.2 4.0 convolution_convert_fusion.6
  247.6 1.2 multiply_reduce_fusion.5
  249.9 6.6 %shard_map.199 = f32[128,512]{1,0:T(8,128)S(1)} custom-call(bf16[128,512]{1,0:T(8,128)(2,1)S(1)} %pad_maximum_fusion.10.p_ref), custom_call_target="tpu_custom_call" | custom-call | tf_op jit(solution)/shard_map/pallas_call | solution.py:160
  257.7 7.9 %fusion.67 = (bf16[128,2560]{1,0:T(8,128)(2,1)}, bf16[2560]{0:T(1024)(128)(2,1)S(1)}) fusion(f32[128,2560]{1,0:T(8,128)S(1)} %get-tuple-element.28.x_ref, f32[128]{0:T(128)S(1)} %add_rsqrt_fusion, bf16[2560,1792]{1,0:T(8,128)(2,1)} %get-tuple-element.33, bf16[128,1280]{0,1:T(8,128)(2,1)S(1)} %bitcast.163, bf16[128,512]{0,1:T(8,128)(2,1)S(1)} %copy.120), kind=kOutput, calls=%fused_computation.143 | convolution fusion | flops 1176630784 | bytes 11605504 | tf_op jit(solution)/shard_map/dot_general | solution.py:992
  265.6 4.7 %convolution_convert_fusion.o_ref = bf16[2560,1280]{1,0:T(8,128)(2,1)} fusion(bf16[128,1280]{0,1:T(8,128)(2,1)S(1)} %bitcast.162, f32[128,2560]{1,0:T(8,128)S(1)} %copy-done.14), kind=kOutput, calls=%fused_computation | convolution fusion | flops 842465280 | bytes 8192000 | tf_op jit(solution)/shard_map/dot_general | solution.py:992
  270.4 6.3 %convolution_convert_fusion.1.a_ref = bf16[2560,1792]{1,0:T(8,128)(2,1)} fusion(bf16[128,1280]{0,1:T(8,128)(2,1)S(1)} %bitcast.164, bf16[128,512]{0,1:T(8,128)(2,1)S(1)} %copy.119, f32[128,2560]{1,0:T(8,128)S(1)} %get-tuple-element.28.x_ref, f32[2560]{0:T(1024)S(1)} %copy-done.27, f32[128]{0:T(128)S(1)} %add_rsqrt_fusion), kind=kOutput, calls=%fused_computation.1 | convolution fusion | flops 1180893184 | bytes 10955264 | tf_op jit(solution)/shard_map/dot_general | solution.py:992
  276.6 6.2 %convolution_convert_fusion.2.f_ref = bf16[2560,1024]{1,0:T(8,128)(2,1)} fusion(bf16[16,2560]{1,0:T(8,128)(2,1)S(1)} %fusion.35, bf16[512,2560]{1,0:T(8,128)(2,1)S(1)} %bitcast.149, bf16[16,1024]{1,0:T(8,128)(2,1)S(1)} %copy-done.41, bf16[512,1024]{1,0:T(8,128)(2,1)S(1)} %copy-done.42), kind=kOutput, calls=%fused_computation.2 | convolution fusion | flops 2778431488 | bytes 9027584 | tf_op jit(solution)/shard_map/dot_general | solution.py:992
  282.8 4.3 convolution_convert_fusion.3
  287.1 2.5 reduce-scatter.2.cloned.1.call-done
  289.6 2.3 reshape.447
  291.9 1.0 copy.121
  292.9 114.7 %shard_map.201 = (f32[40,3072]{1,0:T(8,128)}, f32[4,40,1024]{2,1,0:T(8,128)}, bf16[4,80,1024]{2,1,0:T(8,128)(2,1)}, bf16[128,2560]{1,0:T(8,128)(2,1)}, bf16[128,2560]{1,0:T(8,128)(2,1)}) custom-call(bf16[2560,1792]{1,0:T(8,128)(2,1)} %convolution_convert_fusion.1.a_ref, bf16[2560,1280]{1,0:T(8,128)(2,1)} %convolution_convert_fusion.o_ref, ...), custom_call_target="tpu_custom_call" | custom-call | tf_op jit(solution)/shard_map/pallas_call | solution.py:890
  407.6 1.0 slice_reduce_fusion
  408.6 1.1 slice_bitcast_fusion
  409.7 1.6 slice.132
  411.3 1.8 slice_bitcast_fusion.3
  413.1 0.7 slice_reduce_fusion.1
  413.8 0.4 copy.123
  414.3 1.4 reshape.451
  415.8 0.4 copy.124
  416.3 1.4 reshape.453
  417.8 0.4 copy.122
  418.2 1.4 reshape.452
  419.7 0.8 copy.142
  420.5 0.8 copy.143
  (145 shorter events, 6.5 us)
Async XLA Ops:
  7.2 2.9 copy-start.28
  7.2 3.5 copy-start.39
  7.2 3.5 copy-start.40
  7.2 169.1 %all-gather.2.cloned.1.call-start = ((), (), s32[]{:S(2)}) async-start(), calls=%async_computation.1 | async-start | bytes 11141120 | tf_op jit(solution)/shard_map/all_gather | solution.py:1042
  10.5 1.1 copy-start.3
  10.5 1.3 copy-start.8
  10.5 1.5 copy-start.9
  28.8 0.8 copy-start.6
  29.6 0.6 copy-start.10
  30.3 240.1 %copy-start = (f32[128,2560]{1,0:T(8,128)}, f32[128,2560]{1,0:T(8,128)S(1)}, u32[]{:S(2)}) copy-start(f32[128,2560]{1,0:T(8,128)S(1)} %get-tuple-element.28.x_ref) | copy-start | bytes 3932164
  30.3 1.8 copy-start.29
  32.0 257.6 %reduce-scatter.2.cloned.1.call-start = ((), (), s32[]{:S(2)}) async-start(), calls=%async_computation.2 | async-start | bytes 11141120 | tf_op jit(solution)/shard_map/reduce_scatter | solution.py:1089
  117.1 5.6 %copy-start.30 = (f32[1,64,40]{2,1,0:T(8,128)}, f32[1,64,40]{2,1,0:T(8,128)S(1)}, u32[]{:S(2)}) copy-start(f32[1,64,40]{2,1,0:T(8,128)S(1)} %get-tuple-element.72) | copy-start | bytes 30724
  117.1 5.6 %copy-start.32 = (f32[1,64,40]{2,1,0:T(8,128)}, f32[1,64,40]{2,1,0:T(8,128)S(1)}, u32[]{:S(2)}) copy-start(f32[1,64,40]{2,1,0:T(8,128)S(1)} %get-tuple-element.71) | copy-start | bytes 30724
  117.3 5.4 %copy-start.26 = (f32[2560]{0:T(1024)}, f32[2560]{0:T(1024)S(1)}, u32[]{:S(2)}) copy-start(f32[2560]{0:T(1024)S(1)} %mul.457) | copy-start | bytes 30724
  122.8 6.5 %copy-start.15 = (f32[128,1792]{1,0:T(8,128)}, f32[128,1792]{1,0:T(8,128)S(1)}, u32[]{:S(2)}) copy-start(f32[128,1792]{1,0:T(8,128)S(1)} %fusion.66) | copy-start | bytes 2752516
  127.8 1.8 copy-start.34
  127.8 1.8 copy-start.36
  129.6 5.4 %copy-start.16 = (bf16[256,5,128]{2,0,1:T(8,128)(2,1)}, bf16[256,5,128]{2,0,1:T(8,128)(2,1)S(1)}, u32[]{:S(2)}) copy-start(bf16[256,5,128]{2,0,1:T(8,128)(2,1)S(1)} %convolution_convert_fusion.7) | copy-start | bytes 983044
  129.6 43.9 %copy-start.18 = (bf16[4,128,2560]{2,1,0:T(8,128)(2,1)S(1)}, bf16[4,128,2560]{2,1,0:T(8,128)(2,1)}, u32[]{:S(2)}) copy-start(bf16[4,128,2560]{2,1,0:T(8,128)(2,1)} %get-tuple-element.34) | copy-start | bytes 7864324
  169.7 2.3 copy-start.11
  172.0 1.5 copy-start.4
  172.0 69.2 %copy-start.1 = (f32[128,2560]{1,0:T(8,128)}, f32[128,2560]{1,0:T(8,128)S(1)}, u32[]{:S(2)}) copy-start(f32[128,2560]{1,0:T(8,128)S(1)} %get-tuple-element.40.mid_ref) | copy-start | bytes 3932164
  176.3 9.2 %copy-start.12 = (bf16[2560,1024]{1,0:T(8,128)(2,1)S(1)}, bf16[2560,1024]{1,0:T(8,128)(2,1)}, u32[]{:S(2)}) copy-start(bf16[2560,1024]{1,0:T(8,128)(2,1)} %copy-done.11) | copy-start | bytes 15728644
  176.3 9.2 %copy-start.19 = (bf16[4,128,2560]{2,1,0:T(8,128)(2,1)S(1)}, bf16[4,128,2560]{2,1,0:T(8,128)(2,1)}, u32[]{:S(2)}) copy-start(bf16[4,128,2560]{2,1,0:T(8,128)(2,1)} %get-tuple-element.34) | copy-start | bytes 7864324
  185.5 6.8 %copy-start.2 = (bf16[2,512,2560]{2,1,0:T(8,128)(2,1)S(1)}, bf16[2,512,2560]{2,1,0:T(8,128)(2,1)}, u32[]{:S(2)}) copy-start(bf16[2,512,2560]{2,1,0:T(8,128)(2,1)} %pad_maximum_fusion.l_ref) | copy-start | bytes 15728644
  190.8 1.0 copy-start.20
  190.8 1.3 copy-start.22
  201.5 0.8 copy-start.33
  201.5 0.8 copy-start.31
  240.7 1.1 copy-start.7
  242.2 1.1 copy-start.13
  247.3 1.6 copy-start.35
  247.3 1.6 copy-start.37
  247.3 1.6 copy-start.38
  257.7 7.9 %copy-start.14 = (f32[128,2560]{1,0:T(8,128)S(1)}, f32[128,2560]{1,0:T(8,128)}, u32[]{:S(2)}) copy-start(f32[128,2560]{1,0:T(8,128)} %copy-done.13) | copy-start | bytes 3932164
  257.7 7.9 %copy-start.17 = (bf16[256,5,128]{2,0,1:T(8,128)(2,1)S(1)}, bf16[256,5,128]{2,0,1:T(8,128)(2,1)}, u32[]{:S(2)}) copy-start(bf16[256,5,128]{2,0,1:T(8,128)(2,1)} %copy-done.16) | copy-start | bytes 983044
  265.6 4.7 %copy-start.27 = (f32[2560]{0:T(1024)S(1)}, f32[2560]{0:T(1024)}, u32[]{:S(2)}) copy-start(f32[2560]{0:T(1024)} %copy-done.26) | copy-start | bytes 30724
  270.3 6.3 %copy-start.5 = (bf16[4,128,2560]{2,1,0:T(8,128)(2,1)S(1)}, bf16[4,128,2560]{2,1,0:T(8,128)(2,1)}, u32[]{:S(2)}) copy-start(bf16[4,128,2560]{2,1,0:T(8,128)(2,1)} %copy-done.4) | copy-start | bytes 7864324
  270.3 6.3 %copy-start.41 = (bf16[16,1024]{1,0:T(8,128)(2,1)S(1)}, bf16[16,1024]{1,0:T(8,128)(2,1)}, u32[]{:S(2)}) copy-start(bf16[16,1024]{1,0:T(8,128)(2,1)} %constant.46.clone) | copy-start | bytes 98308
  270.3 6.3 %copy-start.42 = (bf16[512,1024]{1,0:T(8,128)(2,1)S(1)}, bf16[512,1024]{1,0:T(8,128)(2,1)}, u32[]{:S(2)}) copy-start(bf16[512,1024]{1,0:T(8,128)(2,1)} %get-tuple-element.53) | copy-start | bytes 3145732
  270.3 12.5 %slice-start = ((s8[5242880]{0:T(1024)(128)(4,1)}), s8[4194304]{0:T(1024)(128)(4,1)S(1)}, s32[]{:S(2)}) async-start(s8[5242880]{0:T(1024)(128)(4,1)} %bitcast.157), calls=%async_computation.3 | async-start | bytes 8388608
  276.6 6.2 %slice-start.1 = ((s8[5242880]{0:T(1024)(128)(4,1)}), s8[1048576]{0:T(1024)(128)(4,1)S(1)}, s32[]{:S(2)}) async-start(s8[5242880]{0:T(1024)(128)(4,1)} %bitcast.157), calls=%async_computation.4 | async-start | bytes 2097152
  276.6 6.2 %copy-start.21 = (bf16[512,1024]{1,0:T(8,128)(2,1)S(1)}, bf16[512,1024]{1,0:T(8,128)(2,1)}, u32[]{:S(2)}) copy-start(bf16[512,1024]{1,0:T(8,128)(2,1)} %copy-done.20) | copy-start | bytes 3145732
  409.7 6.0 %copy-start.25 = (bf16[4,80,1024]{2,1,0:T(8,128)(2,1)S(1)}, bf16[4,80,1024]{2,1,0:T(8,128)(2,1)}, u32[]{:S(2)}) copy-start(bf16[4,80,1024]{2,1,0:T(8,128)(2,1)} %get-tuple-element.45) | copy-start | bytes 1966084
  417.7 2.0 copy-start.24
  417.8 2.7 copy-start.23
Sparse Core Ops, SparseCore 0:
  32.1 105.6 all-gather.1
  201.7 87.8 reduce-scatter.1

commit v3 on v2

--- a/solution.py
+++ b/solution.py
@@ -175,10 +175,6 @@
 
 def ring_of(axis, at):
     return {axis: lax.rem(at + 3, 4)}, {axis: lax.rem(at + 1, 4)}
-
-
-def block_rows(row, column, start=0, size=160):
-    return pl.ds(pl.multiple_of((row * 4 + column) * 160 + start, 16), size)
 
 
 def send_blocks(ins, outs, here, send, recv):
@@ -558,86 +554,84 @@
     )(p, x, gain, down)
 
 
-SEGMENTS = ((0, 0, 256), (256, 256, 512), (WIDE, 768, 768))
+def finish_kernel(s_ref, down_ref, gate_ref, up_ref, landed, here, send, recv):
+    greet(group_peers())
+    send_blocks([s_ref], [landed], here, send, recv)()
+    for t in range(4):
+        v = landed[t].astype(jnp.float32)
+        for k, out in enumerate((down_ref, gate_ref, up_ref)):
+            for h in range(2):
+                width = min(FEED, 960 - h * FEED)
+                first = t * 960 + h * FEED
+                out[:, first : first + width] = v[(2 * k + h) * 40 : (2 * k + h + 1) * 40, :width]
+
+
+def finish(sent, cid):
+    dma = pltpu.SemaphoreType.DMA
+    vmem = pl.BlockSpec(memory_space=pltpu.VMEM)
+    return pl.pallas_call(
+        finish_kernel,
+        out_shape=[jax.ShapeDtypeStruct((40, 3840), jnp.float32)] * 3,
+        in_specs=[pl.BlockSpec(memory_space=pl.ANY)],
+        out_specs=[vmem] * 3,
+        scratch_shapes=[pltpu.VMEM(sent.shape, sent.dtype), dma((1,)), dma((3,)), dma((3,))],
+        compiler_params=pltpu.CompilerParams(
+            collective_id=cid, has_side_effects=True, vmem_limit_bytes=32 * 2**20
+        ),
+    )(sent)
+
+
+class SumPiece:
+    def __init__(self, h, sums, columns, via, main, sems, rows=160):
+        self.h, self.sums, self.columns, self.via, self.main, self.sems, self.rows = (
+            h, sums, columns, via, main, sems, rows,
+        )
+
+    def first(self, i1, i2, part=0):
+        row, column = (i2, i1) if self.h == 0 else (i1, i2)
+        return (row * 4 + column) * self.rows + part * (self.rows // 2)
+
+    def at(self, i1, i2, part=None):
+        size = self.rows if part is None else self.rows // 2
+        return self.sums.at[pl.ds(pl.multiple_of(self.first(i1, i2, part or 0), 16), size), self.columns]
 
 
 def plane_sum_kernel(
-    a_ref, o_ref, f_ref, s_ref, p_ref, t_ref, x_ref, mid_ref, dmid_ref, g_ref, order_ref,
-    attn_ref, feed_ref, so_ref, block_ref, grad_ref,
-    sums, from_core, via, main, from_chip, attn_low, feed_low, gains,
+    xn_ref, dq_ref, dl_ref, m_ref, gi_ref, p_ref, t_ref, x_ref, mid_ref, dmid_ref, g_ref, order_ref,
+    attn_ref, go_ref, block_ref, grad_ref,
+    left, right, left_o, right_o, sums, via, main, gsums, gvia, gmain, from_chip, attn_low, gfar, gsum, gall,
     t_core, t_other, t_chips, t_own, t_far, landed, block_low, grad_low,
     here, csend, crecv, send, recv, esend, erecv, tsend, trecv, shere, ssend, srecv,
 ):
     y, x, c, zl, zh = (lax.axis_index(k) for k in ("y", "x", "c", "zl", "zh"))
     core, chip, far_peer = {"c": 1 - c}, {"zl": 1 - zl}, {"zh": 1 - zh}
-    diagonal = {"zl": 1 - zl, "zh": 1 - zh}
     chips = [{"zl": 1 - zl, "zh": k} for k in range(2)]
     greet(
-        [
-            *ring_of("x", x), *ring_of("y", y), core, chip, far_peer, diagonal,
-            {"zl": 1 - zl, "c": 1 - c},
-        ]
+        [*ring_of("x", x), *ring_of("y", y), core, *chips, far_peer, {"zl": 1 - zl, "c": 1 - c}]
     )
     step = 16
     f32, low = jnp.float32, jnp.bfloat16
-
     order = (2, 1, 3, 0)
-
-    def chunk(q):
-        return pl.ds(pl.multiple_of(shift(y, order[q]) * 640, 640), 640)
-
-    def load(q, side, remote_side):
-        rows = chunk(q)
-        if side == 0:
-            parts = [a_ref.at[rows, pl.ds(0, 256)], a_ref.at[rows, pl.ds(256, 512)], a_ref.at[rows, pl.ds(768, 768)]]
-        else:
-            parts = [a_ref.at[rows, pl.ds(1536, 256)], o_ref.at[rows, pl.ds(0, 512)], o_ref.at[rows, pl.ds(512, 768)]]
-        out = []
-        for s, (at, landing, width) in enumerate(SEGMENTS):
-            k = q * 3 + s
-            if remote_side:
-                out.append(
-                    remote(parts[s], from_core.at[rows, pl.ds(landing, width)], csend.at[k], crecv.at[k], core)
-                )
-            else:
-                out.append(pltpu.make_async_copy(parts[s], sums.at[rows, pl.ds(at, width)], here.at[k]))
-        return out
-
-    def feed_load(q):
-        rows = chunk(q)
-        return [
-            pltpu.make_async_copy(
-                f_ref.at[rows, pl.ds(h * FEED, FEED)],
-                sums.at[rows, pl.ds(h * WIDE + ATTN, FEED)],
-                here.at[12 + q * 2 + h],
-            )
-            for h in range(2)
-        ]
-
-    for side in range(2):
-
-        @pl.when(c == side)
-        def _(side=side):
-            for q in range(4):
-                for copy in load(q, 1 - side, True):
-                    copy.start()
-                for copy in load(q, side, False):
-                    copy.start()
-
-    for q in range(4):
-        for copy in feed_load(q):
-            copy.start()
-    finish = send_blocks([s_ref], [so_ref], shere, ssend, srecv)
-    pair = remote(t_ref, landed, tsend.at[6], trecv.at[6], far_peer)
-    pair.start()
     tokens = p_ref.shape[1]
     half = tokens // 2
+
+    inputs = [(xn_ref, left), (dq_ref, right), (dl_ref, left_o), (m_ref, right_o)]
+    mine, theirs_at = pl.ds(0, tokens), pl.ds(tokens, tokens)
+    shared = [
+        remote(src, dst.at[theirs_at], csend.at[k], crecv.at[k], core) for k, (src, dst) in enumerate(inputs)
+    ]
+    kept = [pltpu.make_async_copy(src, dst.at[mine], here.at[k]) for k, (src, dst) in enumerate(inputs)]
+    kept.append(pltpu.make_async_copy(gi_ref, gsums, here.at[4]))
+    for copy in (*shared, *kept):
+        copy.start()
     t_cores = [
         remote(p_ref.at[z * 2 + 1 - c], t_core.at[i], tsend.at[i], trecv.at[i], core)
         for i, z in enumerate((1 - zl, zl))
     ]
     for copy in t_cores:
         copy.start()
+    pair = remote(t_ref, landed, tsend.at[6], trecv.at[6], far_peer)
+    pair.start()
     t_sent = []
 
     def tokens_to_chips():
@@ -705,208 +699,188 @@
 
         reorder(block_low, order_ref, block_ref, True)
 
-    def columns(h):
-        return pl.ds(h * WIDE, WIDE)
-
-    def rows_at(h, i1, i2, start=0, size=160):
-        row, column = (i2, i1) if h == 0 else (i1, i2)
-        return block_rows(row, column, start, size)
-
-    def add(h, first, size, terms):
+    def products(q):
+        top = shift(y, order[q]) * 640
+        for side in range(2):
+
+            @pl.when(c == side)
+            def _(side=side):
+                if side == 0:
+                    parts = [(left, right, 0, 0, 768), (left, right, 768, 768, 768)]
+                else:
+                    parts = [
+                        (left, right, 1536, 0, 256),
+                        (left_o, right_o, 0, 256, 512),
+                        (left_o, right_o, 512, 768, 768),
+                    ]
+
+                @pl.loop(0, 5)
+                def _(i):
+                    at = pl.ds(pl.multiple_of(top + i * 128, 128), 128)
+                    for lhs, rhs, source, target, width in parts:
+                        sums[at, pl.ds(target, width)] = lax.dot_general(
+                            lhs[:, at],
+                            rhs[:, pl.ds(source, width)],
+                            (((0,), (0,)), ((), ())),
+                            preferred_element_type=f32,
+                        ).astype(low)
+
+    pieces = [
+        SumPiece(h, sums, pl.ds(h * ATTN, ATTN), via.at[h], main.at[h], h * 20) for h in range(2)
+    ]
+    pieces.append(SumPiece(0, gsums, pl.ds(0, 128), gvia, gmain, 40, 64))
+
+    def add(p, first, size, terms):
         @pl.loop(0, size // step)
         def _(i):
             at = pl.ds(pl.multiple_of(first + i * step, step), step)
-            total = sums[at, columns(h)].astype(f32)
+            total = p.sums[at, p.columns].astype(f32)
             for ref, index, start in terms:
                 total += ref[(*index, pl.ds(pl.multiple_of(start + i * step, step), step))].astype(f32)
-            sums[at, columns(h)] = total.astype(low)
+            p.sums[at, p.columns] = total.astype(low)
 
     started = []
 
-    def go(h, ring, slot, src, dst, peer):
-        k = (h * 5 + ring) * 4 + slot
+    def go(p, ring, slot, src, dst, peer):
+        k = p.sems + ring * 4 + slot
         copy = remote(src, dst, send.at[k], recv.at[k], peer)
         copy.start()
         started.append(copy)
 
-    def arrived(h, ring, slot, dst):
-        k = (h * 5 + ring) * 4 + slot
+    def arrived(p, ring, slot, dst):
+        k = p.sems + ring * 4 + slot
         remote(dst, dst, send.at[k], recv.at[k], core).wait_recv()
 
-    def first_row(h, i1, i2):
-        row, column = (i2, i1) if h == 0 else (i1, i2)
-        return (row * 4 + column) * 160
-
-    def out_via(h, ring, place, at, ring_peers):
-        back, ahead = ring_peers
-        far = shift(at, 2)
-        go(h, ring, 0, sums.at[place(far, 0, 80), columns(h)], via.at[h, ring, 0], ahead)
-        go(h, ring, 1, sums.at[place(far, 80, 80), columns(h)], via.at[h, ring, 1], back)
-
-    def out_main(h, ring, place, first, at, ring_peers):
-        back, ahead = ring_peers
-        arrived(h, ring, 0, via.at[h, ring, 0])
-        add(h, first(shift(at, 1)), 80, [(via, (h, ring, 0), 0)])
-        go(h, ring, 2, sums.at[place(shift(at, 1), 0, 160), columns(h)], main.at[h, ring, 0], ahead)
-        arrived(h, ring, 1, via.at[h, ring, 1])
-        add(h, first(shift(at, 3)) + 80, 80, [(via, (h, ring, 1), 0)])
-        go(h, ring, 3, sums.at[place(shift(at, 3), 0, 160), columns(h)], main.at[h, ring, 1], back)
-
-    def take(h, ring, first, at):
-        arrived(h, ring, 2, main.at[h, ring, 0])
-        arrived(h, ring, 3, main.at[h, ring, 1])
-        add(h, first(at), 160, [(main, (h, ring, 0), 0), (main, (h, ring, 1), 0)])
-
-    def along_second(h, j):
-        i1, _, i2, peers = around(h, y, x)
+    def line(p, j):
+        i1, peers1, i2, peers2 = around(p.h, y, x)
+        if j == 4:
+            return lambda k: (k, i2), i1, peers1
         fixed = shift(i1, order[j])
-        return (
-            lambda k, start, size: rows_at(h, fixed, k, start, size),
-            lambda k: first_row(h, fixed, k),
-            i2,
-            peers,
-        )
-
-    def along_first(h):
-        i1, peers, i2, _ = around(h, y, x)
-        return (
-            lambda k, start, size: rows_at(h, k, i2, start, size),
-            lambda k: first_row(h, k, i2),
-            i1,
-            peers,
-        )
-
+        return lambda k: (fixed, k), i2, peers2
+
+    def out_via(p, ring):
+        place, at, (back, ahead) = line(p, ring)
+        far = place(shift(at, 2))
+        go(p, ring, 0, p.at(*far, 0), p.via.at[ring, 0], ahead)
+        go(p, ring, 1, p.at(*far, 1), p.via.at[ring, 1], back)
+
+    def out_main(p, ring):
+        place, at, (back, ahead) = line(p, ring)
+        small = p.rows // 2
+        arrived(p, ring, 0, p.via.at[ring, 0])
+        add(p, p.first(*place(shift(at, 1)), 0), small, [(p.via, (ring, 0), 0)])
+        go(p, ring, 2, p.at(*place(shift(at, 1))), p.main.at[ring, 0], ahead)
+        arrived(p, ring, 1, p.via.at[ring, 1])
+        add(p, p.first(*place(shift(at, 3)), 1), small, [(p.via, (ring, 1), 0)])
+        go(p, ring, 3, p.at(*place(shift(at, 3))), p.main.at[ring, 1], back)
+
+    def take(p, ring):
+        place, at, _ = line(p, ring)
+        arrived(p, ring, 2, p.main.at[ring, 0])
+        arrived(p, ring, 3, p.main.at[ring, 1])
+        add(p, p.first(*place(at)), p.rows, [(p.main, (ring, 0), 0), (p.main, (ring, 1), 0)])
+
+    y_first, x_first, gain = pieces
+    for copy in kept:
+        copy.wait()
+    for copy in shared:
+        copy.wait_recv()
     for q in range(4):
-        for copy in load(q, 0, False):
-            copy.wait()
-        for copy in feed_load(q):
-            copy.wait()
-        for copy in load(q, 0, True):
-            copy.wait_recv()
-        top = shift(y, order[q]) * 640
-
-        @pl.loop(0, 640 // step)
-        def _(i, top=top):
-            at = pl.ds(pl.multiple_of(top + i * step, step), step)
-            for place, landing, width in SEGMENTS:
-                total = sums[at, pl.ds(place, width)].astype(f32) + from_core[
-                    at, pl.ds(landing, width)
-                ].astype(f32)
-                sums[at, pl.ds(place, width)] = total.astype(low)
-
+        products(q)
         if q == 0:
             for j in range(4):
-                place, first, at, peers = along_second(0, j)
-                out_via(0, j, place, at, peers)
-        place, first, at, peers = along_second(1, q)
-        out_via(1, q, place, at, peers)
+                out_via(y_first, j)
+                out_via(gain, j)
+        out_via(x_first, q)
         if q > 0:
-            place, first, at, peers = along_second(1, q - 1)
-            out_main(1, q - 1, place, first, at, peers)
-        if q == 1:
-            tokens_to_chips()
-        if q == 2:
+            out_main(x_first, q - 1)
+    tokens_to_chips()
+    for j in range(4):
+        out_main(y_first, j)
+        out_main(gain, j)
+        if j == 0:
+            out_main(x_first, 3)
             tokens_to_far(0)
     for j in range(4):
-        place, first, at, peers = along_second(0, j)
-        out_main(0, j, place, first, at, peers)
+        for p in (x_first, y_first, gain):
+            take(p, j)
+            if j == 0:
+                out_via(p, 4)
         if j == 0:
-            place, first, at, peers = along_second(1, 3)
-            out_main(1, 3, place, first, at, peers)
-        if j == 1:
             tokens_to_far(1)
-        if j == 3:
-            tokens_gradient()
-    for j in range(4):
-        for h in (1, 0):
-            place, first, at, peers = along_second(h, j)
-            take(h, j, first, at)
-            if j == 0:
-                place, first, at, peers = along_first(h)
-                out_via(h, 4, place, at, peers)
-    for h in (1, 0):
-        place, first, at, peers = along_first(h)
-        out_main(h, 4, place, first, at, peers)
+    tokens_gradient()
+    for p in (x_first, y_first, gain):
+        out_main(p, 4)
     tokens_output()
-    for h in (1, 0):
-        place, first, at, peers = along_first(h)
-        take(h, 4, first, at)
+    for p in (gain, x_first, y_first):
+        take(p, 4)
     home = (y * 4 + x) * 160
+    ghome = pl.ds(pl.multiple_of((y * 4 + x) * 64, 16), 64)
     theirs = pl.ds(pl.multiple_of(home + (1 - zl) * 80, 16), 80)
-    yours = pl.ds(pl.multiple_of(home + zl * 80, 16), 80)
-    tile = pl.ds(2 * WIDE - 128, 128)
-    away = [
-        remote(sums.at[theirs], from_chip, esend.at[0], erecv.at[0], chip),
-        remote(sums.at[yours, tile], gains.at[0], esend.at[4], erecv.at[4], far_peer),
-        remote(sums.at[theirs, tile], gains.at[1], esend.at[5], erecv.at[5], diagonal),
-    ]
-    for copy in away:
-        copy.start()
-    finish()
-    for copy in away:
-        copy.wait()
-    is_gain = lax.broadcasted_iota(jnp.int32, (step, 128), 1) >= 64
+    across = remote(gsums.at[ghome], gfar, esend.at[0], erecv.at[0], far_peer)
+    across.start()
+    away = remote(sums.at[theirs], from_chip, esend.at[1], erecv.at[1], chip)
+    away.start()
+    across.wait()
+    both = gsums[ghome].astype(f32) + gfar[...].astype(f32)
+    for t in range(4):
+        gsum[t] = both[t * 16 : (t + 1) * 16].astype(low)
+    finish_gains = send_blocks([gsum], [gall], shere, ssend, srecv)
+    away.wait()
 
     @pl.loop(0, 80 // step)
     def _(i):
         here_at = pl.ds(pl.multiple_of(home + zl * 80 + i * step, step), step)
         at = pl.ds(pl.multiple_of(i * step, step), step)
-        for h in range(2):
-            a = pl.ds(h * WIDE, ATTN)
-            attn_low[at, pl.ds(h * ATTN, ATTN)] = sums[here_at, a].astype(f32) + from_chip[at, a].astype(f32)
-            f = pl.ds(h * WIDE + ATTN, FEED)
-            feed_low[0, at, pl.ds(h * FEED, FEED)] = sums[here_at, f].astype(f32)
-            feed_low[1, at, pl.ds(h * FEED, FEED)] = from_chip[at, f].astype(f32)
-        end = pl.ds(2 * FEED - 128, 128)
-        for k in range(2):
-            v = feed_low[k, at, end]
-            feed_low[k, at, end] = jnp.where(is_gain, v + gains[k, at].astype(f32), v)
+        attn_low[at] = sums[here_at].astype(f32) + from_chip[at].astype(f32)
 
     ours = pl.ds(pl.multiple_of(c * 40, 8), 40)
     for_core = pl.ds(pl.multiple_of((1 - c) * 40, 8), 40)
-    half = pl.ds(pl.multiple_of(c * 2 * ATTN, 128), 2 * ATTN)
-    last = [remote(attn_low.at[for_core], attn_ref.at[:, half], esend.at[1], erecv.at[1], core)]
-    keep = [pltpu.make_async_copy(attn_low.at[ours], attn_ref.at[:, half], here.at[0])]
-    for k, source in enumerate((zl * 2 + c, (1 - zl) * 2 + c)):
-        last.append(
-            remote(feed_low.at[k, for_core], feed_ref.at[source], esend.at[2 + k], erecv.at[2 + k], core)
-        )
-        keep.append(pltpu.make_async_copy(feed_low.at[k, ours], feed_ref.at[source], here.at[1 + k]))
-    for copy in (*last, *keep):
-        copy.start()
-    for copy in (*last, *keep):
-        copy.wait()
-    for copy in (*started, pair, *t_cores, *t_sent):
+    columns = pl.ds(pl.multiple_of(c * 2 * ATTN, 128), 2 * ATTN)
+    last = remote(attn_low.at[for_core], attn_ref.at[:, columns], esend.at[2], erecv.at[2], core)
+    keep = pltpu.make_async_copy(attn_low.at[ours], attn_ref.at[:, columns], here.at[0])
+    last.start()
+    keep.start()
+    finish_gains()
+    go_ref[...] = (
+        gall[0].astype(f32) + gall[1].astype(f32) + gall[2].astype(f32) + gall[3].astype(f32)
+    )
+    last.wait()
+    keep.wait()
+    for copy in (*started, *shared, pair, *t_cores, *t_sent):
         copy.wait_send()
-    for q in range(4):
-        for copy in load(q, 0, True):
-            copy.wait_send()
-
-
-def plane_sum(a, o, f, sent, down, d_xn, x, mid, d_mid, gain, order, cid):
+
+
+def plane_sum(xn, d_q_kv, d_low, mixed, gains, down, d_xn, x, mid, d_mid, gain, order, cid):
     low, dma, f32 = jnp.bfloat16, pltpu.SemaphoreType.DMA, jnp.float32
     rows, width = x.shape
-    anywhere, vmem = pl.BlockSpec(memory_space=pl.ANY), pl.BlockSpec(memory_space=pltpu.VMEM)
+    vmem = pl.BlockSpec(memory_space=pltpu.VMEM)
     return pl.pallas_call(
         plane_sum_kernel,
         out_shape=[
             jax.ShapeDtypeStruct((40, 4 * ATTN), f32),
-            jax.ShapeDtypeStruct((4, 40, 2 * FEED), f32),
-            jax.ShapeDtypeStruct(sent.shape, low),
+            jax.ShapeDtypeStruct((16, 128), f32),
             jax.ShapeDtypeStruct(x.shape, low),
             jax.ShapeDtypeStruct(x.shape, low),
         ],
-        in_specs=[anywhere] * 4 + [vmem] * 7,
-        out_specs=[vmem, vmem, anywhere, vmem, vmem],
+        in_specs=[vmem] * 12,
+        out_specs=[vmem] * 4,
         scratch_shapes=[
-            pltpu.VMEM((2560, 2 * WIDE), low),
+            pltpu.VMEM((2 * rows, width), low),
+            pltpu.VMEM((2 * rows, d_q_kv.shape[1]), low),
+            pltpu.VMEM((2 * rows, width), low),
+            pltpu.VMEM((2 * rows, mixed.shape[1]), low),
             pltpu.VMEM((2560, 2 * ATTN), low),
-            pltpu.VMEM((2, 5, 2, 80, WIDE), low),
-            pltpu.VMEM((2, 5, 2, 160, WIDE), low),
-            pltpu.VMEM((80, 2 * WIDE), low),
+            pltpu.VMEM((2, 5, 2, 80, ATTN), low),
+            pltpu.VMEM((2, 5, 2, 160, ATTN), low),
+            pltpu.VMEM((1024, 128), low),
+            pltpu.VMEM((5, 2, 32, 128), low),
+            pltpu.VMEM((5, 2, 64, 128), low),
+            pltpu.VMEM((80, 2 * ATTN), low),
             pltpu.VMEM((80, 2 * ATTN), f32),
-            pltpu.VMEM((2, 80, 2 * FEED), f32),
-            pltpu.VMEM((2, 80, 128), low),
+            pltpu.VMEM((64, 128), low),
+            pltpu.VMEM((4, 16, 128), low),
+            pltpu.VMEM((4, 16, 128), low),
             pltpu.VMEM((2, rows, width), low),
             pltpu.VMEM((rows, width), low),
             pltpu.VMEM((2, rows // 2, width), low),
@@ -915,13 +889,13 @@
             pltpu.VMEM((rows, width), low),
             pltpu.VMEM((rows, width), low),
             pltpu.VMEM((rows, width), low),
-            dma((20,)),
-            dma((12,)),
-            dma((12,)),
-            dma((40,)),
-            dma((40,)),
-            dma((6,)),
-            dma((6,)),
+            dma((5,)),
+            dma((4,)),
+            dma((4,)),
+            dma((60,)),
+            dma((60,)),
+            dma((3,)),
+            dma((3,)),
             dma((7,)),
             dma((7,)),
             dma((1,)),
@@ -929,37 +903,42 @@
             dma((3,)),
         ],
         compiler_params=pltpu.CompilerParams(
-            collective_id=cid, has_side_effects=True, vmem_limit_bytes=56 * 2**20
+            collective_id=cid, has_side_effects=True, vmem_limit_bytes=52 * 2**20
         ),
-    )(a, o, f, sent, down, d_xn, x, mid, d_mid, gain, order)
-
-
-def grads_kernel(l_ref, r_ref, o_ref):
-    o_ref[...] = lax.dot_general(
-        l_ref[0], r_ref[0], (((0,), (0,)), ((), ())), preferred_element_type=jnp.float32
-    ).astype(o_ref.dtype)
-
-
-def pair_of_grads(left, right):
-    n, depth, rows = left.shape
-    columns, tile = right.shape[2], 256
-    per = columns // tile
+    )(xn, d_q_kv, d_low, mixed, gains, down, d_xn, x, mid, d_mid, gain, order)
+
+
+def grads_kernel(dy_ref, xn_ref, h_ref, d_ref, o_ref):
+    def product(left, right):
+        o_ref[...] = lax.dot_general(
+            left[...], right[...], (((0,), (0,)), ((), ())), preferred_element_type=jnp.float32
+        ).astype(o_ref.dtype)
+
+    pl.when(pl.program_id(0) < 4)(lambda: product(dy_ref, h_ref))
+    pl.when(pl.program_id(0) >= 4)(lambda: product(xn_ref, d_ref))
+
+
+def feed_grads(dy, xn, hidden, d_gate_up):
+    depth, rows = dy.shape
+    tile = 256
     return pl.pallas_call(
         grads_kernel,
-        grid=(n, per),
-        out_shape=jax.ShapeDtypeStruct((rows, n * columns), jnp.bfloat16),
+        grid=(12,),
+        out_shape=jax.ShapeDtypeStruct((rows, 12 * tile), jnp.bfloat16),
         in_specs=[
-            pl.BlockSpec((1, depth, rows), lambda b, j: (b, 0, 0)),
-            pl.BlockSpec((1, depth, tile), lambda b, j: (b, 0, j)),
+            pl.BlockSpec((depth, rows), lambda j: (0, 0)),
+            pl.BlockSpec((depth, rows), lambda j: (0, 0)),
+            pl.BlockSpec((depth, tile), lambda j: (0, jnp.minimum(j, 3))),
+            pl.BlockSpec((depth, tile), lambda j: (0, jnp.maximum(j - 4, 0))),
         ],
-        out_specs=pl.BlockSpec((rows, tile), lambda b, j: (0, b * per + j)),
+        out_specs=pl.BlockSpec((rows, tile), lambda j: (0, j)),
         compiler_params=pltpu.CompilerParams(vmem_limit_bytes=40 * 2**20),
         cost_estimate=pl.CostEstimate(
-            flops=2 * n * depth * rows * columns,
-            bytes_accessed=2 * n * (depth * rows + depth * columns + rows * columns),
+            flops=2 * depth * rows * 12 * tile,
+            bytes_accessed=4 * depth * rows + 2 * rows * 12 * tile,
             transcendentals=0,
         ),
-    )(left, right)
+    )(dy, xn, hidden, d_gate_up)
 
 
 def rms_norm(values, gain_row):
@@ -996,10 +975,6 @@
 
 def padded(weight):
     return jnp.pad(weight.reshape(40, 4, 960), ((0, 0), (0, 0), (0, 64)))
-
-
-def joined(slices):
-    return slices[:, :, :960].transpose(1, 0, 2).reshape(40, 3840).astype(jnp.float32)
 
 
 def local(
@@ -1083,17 +1058,17 @@
     d_gate_pre, d_up_pre = geglu_pull(d_hidden)
     d_gate_low = d_gate_pre.astype(low)
     d_up_low = d_up_pre.astype(low)
-    d_xn_two_part = contract(jnp.concatenate([d_gate_low, d_up_low], axis=1), w_gate_up, 1, 1)
+    d_gate_up = jnp.concatenate([d_gate_low, d_up_low], axis=1)
+    sent = feed_grads(dy, xn_all, hidden, d_gate_up)
+    sent = lax.psum_scatter(sent, PLANE, scatter_dimension=0, tiled=True)
+    sent = sent.reshape(4, 40, 3, 2, FEED).transpose(0, 2, 3, 1, 4).reshape(4, 240, FEED)
+    d_xn_two_part = contract(d_gate_up, w_gate_up, 1, 1)
     d_xn_two = token_sum(d_xn_two_part.astype(low).reshape(4, rows, -1), 3)
-    sent = pair_of_grads(jnp.stack([dy, xn_all]), jnp.stack([hidden, d_gate_low]))
-    sent = lax.psum_scatter(sent, PLANE, scatter_dimension=0, tiled=True)
-    sent = sent.reshape(4, 40, 2, 2 * FEED).transpose(0, 2, 1, 3).reshape(4, 80, 2 * FEED)
 
     norm_two_pull = jax.vjp(rms_norm, x_mid, gain_two)[1]
     d_mid_norm, d_gain_two = norm_two_pull(d_xn_two)
     d_mid = dy_here.astype(jnp.float32) + d_mid_norm
     d_mid_low = d_mid.astype(low)
-    d_out_t = contract(d_mid_low, mixed_heads, 0, 0)
     d_mixed = (
         jnp.dot(d_mid_low, w_out_t, preferred_element_type=jnp.float32)
         .astype(low)
@@ -1117,23 +1092,18 @@
     d_k_pre = rotate(d_keys, cosine, -sine).reshape(rows, HEAD_DIM)
     d_kv_part = jnp.concatenate([d_k_pre, d_values.reshape(rows, HEAD_DIM)], axis=-1)
     d_kv_low = pair_sum(d_kv_part.astype(low), 4).astype(low)
-    d_q_kv_w = contract(xn_one, jnp.concatenate([d_q_pre, d_kv_low], axis=1), 0, 0).astype(low)
     d_xn_one = contract(jnp.concatenate([d_q_pre, d_kv_low * 0.5], axis=1), w_q_kv, 1, 1)
     norm_one_pull = jax.vjp(lambda g: rms_norm(x_in, g), gain_one)[1]
     d_gain_one = norm_one_pull(d_xn_one)[0]
-    d_gains = jnp.pad(jnp.stack([d_gain_one, 0.5 * d_gain_two], axis=0).astype(low), ((0, 14), (0, 0)))
-    chosen = jnp.asarray(np.eye(16, 2 * FEED, 960) * (np.arange(16) < 2)[:, None], low)
-    d_up_w = contract(
-        jnp.concatenate([xn_all, d_gains], axis=0),
-        jnp.concatenate([d_up_low, chosen], axis=0),
-        0,
-        0,
-    ).astype(low)
-    attn_out, up_out, sent, block_out, tokens_grad = plane_sum(
-        d_q_kv_w,
-        d_out_t.astype(low),
-        d_up_w,
-        sent,
+    d_gains = jnp.stack([d_gain_one, 0.5 * d_gain_two], axis=0).astype(low)
+    d_gains = d_gains.reshape(2, 64, 40).transpose(1, 0, 2)
+    d_gains = jnp.pad(d_gains, ((0, 0), (0, 14), (0, 88))).reshape(1024, 128)
+    attn_out, gain_out, block_out, tokens_grad = plane_sum(
+        xn_one,
+        jnp.concatenate([d_q_pre, d_kv_low], axis=1),
+        d_mid_low,
+        mixed_heads,
+        d_gains,
         down_part.reshape(4, rows, -1),
         d_xn_one.astype(low),
         x_in,
@@ -1143,19 +1113,18 @@
         order,
         7,
     )
-    sent = sent.reshape(4, 2, 40, 2 * FEED)
-    gain_out = up_out[:, :, 960:962].sum(axis=0)
+    down_out, gate_out, up_out = finish(sent, 8)
     return (
         block_out,
         tokens_grad,
-        gain_out[:, 0],
+        gain_out[0, :40],
         attn_out[:, :wide],
         attn_out[:, wide : wide + 2 * HEAD_DIM],
         attn_out[:, wide + 2 * HEAD_DIM :].T,
-        gain_out[:, 1],
-        joined(sent[:, 1]),
-        joined(up_out),
-        joined(sent[:, 0]).T,
+        gain_out[1, :40],
+        gate_out,
+        up_out,
+        down_out.T,
     )
 
 

time: 436 us -> 409 us (0.938)
  matrix products: 71 us -> 56.6 us
  local copies, waits for them, and re-layouts: 40.5 us -> 35.5 us
    pallas_call x1, Pallas kernels: 115 us -> 92.7 us  [plane_sum(): pl.pallas_call(plane_sum_kernel, out_shape=[jax.ShapeDtypeStruct((40, 4 *...]
    pallas_call x1 -> x2, Pallas kernels: 9.21 us -> 27.3 us  [the longest x1 13.9 us: feed_grads(): pl.pallas_call(grads_kernel, grid=(12,), out_shape=jax.ShapeDtypeStruct((...]
    dot_general x7 -> x4, matrix products: 43.5 us -> 29.3 us  [contract(): lax.dot_general(left, right, (((left_dim,), (right_dim,)), ((), ())), pre...]
    unnamed x96 -> x94, local copies, waits for them, and re-layouts: 14.1 us -> 16.8 us
  transfers between devices with their start and end apart: 2 -> 2, of which waited for: 1 -> 0; matrix products, arithmetic and copies ran while one was open for 17% -> 16% of each run, Pallas kernels for 35% -> 60%
where the time goes in v3:
time: 409 us; the launch traced here: 402 us
  Pallas kernels  287 us (70%)
  matrix products  56.6 us (14%)
  local copies, waits for them, and re-layouts  35.5 us (9%)
  between operations  15.3 us (4%)
  other arithmetic  7.78 us (2%)
    pallas_call x1, Pallas kernels, plane_sum(): pl.pallas_call(plane_sum_kernel, out_shape=[jax.ShapeDtypeStruct((40, 4 *...  92.7 us
    pallas_call x1, Pallas kernels, attention_gather(): pl.pallas_call(attention_gather_kernel, out_shape=[jax.ShapeDtypeStruct((...  81 us
    pallas_call x1, Pallas kernels, middle(): pl.pallas_call(middle_kernel, out_shape=[jax.ShapeDtypeStruct(x.shape, jn...  34.5 us
    dot_general x4, matrix products, contract(): lax.dot_general(left, right, (((left_dim,), (right_dim,)), ((), ())), pre...  29.3 us
    pallas_call x1, Pallas kernels, token_sum(): pl.pallas_call(sum_kernel, out_shape=jax.ShapeDtypeStruct((rows, width),...  28.1 us
    unnamed x94, local copies, waits for them, and re-layouts  16.8 us
    pallas_call x1, Pallas kernels, group_exchange(): pl.pallas_call(exchange_kernel, out_shape=[*(like(a, a.dtype) for a in ar...  16.8 us
    pallas_call x1, Pallas kernels, feed_grads(): pl.pallas_call(grads_kernel, grid=(12,), out_shape=jax.ShapeDtypeStruct((...  13.9 us
  transfers between devices with their start and end apart: 2, of which 0 were waited for; matrix products, arithmetic and copies ran while one was open for 16% of the time, Pallas kernels for 60%

profile of v3, /device:TPU:1, one launch (start us, length us, event | category | flops | bytes accessed | tf_op | source)
XLA Modules:
  0.0 402.4 jit_solution(1375009713497204673)
XLA Ops:
  7.3 1.0 pad_maximum_fusion.5
  8.5 1.4 reshape.420
  10.0 0.5 reshape.421
  10.9 0.8 copy-done.2
  12.0 16.8 %shard_map.186 = (bf16[4,80,768]{2,1,0:T(8,128)(2,1)S(1)}, bf16[4,16,128]{2,1,0:T(8,128)(2,1)S(1)}, bf16[4,80,1024]{2,1,0:T(8,128)(2,1)S(1)}, f32[128,2560]{1,0:T(8,128)S(1)}, bf16[128,2560]{1,0:T(8,128)(2,1)S(1)}) custom-call(bf16[4,80,768]{2,1,0:T(8,128)(2,1)S(1)} %bitcast.143, bf16[4,16,128]{2,1,0:T(8,128)(2,1)S(1)} %broadcast_in_dim.17.g_ref, ...), custom_call_target="tpu_custom_call" | custom-call | tf_op jit(solution)/shard_map/pallas_call | solution.py:231
  28.8 0.8 copy-done.3
  29.7 0.7 copy.54
  30.3 1.0 copy.81
  31.4 0.5 reshape.426
  32.3 0.8 copy.45
  33.0 0.8 copy.43
  33.8 81.0 %shard_map.187 = (bf16[2560,1792]{1,0:T(8,128)(2,1)}, bf16[2560,1280]{1,0:T(8,128)(2,1)}, bf16[1024,128]{1,0:T(8,128)(2,1)}, bf16[4,128,2560]{2,1,0:T(8,128)(2,1)}, bf16[4,80,512]{2,1,0:T(8,128)(2,1)}) custom-call(bf16[2,160,768]{2,1,0:T(8,128)(2,1)} %bitcast.165, bf16[64,128]{1,0:T(8,128)(2,1)} %bitcast.149, bf16[128,2560]{1,0:T(8,128)(2,1)} %copy-done.3, ...), custom_call_target="tpu_custom_call" | custom-call | tf_op jit(solution)/shard_map/pallas_call | solution.py:433
  114.9 0.9 slice.116
  116.0 1.0 copy.53
  117.4 0.3 copy-done.38
  117.7 5.4 %fusion.56 = f32[128,1792]{1,0:T(8,128)S(1)} fusion(bf16[128,2560]{1,0:T(8,128)(2,1)S(1)} %multiply_convert_fusion.2.xn_ref, bf16[2560,1792]{1,0:T(8,128)(2,1)} %get-tuple-element.35), kind=kOutput, calls=%fused_computation.120 | convolution fusion | flops 1174405120 | bytes 10747904 | tf_op jit(solution)/shard_map/dot_general | solution.py:1026
  123.2 1.1 copy.47
  124.2 1.0 slice.125
  125.3 0.8 copy.80
  126.1 1.0 fusion.53
  127.5 0.3 fusion.34
  127.8 0.3 fusion.36
  128.2 1.4 fusion.55
  129.7 0.3 convolution_convert_fusion.4
  130.0 5.3 %convolution_convert_fusion.2.p_ref = bf16[128,2560]{1,0:T(8,128)(2,1)S(1)} fusion(bf16[128,1280]{0,1:T(8,128)(2,1)S(1)} %bitcast.154, bf16[2560,1280]{1,0:T(8,128)(2,1)} %get-tuple-element.37), kind=kOutput, calls=%fused_computation.2 | convolution fusion | flops 839188480 | bytes 7536640 | tf_op jit(solution)/shard_map/dot_general | solution.py:971
  135.3 34.5 %shard_map.188 = (f32[128,2560]{1,0:T(8,128)S(1)}, bf16[4,128,2560]{2,1,0:T(8,128)(2,1)S(1)}, bf16[2560,1024]{1,0:T(8,128)(2,1)S(1)}) custom-call(bf16[128,2560]{1,0:T(8,128)(2,1)S(1)} %convolution_convert_fusion.2.p_ref, f32[128,2560]{1,0:T(8,128)S(1)} %get-tuple-element.30.x_ref, f32[1,2560]{1,0:T(1,128)S(1)} %slice.101.g_ref, ...), custom_call_target="tpu_custom_call" | custom-call | tf_op jit(solution)/shard_map/pallas_call | solution.py:532
  169.8 2.4 copy-done.8
  172.2 1.5 copy-done.11
  173.7 9.6 %fusion.57 = f32[512,2048]{1,0:T(8,128)S(1)} fusion(bf16[512,2560]{1,0:T(8,128)(2,1)} %bitcast.152, bf16[2560,2048]{1,0:T(8,128)(2,1)} %all-gather.2.cloned.1.call-done), kind=kOutput, calls=%fused_computation.121 | convolution fusion | flops 5368709120 | bytes 17301504 | tf_op jit(solution)/shard_map/dot_general | solution.py:1052
  183.3 4.4 %fusion.6 = (bf16[512,1024]{1,0:T(8,128)(2,1)S(1)}, bf16[512,1024]{1,0:T(8,128)(2,1)S(1)}, bf16[512,1024]{1,0:T(8,128)(2,1)S(1)}) fusion(f32[512,2048]{1,0:T(8,128)S(1)} %fusion.57, bf16[512,2560]{1,0:T(8,128)(2,1)S(1)} %bitcast.150, bf16[2560,1024]{1,0:T(8,128)(2,1)S(1)} %copy-done.9), kind=kOutput, calls=%fused_computation.12 | convolution fusion | flops 2697986048 | bytes 15204352 | tf_op jit(solution)/shard_map/dot_general | solution.py:1056
  188.0 0.8 copy-done.19
  188.7 0.4 copy-done.20
  189.1 0.3 copy-done.13
  189.4 1.3 copy-done.12
  190.7 13.9 %shard_map.192 = bf16[2560,3072]{1,0:T(8,128)(2,1)} custom-call(bf16[512,2560]{1,0:T(8,128)(2,1)S(1)} %bitcast.151, bf16[512,2560]{1,0:T(8,128)(2,1)S(1)} %bitcast.153, bf16[512,1024]{1,0:T(8,128)(2,1)S(1)} %get-tuple-element.58.h_ref, bf16[512,2048]{1,0:T(8,128)(2,1)S(1)} %pad_maximum_fusion.d_ref), custom_call_target="tpu_custom_call" | custom-call | flops 8053063680 | bytes 20971520 | tf_op jit(solution)/shard_map/pallas_call | solution.py:924
  204.8 1.1 copy.65.m_ref
  206.1 9.0 %convolution_convert_fusion.1 = bf16[512,2560]{1,0:T(8,128)(2,1)S(1)} fusion(bf16[2560,2048]{1,0:T(8,128)(2,1)} %all-gather.2.cloned.1.call-done, bf16[512,1024]{1,0:T(8,128)(2,1)} %copy-done.20, bf16[512,1024]{1,0:T(8,128)(2,1)} %copy-done.19), kind=kOutput, calls=%fused_computation.1 | convolution fusion | flops 5374214144 | bytes 15204352 | tf_op jit(solution)/shard_map/dot_general | solution.py:971
  215.1 28.1 %shard_map.189 = f32[128,2560]{1,0:T(8,128)S(1)} custom-call(bf16[4,128,2560]{2,1,0:T(8,128)(2,1)S(1)} %bitcast.141), custom_call_target="tpu_custom_call" | custom-call | tf_op jit(solution)/shard_map/pallas_call | solution.py:123
  243.3 0.5 multiply_reduce_fusion
  243.8 0.6 copy-done.4
  244.4 1.6 fusion.50
  246.0 0.8 copy-done.16
  246.8 4.3 %convolution_convert_fusion.3 = bf16[128,1280]{1,0:T(8,128)(2,1)S(1)} fusion(bf16[128,2560]{1,0:T(8,128)(2,1)S(1)} %get-tuple-element.54.dl_ref, bf16[2560,1280]{1,0:T(8,128)(2,1)} %get-tuple-element.37), kind=kOutput, calls=%fused_computation.5 | convolution fusion | flops 839024640 | bytes 7536640 | tf_op jit(solution)/shard_map/dot_general | solution.py:1073
  251.3 0.7 mul.535
  252.1 1.1 multiply_reduce_fusion.5
  253.3 0.3 fusion.12
  253.7 0.9 subtract_convert_fusion.2
  255.0 6.6 %shard_map.190 = f32[128,512]{1,0:T(8,128)S(1)} custom-call(bf16[128,512]{1,0:T(8,128)(2,1)S(1)} %pad_maximum_fusion.6.p_ref), custom_call_target="tpu_custom_call" | custom-call | tf_op jit(solution)/shard_map/pallas_call | solution.py:160
  261.6 0.7 broadcast_multiply_fusion
  262.4 0.3 fusion.8
  263.6 8.2 %fusion.52 = (bf16[128,2560]{1,0:T(8,128)(2,1)}, bf16[2560]{0:T(1024)(128)(2,1)S(1)}) fusion(f32[128,2560]{1,0:T(8,128)S(1)} %get-tuple-element.30.x_ref, f32[128]{0:T(128)S(1)} %copy-done.39, bf16[2560,1792]{1,0:T(8,128)(2,1)} %get-tuple-element.35, bf16[128,512]{0,1:T(8,128)(2,1)S(1)} %copy.63, bf16[128,1280]{0,1:T(8,128)(2,1)S(1)} %bitcast.157), kind=kOutput, calls=%fused_computation.116 | convolution fusion | flops 1176630784 | bytes 11605504 | tf_op jit(solution)/shard_map/dot_general | solution.py:971
  272.1 0.9 pad_maximum_fusion.2.dq_ref
  273.0 6.8 %convolution_convert_fusion = bf16[512,2560]{1,0:T(8,128)(2,1)} fusion(bf16[512,1024]{1,0:T(8,128)(2,1)S(1)} %copy-done.14, bf16[2560,1024]{1,0:T(8,128)(2,1)} %copy-done.8), kind=kOutput, calls=%fused_computation | convolution fusion | flops 2685665280 | bytes 8912896 | tf_op jit(solution)/shard_map/dot_general | solution.py:971
  279.9 92.7 %shard_map.191 = (f32[40,3072]{1,0:T(8,128)S(1)}, f32[16,128]{1,0:T(8,128)S(1)}, bf16[128,2560]{1,0:T(8,128)(2,1)}, bf16[128,2560]{1,0:T(8,128)(2,1)}) custom-call(bf16[128,2560]{1,0:T(8,128)(2,1)} %copy-done.15, bf16[128,1792]{1,0:T(8,128)(2,1)S(1)} %pad_maximum_fusion.2.dq_ref, bf16[128,2560]{1,0:T(8,128)(2,1)} %copy-done.16, ...), custom_call_target="tpu_custom_call" | custom-call | tf_op jit(solution)/shard_map/pallas_call | solution.py:858
  372.6 0.6 slice.113
  373.2 0.5 slice_bitcast_fusion.2
  373.7 0.8 slice_bitcast_fusion
  374.5 3.0 reshape.445
  377.7 13.4 %shard_map.193 = (f32[40,3840]{1,0:T(8,128)S(1)}, f32[40,3840]{1,0:T(8,128)S(1)}, f32[40,3840]{1,0:T(8,128)S(1)}) custom-call(bf16[4,240,512]{2,1,0:T(8,128)(2,1)S(1)} %bitcast.140), custom_call_target="tpu_custom_call" | custom-call | tf_op jit(solution)/shard_map/pallas_call | solution.py:572
  391.2 0.8 copy.88
  392.0 0.8 copy.89
  392.9 0.8 copy.90
  393.7 0.8 copy.91
  394.5 0.8 copy.92
  (132 shorter events, 5.2 us)
Async XLA Ops:
  7.2 2.9 copy-start.23
  7.2 3.5 copy-start.40
  7.2 3.5 copy-start.41
  7.2 166.5 %all-gather.2.cloned.1.call-start = ((), (), s32[]{:S(2)}) async-start(), calls=%async_computation.1 | async-start | bytes 11141120 | tf_op jit(solution)/shard_map/all_gather | solution.py:1017
  10.5 1.1 copy-start.2
  10.5 1.3 copy-start.5
  10.5 1.5 copy-start.6
  28.8 0.8 copy-start.3
  29.6 2.3 copy-start.7
  29.7 233.9 %copy-start = (f32[128,2560]{1,0:T(8,128)}, f32[128,2560]{1,0:T(8,128)S(1)}, u32[]{:S(2)}) copy-start(f32[128,2560]{1,0:T(8,128)S(1)} %get-tuple-element.30.x_ref) | copy-start | bytes 3932164
  29.7 1.8 copy-start.24
  31.4 343.2 %reduce-scatter.2.cloned.1.call-start = ((), (), s32[]{:S(2)}) async-start(), calls=%async_computation.2 | async-start | bytes 16711680 | tf_op jit(solution)/shard_map/reduce_scatter | solution.py:1063
  117.2 0.5 copy-start.38
  117.7 5.4 %copy-start.15 = (bf16[128,2560]{1,0:T(8,128)(2,1)}, bf16[128,2560]{1,0:T(8,128)(2,1)S(1)}, u32[]{:S(2)}) copy-start(bf16[128,2560]{1,0:T(8,128)(2,1)S(1)} %multiply_convert_fusion.2.xn_ref) | copy-start | bytes 1966084
  123.1 6.6 %copy-start.17 = (f32[128,1792]{1,0:T(8,128)}, f32[128,1792]{1,0:T(8,128)S(1)}, u32[]{:S(2)}) copy-start(f32[128,1792]{1,0:T(8,128)S(1)} %fusion.56) | copy-start | bytes 2752516
  127.4 0.7 copy-start.37
  127.5 7.8 %copy-start.30 = (bf16[128,128]{1,0:T(8,128)(2,1)}, bf16[128,128]{1,0:T(8,128)(2,1)S(1)}, u32[]{:S(2)}) copy-start(bf16[128,128]{1,0:T(8,128)(2,1)S(1)} %fusion.33) | copy-start | bytes 98308
  127.8 2.2 copy-start.34
  127.8 7.5 %copy-start.32 = (bf16[128,64]{1,0:T(8,128)(2,1)}, bf16[128,64]{1,0:T(8,128)(2,1)S(1)}, u32[]{:S(2)}) copy-start(bf16[128,64]{1,0:T(8,128)(2,1)S(1)} %get-tuple-element.71) | copy-start | bytes 49156
  128.2 1.8 copy-start.25
  128.2 1.8 copy-start.27
  130.0 5.3 %copy-start.18 = (bf16[256,5,128]{2,0,1:T(8,128)(2,1)}, bf16[256,5,128]{2,0,1:T(8,128)(2,1)S(1)}, u32[]{:S(2)}) copy-start(bf16[256,5,128]{2,0,1:T(8,128)(2,1)S(1)} %convolution_convert_fusion.4) | copy-start | bytes 983044
  169.8 2.4 copy-start.8
  172.2 1.5 copy-start.11
  173.7 70.1 %copy-start.1 = (f32[128,2560]{1,0:T(8,128)}, f32[128,2560]{1,0:T(8,128)S(1)}, u32[]{:S(2)}) copy-start(f32[128,2560]{1,0:T(8,128)S(1)} %get-tuple-element.42.mid_ref) | copy-start | bytes 3932164
  173.7 9.6 %copy-start.9 = (bf16[2560,1024]{1,0:T(8,128)(2,1)S(1)}, bf16[2560,1024]{1,0:T(8,128)(2,1)}, u32[]{:S(2)}) copy-start(bf16[2560,1024]{1,0:T(8,128)(2,1)} %copy-done.8) | copy-start | bytes 15728644
  173.7 9.6 %copy-start.10 = (bf16[4,128,2560]{2,1,0:T(8,128)(2,1)S(1)}, bf16[4,128,2560]{2,1,0:T(8,128)(2,1)}, u32[]{:S(2)}) copy-start(bf16[4,128,2560]{2,1,0:T(8,128)(2,1)} %get-tuple-element.36) | copy-start | bytes 7864324
  187.8 1.0 copy-start.19
  187.8 1.3 copy-start.20
  187.8 1.6 copy-start.13
  187.8 2.9 copy-start.12
  243.3 1.1 copy-start.4
  246.0 0.8 copy-start.16
  251.1 2.2 copy-start.26
  251.1 2.2 copy-start.28
  251.1 2.2 copy-start.29
  253.3 9.1 %copy-start.31 = (bf16[128,128]{1,0:T(8,128)(2,1)S(1)}, bf16[128,128]{1,0:T(8,128)(2,1)}, u32[]{:S(2)}) copy-start(bf16[128,128]{1,0:T(8,128)(2,1)} %copy-done.30) | copy-start | bytes 98308
  253.3 9.1 %copy-start.33 = (bf16[128,64]{1,0:T(8,128)(2,1)S(1)}, bf16[128,64]{1,0:T(8,128)(2,1)}, u32[]{:S(2)}) copy-start(bf16[128,64]{1,0:T(8,128)(2,1)} %copy-done.32) | copy-start | bytes 49156
  253.3 9.1 %copy-start.35 = (bf16[128,64]{1,0:T(8,128)(2,1)S(1)}, bf16[128,64]{1,0:T(8,128)(2,1)}, u32[]{:S(2)}) copy-start(bf16[128,64]{1,0:T(8,128)(2,1)} %copy-done.34) | copy-start | bytes 49156
  262.4 1.2 copy-start.39
  263.6 8.4 %copy-start.36 = (bf16[1,64,40]{2,1,0:T(8,128)(2,1)S(1)}, bf16[1,64,40]{2,1,0:T(8,128)(2,1)}, u32[]{:S(2)}) copy-start(bf16[1,64,40]{2,1,0:T(8,128)(2,1)} %mul.535) | copy-start | bytes 15364
  263.6 9.4 %copy-start.14 = (bf16[512,1024]{1,0:T(8,128)(2,1)S(1)}, bf16[512,1024]{1,0:T(8,128)(2,1)}, u32[]{:S(2)}) copy-start(bf16[512,1024]{1,0:T(8,128)(2,1)} %copy-done.13) | copy-start | bytes 3145732
  374.5 16.6 %copy-start.22 = (bf16[128,2560]{1,0:T(8,128)(2,1)S(1)}, bf16[128,2560]{1,0:T(8,128)(2,1)}, u32[]{:S(2)}) copy-start(bf16[128,2560]{1,0:T(8,128)(2,1)} %get-tuple-element.96) | copy-start | bytes 1966084
  377.5 14.5 %copy-start.21 = (bf16[128,2560]{1,0:T(8,128)(2,1)S(1)}, bf16[128,2560]{1,0:T(8,128)(2,1)}, u32[]{:S(2)}) copy-start(bf16[128,2560]{1,0:T(8,128)(2,1)} %get-tuple-element.97) | copy-start | bytes 1966084
Sparse Core Ops, SparseCore 0:
  31.5 105.6 all-gather.1
  204.7 113.3 reduce-scatter.1

commit v4 on v3

--- a/solution.py
+++ b/solution.py
@@ -51,126 +51,18 @@
     )
 
 
-def sum_kernel(p_ref, o_ref, from_core, other, from_chips, own, own_low, from_far, send, recv):
-    zl, c, zh = lax.axis_index("zl"), lax.axis_index("c"), lax.axis_index("zh")
-    rows = p_ref.shape[1]
-    half = rows // 2
-    core, far = {"c": 1 - c}, {"zh": 1 - zh}
-    chips = [{"zl": 1 - zl, "zh": k} for k in range(2)]
-    greet([core, far, *chips])
-    order = [1 - zl, zl]
-    cores = [
-        remote(p_ref.at[z * 2 + 1 - c], from_core.at[i], send.at[i], recv.at[i], core)
-        for i, z in enumerate(order)
-    ]
-    for copy in cores:
+def fetch(pairs, sems):
+    copies = [pltpu.make_async_copy(src, dst, sems.at[k]) for k, (src, dst) in enumerate(pairs)]
+    for copy in copies:
         copy.start()
-    step = 16
-    cores[0].wait_recv()
-    aways = []
-    for k in range(2):
-
-        @pl.loop(0, half // step)
-        def _(j, k=k):
-            at = pl.ds(pl.multiple_of(k * half + j * step, step), step)
-            total = p_ref[(1 - zl) * 2 + c, at].astype(jnp.float32) + from_core[0, at].astype(jnp.float32)
-            other[at] = total.astype(jnp.bfloat16)
-
-        away = remote(
-            other.at[pl.ds(k * half, half)], from_chips.at[zh], send.at[2 + k], recv.at[2 + zh], chips[k]
-        )
-        away.start()
-        aways.append(away)
-    cores[1].wait_recv()
-    fars = []
-    for k in range(2):
-        piece = (1 - zh) if k == 0 else zh
-        if k == 1:
-            for i in range(2):
-                remote(
-                    other.at[pl.ds(0, half)], from_chips.at[i], send.at[2 + i], recv.at[2 + i], chips[i]
-                ).wait_recv()
-
-        @pl.loop(0, half // step)
-        def _(j, k=k, piece=piece):
-            at = pl.ds(pl.multiple_of(piece * half + j * step, step), step)
-            total = p_ref[zl * 2 + c, at].astype(jnp.float32) + from_core[1, at].astype(jnp.float32)
-            if k == 1:
-                here = pl.ds(pl.multiple_of(j * step, step), step)
-                total += from_chips[0, here].astype(jnp.float32) + from_chips[1, here].astype(jnp.float32)
-            own[at] = total.astype(jnp.bfloat16)
-
-        at = pl.ds(pl.multiple_of(piece * half, half), half)
-        copy = remote(own.at[at], from_far.at[at], send.at[4 + k], recv.at[4 + k], far)
-        copy.start()
-        fars.append(copy)
-    for k in range(2):
-        fars[k].wait_recv()
-        piece = zh if k == 0 else (1 - zh)
-
-        @pl.loop(0, half // step)
-        def _(j, piece=piece):
-            at = pl.ds(pl.multiple_of(piece * half + j * step, step), step)
-            o_ref[at] = own[at].astype(jnp.float32) + from_far[at].astype(jnp.float32)
-
-    for copy in (*cores, *aways, *fars):
-        copy.wait_send()
-
-
-def token_sum(p, cid):
-    rows, width = p.shape[1:]
-    low = jnp.bfloat16
-    return pl.pallas_call(
-        sum_kernel,
-        out_shape=jax.ShapeDtypeStruct((rows, width), jnp.float32),
-        in_specs=[pl.BlockSpec(memory_space=pltpu.VMEM)],
-        out_specs=pl.BlockSpec(memory_space=pltpu.VMEM),
-        scratch_shapes=[
-            pltpu.VMEM((2, rows, width), low),
-            pltpu.VMEM((rows, width), low),
-            pltpu.VMEM((2, rows // 2, width), low),
-            pltpu.VMEM((rows, width), low),
-            pltpu.VMEM((rows, width), low),
-            pltpu.VMEM((rows, width), low),
-            pltpu.SemaphoreType.DMA((6,)),
-            pltpu.SemaphoreType.DMA((6,)),
-        ],
-        compiler_params=pltpu.CompilerParams(
-            collective_id=cid, has_side_effects=True, vmem_limit_bytes=32 * 2**20
-        ),
-    )(p)
-
-
-def pair_kernel(p_ref, o_ref, landed, send, recv):
-    far = {"zh": 1 - lax.axis_index("zh")}
-    rows = p_ref.shape[0]
-    greet([far])
-    copy = remote(p_ref, landed, send, recv, far)
-    copy.start()
-    copy.wait()
-    step = 16
-
-    @pl.loop(0, rows // step)
-    def _(j):
-        at = pl.ds(pl.multiple_of(j * step, step), step)
-        o_ref[at] = p_ref[at].astype(jnp.float32) + landed[at].astype(jnp.float32)
-
-
-def pair_sum(p, cid):
-    return pl.pallas_call(
-        pair_kernel,
-        out_shape=jax.ShapeDtypeStruct(p.shape, jnp.float32),
-        in_specs=[pl.BlockSpec(memory_space=pltpu.VMEM)],
-        out_specs=pl.BlockSpec(memory_space=pltpu.VMEM),
-        scratch_shapes=[
-            pltpu.VMEM(p.shape, p.dtype),
-            pltpu.SemaphoreType.DMA,
-            pltpu.SemaphoreType.DMA,
-        ],
-        compiler_params=pltpu.CompilerParams(
-            collective_id=cid, has_side_effects=True, vmem_limit_bytes=32 * 2**20
-        ),
-    )(p)
+    return copies
+
+
+def buffers(*arrays):
+    return [pltpu.VMEM(a.shape, a.dtype) for a in arrays]
+
+
+HBM = pl.BlockSpec(memory_space=pltpu.HBM)
 
 
 def ring_of(axis, at):
@@ -215,37 +107,57 @@
 
 
 def exchange_kernel(
-    a_ref, g_ref, s_ref, tok_ref, cot_ref, order_ref, ao_ref, go_ref, so_ref, x_ref, dy_ref, here, send, recv
+    a_ref, g_ref, s_ref, tok_ref, cot_ref, order_ref,
+    ao_out, go_ref, so_out, x_out, dy_out,
+    al, sl, ao_ref, so_ref, x_ref, dy_ref, here, send, recv, out_sem
 ):
     greet(group_peers())
-    finish = send_blocks([a_ref, g_ref, s_ref], [ao_ref, go_ref, so_ref], here, send, recv)
+    finish = send_blocks([a_ref, g_ref, s_ref], [al, go_ref, sl], here, send, recv)
     reorder(tok_ref, order_ref, x_ref, False)
     reorder(cot_ref, order_ref, dy_ref, False)
+    puts = fetch([(x_ref, x_out), (dy_ref, dy_out)], out_sem)
     finish()
-
-
-def group_exchange(arrays, tokens, cotangent, order, cid):
-    n = len(arrays)
-    like = lambda a, kind: jax.ShapeDtypeStruct(a.shape, kind)
+    f32, low = jnp.float32, jnp.bfloat16
+    for h in range(2):
+        parts = [al[t].astype(f32)[h * 40 : (h + 1) * 40] for t in range(4)]
+        ao_ref[h] = jnp.concatenate(parts, axis=0).astype(low)
+    for k in range(2):
+        parts = [sl[t].astype(f32) for t in (2 * k, 2 * k + 1)]
+        parts = [jnp.concatenate([v[:40], v[40:]], axis=1) for v in parts]
+        so_ref[pl.ds(k * 80, 80)] = jnp.concatenate(parts, axis=0).astype(low)
+    last = fetch([(ao_ref, ao_out), (so_ref, so_out)], out_sem.at[pl.ds(2, 2)])
+    for put in (*puts, *last):
+        put.wait()
+
+
+def group_exchange(attn, gains, second, tokens, cotangent, order, cid):
+    low, dma = jnp.bfloat16, pltpu.SemaphoreType.DMA
     anywhere, vmem = pl.BlockSpec(memory_space=pl.ANY), pl.BlockSpec(memory_space=pltpu.VMEM)
+    shapes = [
+            jax.ShapeDtypeStruct((2, 160, attn.shape[2]), low),
+            jax.ShapeDtypeStruct(gains.shape, low),
+            jax.ShapeDtypeStruct((160, 2 * second.shape[2]), low),
+            jax.ShapeDtypeStruct(tokens.shape, jnp.float32),
+            jax.ShapeDtypeStruct(cotangent.shape, low),
+        ]
     return pl.pallas_call(
         exchange_kernel,
-        out_shape=[
-            *(like(a, a.dtype) for a in arrays),
-            like(tokens, jnp.float32),
-            like(cotangent, jnp.bfloat16),
-        ],
-        in_specs=[anywhere] * n + [vmem] * 3,
-        out_specs=[anywhere] * n + [vmem] * 2,
+        out_shape=shapes,
+        in_specs=[anywhere] * 3 + [vmem] * 3,
+        out_specs=[HBM] * 5,
         scratch_shapes=[
-            pltpu.SemaphoreType.DMA((n,)),
-            pltpu.SemaphoreType.DMA((3 * n,)),
-            pltpu.SemaphoreType.DMA((3 * n,)),
+            pltpu.VMEM(attn.shape, low),
+            pltpu.VMEM(second.shape, low),
+            *buffers(shapes[0], *shapes[2:]),
+            dma((3,)),
+            dma((9,)),
+            dma((9,)),
+            dma((4,)),
         ],
         compiler_params=pltpu.CompilerParams(
-            collective_id=cid, has_side_effects=True, vmem_limit_bytes=32 * 2**20
+            collective_id=cid, has_side_effects=True, vmem_limit_bytes=60 * 2**20
         ),
-    )(*arrays, tokens, cotangent, order)
+    )(attn, gains, second, tokens, cotangent, order)
 
 
 ATTN, FEED = 768, 512
@@ -351,8 +263,8 @@
 
 
 def attention_gather_kernel(
-    in_ref, g_ref, dy_ref, d_ref, a_ref, o_ref, go_ref, all_ref, do_ref,
-    here, send, recv, csend, crecv, dsend, drecv, xhere, xsend, xrecv,
+    in_ref, g_ref, dy_ref, d_ref, a_ref, o_ref, go_ref, all_ref, do_out,
+    dl, do_ref, do_sem, here, send, recv, csend, crecv, dsend, drecv, xhere, xsend, xrecv,
 ):
     y, x, c = lax.axis_index("y"), lax.axis_index("x"), lax.axis_index("c")
     zl, zh = lax.axis_index("zl"), lax.axis_index("zh")
@@ -396,7 +308,7 @@
                 i1, _, i2, _ = around(p.h, y, x)
                 keeps.append(pltpu.make_async_copy(p.own(), p.at(i1, i2), here.at[n]))
                 keeps[-1].start()
-            finish = send_blocks([d_ref], [do_ref], xhere, xsend, xrecv)
+            finish = send_blocks([d_ref], [dl], xhere, xsend, xrecv)
             half = dy_ref.shape[0] // 2
             mine, other = zl * 2 + c, (1 - zl) * 2 + c
             part = pl.ds(pl.multiple_of(zh * half, half), half)
@@ -410,6 +322,11 @@
             keeps.append(pltpu.make_async_copy(dy_ref, all_ref.at[mine], here.at[4]))
             keeps[-1].start()
             first_axis()
+            finish()
+            for h in range(2):
+                parts = [dl[t].astype(jnp.float32)[h * 40 : (h + 1) * 40] for t in range(4)]
+                do_ref[h] = jnp.concatenate(parts, axis=0).astype(jnp.bfloat16)
+            puts = fetch([(do_ref, do_out)], do_sem)
             second_axis()
             passed = []
             for k in range(2):
@@ -423,9 +340,8 @@
                 copy.wait()
             for copy in away:
                 copy.wait_send()
-            for keep in keeps:
+            for keep in (*keeps, *puts):
                 keep.wait()
-            finish()
 
 
 def attention_gather(own, gains, dy, down, cid):
@@ -437,11 +353,14 @@
             jax.ShapeDtypeStruct((2560, 1280), kind),
             jax.ShapeDtypeStruct((1024, 128), kind),
             jax.ShapeDtypeStruct((4, *dy.shape), kind),
-            jax.ShapeDtypeStruct(down.shape, kind),
+            jax.ShapeDtypeStruct((2, 160, down.shape[2]), kind),
         ],
-        in_specs=[pl.BlockSpec(memory_space=pl.ANY)] * 4,
-        out_specs=[pl.BlockSpec(memory_space=pl.ANY)] * 5,
+        in_specs=[HBM] * 4,
+        out_specs=[HBM] * 5,
         scratch_shapes=[
+            pltpu.VMEM(down.shape, kind),
+            pltpu.VMEM((2, 160, down.shape[2]), kind),
+            dma((1,)),
             dma((5,)),
             dma((80,)),
             dma((80,)),
@@ -458,22 +377,28 @@
 
 
 def middle_kernel(
-    p_ref, x_ref, g_ref, d_ref, mid_ref, all_ref, w_ref, landed, here, psend, precv, gsend, grecv, send, recv
+    x_in, g1_ref, g2_ref, cos_ref, sin_ref, wq_ref, wo_ref, d_ref,
+    mid_out, all_out, w_ref, xn_out, mixed_out, q_out, kv_out, soft_out,
+    x_ref, mid_ref, all_ref, xn_ref, mixed_ref, q_ref, kv_ref, soft_ref, in_sem, out_sem,
+    wq, wo, p_ref, landed, here, wsem, psend, precv, gsend, grecv, send, recv, csend, crecv,
 ):
     y, x, c = lax.axis_index("y"), lax.axis_index("x"), lax.axis_index("c")
     zl, zh = lax.axis_index("zl"), lax.axis_index("zh")
     core, far = {"c": 1 - c}, {"zh": 1 - zh}
     chips = [{"zl": 1 - zl, "zh": k} for k in range(2)]
+    f32, low = jnp.float32, jnp.bfloat16
+    heads = soft_ref.shape[0]
+    get_x = fetch([(x_in, x_ref)], in_sem)[0]
+    loads = []
+    for k in range(heads + 2):
+        columns = pl.ds(k * HEAD_DIM, HEAD_DIM)
+        loads.append(pltpu.make_async_copy(wq_ref.at[:, columns], wq.at[:, columns], wsem.at[k]))
+    for k in range(5):
+        some = pl.ds(k * 512, 512)
+        loads.append(pltpu.make_async_copy(wo_ref.at[some], wo.at[some], wsem.at[heads + 2 + k]))
+    for k in (heads, heads + 1, *range(heads), *range(heads + 2, heads + 7)):
+        loads[k].start()
     greet([*ring_of("x", x), *ring_of("y", y), core, far, *chips])
-    half, step = p_ref.shape[0] // 2, 16
-    mine, other = zl * 2 + c, (1 - zl) * 2 + c
-    parts = [pl.ds(pl.multiple_of(k * half, half), half) for k in (1 - zh, zh)]
-    pair = [
-        remote(p_ref.at[part], landed.at[part], psend.at[k], precv.at[k], far)
-        for k, part in enumerate(parts)
-    ]
-    for copy in pair:
-        copy.start()
     pieces = [
         Piece(h, d_ref.at[h, pl.ds(0, 160)], w_ref, pl.ds(h * FEED, FEED)) for h in range(2)
     ]
@@ -486,6 +411,66 @@
         i1, _, i2, _ = around(p.h, y, x)
         keeps.append(pltpu.make_async_copy(p.own(), p.at(i1, i2), here.at[n]))
         keeps[-1].start()
+    half, step = x_ref.shape[0] // 2, 16
+    get_x.wait()
+
+    @pl.loop(0, 2 * half // step)
+    def _(i):
+        at = pl.ds(pl.multiple_of(i * step, step), step)
+        v = x_ref[at]
+        r = lax.rsqrt(jnp.mean(v * v, axis=-1, keepdims=True) + norm_eps)
+        xn_ref[c, at] = (v * r * g1_ref[...]).astype(low)
+
+    shared = [remote(xn_ref.at[c], xn_ref.at[c], csend.at[0], crecv.at[0], core)]
+    shared[0].start()
+
+    def projected(k):
+        loads[k].wait()
+        return jnp.dot(xn_ref[c], wq[:, k * HEAD_DIM : (k + 1) * HEAD_DIM], preferred_element_type=f32)
+
+    def rotated(u):
+        turn = u[:, :ROT]
+        turn = turn * cos_ref[...] + pltpu.roll(turn, ROT // 2, 1) * sin_ref[...]
+        return jnp.concatenate([turn, u[:, ROT:]], axis=1).astype(low)
+
+    kv_ref[:, :HEAD_DIM] = rotated(projected(heads))
+    kv_ref[:, HEAD_DIM:] = projected(heads + 1).astype(low)
+    rows = lax.broadcasted_iota(jnp.int32, (SEQ_LEN, SEQ_LEN), 0)
+    behind = rows - lax.broadcasted_iota(jnp.int32, (SEQ_LEN, SEQ_LEN), 1)
+    keep_mask = (behind >= 0) & (behind < WINDOW)
+    for h in range(heads):
+        columns = pl.ds(h * HEAD_DIM, HEAD_DIM)
+        q = rotated(projected(h))
+        q_ref[:, columns] = q
+        scores = lax.dot_general(
+            q, kv_ref[:, :HEAD_DIM], (((1,), (1,)), ((), ())), preferred_element_type=f32
+        )
+        scores = jnp.where(keep_mask, scores * HEAD_DIM**-0.5, -1e30)
+        top = jnp.max(scores, axis=-1, keepdims=True)
+        total = top + jnp.log(jnp.sum(jnp.exp(scores - top), axis=-1, keepdims=True))
+        soft = jnp.exp(scores - total)
+        soft_ref[h] = soft
+        mixed_ref[c, :, columns] = jnp.dot(
+            soft.astype(low), kv_ref[:, HEAD_DIM:], preferred_element_type=f32
+        ).astype(low)
+    shared.append(remote(mixed_ref.at[c], mixed_ref.at[c], csend.at[1], crecv.at[1], core))
+    shared[1].start()
+    puts = fetch([(q_ref, q_out), (kv_ref, kv_out), (soft_ref, soft_out)], out_sem)
+    for k in range(5):
+        loads[heads + 2 + k].wait()
+        some = pl.ds(k * 512, 512)
+        p_ref[:, some] = lax.dot_general(
+            mixed_ref[c], wo[some], (((1,), (1,)), ((), ())), preferred_element_type=f32
+        ).astype(low)
+    mine, other = zl * 2 + c, (1 - zl) * 2 + c
+    parts = [pl.ds(pl.multiple_of(k * half, half), half) for k in (1 - zh, zh)]
+    pair = [
+        remote(p_ref.at[part], landed.at[part], psend.at[k], precv.at[k], far)
+        for k, part in enumerate(parts)
+    ]
+    for copy in pair:
+        copy.start()
+    first_axis()
     away, across = [], []
     for k in range(2):
         part = parts[1 - k]
@@ -495,22 +480,21 @@
         @pl.loop(0, half // step)
         def _(i, first=first):
             at = pl.ds(pl.multiple_of(first + i * step, step), step)
-            branch = p_ref[at].astype(jnp.float32) + landed[at].astype(jnp.float32)
+            branch = p_ref[at].astype(f32) + landed[at].astype(f32)
             v = x_ref[at] + branch
             mid_ref[at] = v
             r = lax.rsqrt(jnp.mean(v * v, axis=-1, keepdims=True) + norm_eps)
-            all_ref[mine, at] = (v * r * g_ref[...]).astype(jnp.bfloat16)
-
-        rows = all_ref.at[mine, part]
+            all_ref[mine, at] = (v * r * g2_ref[...]).astype(low)
+
+        ready = all_ref.at[mine, part]
         if k == 0:
             for i in range(2):
-                away.append(remote(rows, rows, gsend.at[i], grecv.at[zh], chips[i]))
+                away.append(remote(ready, ready, gsend.at[i], grecv.at[zh], chips[i]))
                 away[-1].start()
-        across.append(remote(rows, rows, gsend.at[2 + k], grecv.at[2 + k], core))
+        across.append(remote(ready, ready, gsend.at[2 + k], grecv.at[2 + k], core))
         across[-1].start()
         if k == 0:
-            first_axis()
-    second_axis()
+            second_axis()
     passed = []
     for k in range(2):
         there = all_ref.at[other, pl.ds(k * half, half)]
@@ -518,65 +502,94 @@
         passed.append(remote(there, there, gsend.at[4 + k], grecv.at[4 + k], core))
         passed[-1].start()
     last()
-    for copy in (*across, *passed):
+    for copy in (*across, *passed, *shared):
         copy.wait()
+    puts += fetch(
+        [(mid_ref, mid_out), (all_ref, all_out), (xn_ref, xn_out), (mixed_ref, mixed_out)],
+        out_sem.at[pl.ds(3, 4)],
+    )
     for copy in (*away, *pair):
         copy.wait_send()
-    for keep in keeps:
+    for keep in (*keeps, *puts):
         keep.wait()
 
 
-def middle(p, x, gain, down, cid):
-    dma = pltpu.SemaphoreType.DMA
-    anywhere, vmem = pl.BlockSpec(memory_space=pl.ANY), pl.BlockSpec(memory_space=pltpu.VMEM)
+def middle(x, gain_one, gain_two, cosine, sine, w_q_kv, w_out_t, down, cid):
+    dma, f32, low = pltpu.SemaphoreType.DMA, jnp.float32, jnp.bfloat16
+    vmem = pl.BlockSpec(memory_space=pltpu.VMEM)
+    rows, width = x.shape
+    wide = w_out_t.shape[1]
+    heads = wide // HEAD_DIM
+    shapes = [
+        jax.ShapeDtypeStruct(x.shape, f32),
+        jax.ShapeDtypeStruct((4, *x.shape), low),
+        jax.ShapeDtypeStruct((2560, 2 * FEED), low),
+        jax.ShapeDtypeStruct((2, rows, width), low),
+        jax.ShapeDtypeStruct((2, rows, wide), low),
+        jax.ShapeDtypeStruct((rows, wide), low),
+        jax.ShapeDtypeStruct((rows, 2 * HEAD_DIM), low),
+        jax.ShapeDtypeStruct((heads, rows, rows), f32),
+    ]
     return pl.pallas_call(
         middle_kernel,
-        out_shape=[
-            jax.ShapeDtypeStruct(x.shape, jnp.float32),
-            jax.ShapeDtypeStruct((4, *x.shape), jnp.bfloat16),
-            jax.ShapeDtypeStruct((2560, 2 * FEED), jnp.bfloat16),
-        ],
-        in_specs=[vmem, vmem, vmem, anywhere],
-        out_specs=[vmem, vmem, anywhere],
+        out_shape=shapes,
+        in_specs=[HBM] + [vmem] * 4 + [HBM] * 3,
+        out_specs=[HBM] * 8,
         scratch_shapes=[
-            pltpu.VMEM(p.shape, p.dtype),
+            *buffers(x, *shapes[:2], *shapes[3:]),
+            dma((1,)),
+            dma((7,)),
+            pltpu.VMEM(w_q_kv.shape, low),
+            pltpu.VMEM(w_out_t.shape, low),
+            pltpu.VMEM(x.shape, low),
+            pltpu.VMEM(x.shape, low),
             dma((2,)),
+            dma((heads + 7,)),
             dma((2,)),
             dma((2,)),
             dma((6,)),
             dma((6,)),
             dma((40,)),
             dma((40,)),
+            dma((2,)),
+            dma((2,)),
         ],
         compiler_params=pltpu.CompilerParams(
-            collective_id=cid, has_side_effects=True, vmem_limit_bytes=32 * 2**20
+            collective_id=cid, has_side_effects=True, vmem_limit_bytes=60 * 2**20
         ),
-    )(p, x, gain, down)
-
-
-def finish_kernel(s_ref, down_ref, gate_ref, up_ref, landed, here, send, recv):
+    )(x, gain_one, gain_two, cosine, sine, w_q_kv, w_out_t, down)
+
+
+def finish_kernel(s_in, down_ref, gate_ref, up_ref, s_ref, in_sem, blocks, landed, here, send, recv):
+    get = fetch([(s_in, s_ref)], in_sem)[0]
     greet(group_peers())
-    send_blocks([s_ref], [landed], here, send, recv)()
+    get.wait()
+    wide = s_ref.shape[1] // 2
+    for t in range(4):
+        first = t * 40 // 16 * 16
+        size = (t * 40 + 40 + 15) // 16 * 16 - first
+        v = s_ref[pl.ds(first, size)].astype(jnp.float32)[t * 40 - first : t * 40 - first + 40]
+        blocks[t] = jnp.concatenate([v[:, :wide], v[:, wide:]], axis=0).astype(jnp.bfloat16)
+    send_blocks([blocks], [landed], here, send, recv)()
     for t in range(4):
         v = landed[t].astype(jnp.float32)
+        v = jnp.concatenate([v[:40], v[40:]], axis=1)
         for k, out in enumerate((down_ref, gate_ref, up_ref)):
-            for h in range(2):
-                width = min(FEED, 960 - h * FEED)
-                first = t * 960 + h * FEED
-                out[:, first : first + width] = v[(2 * k + h) * 40 : (2 * k + h + 1) * 40, :width]
+            out[:, t * 960 : (t + 1) * 960] = v[:, k * 2 * FEED : k * 2 * FEED + 960]
 
 
 def finish(sent, cid):
     dma = pltpu.SemaphoreType.DMA
     vmem = pl.BlockSpec(memory_space=pltpu.VMEM)
+    buffer = pltpu.VMEM((4, 80, sent.shape[1] // 2), sent.dtype)
     return pl.pallas_call(
         finish_kernel,
         out_shape=[jax.ShapeDtypeStruct((40, 3840), jnp.float32)] * 3,
-        in_specs=[pl.BlockSpec(memory_space=pl.ANY)],
+        in_specs=[HBM],
         out_specs=[vmem] * 3,
-        scratch_shapes=[pltpu.VMEM(sent.shape, sent.dtype), dma((1,)), dma((3,)), dma((3,))],
+        scratch_shapes=[*buffers(sent), dma((1,)), buffer, buffer, dma((1,)), dma((3,)), dma((3,))],
         compiler_params=pltpu.CompilerParams(
-            collective_id=cid, has_side_effects=True, vmem_limit_bytes=32 * 2**20
+            collective_id=cid, has_side_effects=True, vmem_limit_bytes=60 * 2**20
         ),
     )(sent)
 
@@ -596,16 +609,32 @@
         return self.sums.at[pl.ds(pl.multiple_of(self.first(i1, i2, part or 0), 16), size), self.columns]
 
 
+ORDER = (
+    "P0", "yv0", "yv1", "yv2", "xv0", "P1", "xv1", "P2", "xv2", "P3", "yxm0", "yxv3", "Tc", "yxm1",
+    "T0", "xyt0", "xyv4", "xym2", "gv0", "gv1", "gv2", "gv3", "xyt1", "T1", "xym3", "xyt2", "gm0",
+    "gm1", "gm2", "gm3", "xym4", "xyt3", "gt0", "gt1", "gt2", "gt3", "gv4", "Tg", "gm4", "xyt4",
+    "gt4", "To",
+)
+
+
 def plane_sum_kernel(
-    xn_ref, dq_ref, dl_ref, m_ref, gi_ref, p_ref, t_ref, x_ref, mid_ref, dmid_ref, g_ref, order_ref,
+    left_in, dq_ref, dl_ref, right_in, gi_ref, p_in, t_in, x_in, mid_in, dmid_in, g_ref, order_in,
     attn_ref, go_ref, block_ref, grad_ref,
-    left, right, left_o, right_o, sums, via, main, gsums, gvia, gmain, from_chip, attn_low, gfar, gsum, gall,
+    left, right_o, p_ref, t_ref, x_ref, mid_ref, dmid_ref, order_ref, in_sem,
+    right, left_o, sums, via, main, gsums, gvia, gmain, from_chip, attn_low, gfar, gsum, gall,
     t_core, t_other, t_chips, t_own, t_far, landed, block_low, grad_low,
     here, csend, crecv, send, recv, esend, erecv, tsend, trecv, shere, ssend, srecv,
 ):
     y, x, c, zl, zh = (lax.axis_index(k) for k in ("y", "x", "c", "zl", "zh"))
     core, chip, far_peer = {"c": 1 - c}, {"zl": 1 - zl}, {"zh": 1 - zh}
     chips = [{"zl": 1 - zl, "zh": k} for k in range(2)]
+    get_p, get_t, get_left, get_right, *gets = fetch(
+        [
+            (p_in, p_ref), (t_in, t_ref), (left_in, left), (right_in, right_o), (x_in, x_ref),
+            (mid_in, mid_ref), (dmid_in, dmid_ref), (order_in, order_ref),
+        ],
+        in_sem,
+    )
     greet(
         [*ring_of("x", x), *ring_of("y", y), core, *chips, far_peer, {"zl": 1 - zl, "c": 1 - c}]
     )
@@ -615,21 +644,23 @@
     tokens = p_ref.shape[1]
     half = tokens // 2
 
-    inputs = [(xn_ref, left), (dq_ref, right), (dl_ref, left_o), (m_ref, right_o)]
-    mine, theirs_at = pl.ds(0, tokens), pl.ds(tokens, tokens)
+    inputs = [(dq_ref, right), (dl_ref, left_o)]
+    mine = pl.ds(pl.multiple_of(c * tokens, tokens), tokens)
     shared = [
-        remote(src, dst.at[theirs_at], csend.at[k], crecv.at[k], core) for k, (src, dst) in enumerate(inputs)
+        remote(src, dst.at[mine], csend.at[k], crecv.at[k], core) for k, (src, dst) in enumerate(inputs)
     ]
     kept = [pltpu.make_async_copy(src, dst.at[mine], here.at[k]) for k, (src, dst) in enumerate(inputs)]
-    kept.append(pltpu.make_async_copy(gi_ref, gsums, here.at[4]))
+    kept.append(pltpu.make_async_copy(gi_ref, gsums, here.at[2]))
     for copy in (*shared, *kept):
         copy.start()
     t_cores = [
         remote(p_ref.at[z * 2 + 1 - c], t_core.at[i], tsend.at[i], trecv.at[i], core)
         for i, z in enumerate((1 - zl, zl))
     ]
+    get_p.wait()
     for copy in t_cores:
         copy.start()
+    get_t.wait()
     pair = remote(t_ref, landed, tsend.at[6], trecv.at[6], far_peer)
     pair.start()
     t_sent = []
@@ -785,35 +816,25 @@
         copy.wait()
     for copy in shared:
         copy.wait_recv()
-    for q in range(4):
-        products(q)
-        if q == 0:
-            for j in range(4):
-                out_via(y_first, j)
-                out_via(gain, j)
-        out_via(x_first, q)
-        if q > 0:
-            out_main(x_first, q - 1)
-    tokens_to_chips()
-    for j in range(4):
-        out_main(y_first, j)
-        out_main(gain, j)
-        if j == 0:
-            out_main(x_first, 3)
-            tokens_to_far(0)
-    for j in range(4):
-        for p in (x_first, y_first, gain):
-            take(p, j)
-            if j == 0:
-                out_via(p, 4)
-        if j == 0:
-            tokens_to_far(1)
-    tokens_gradient()
-    for p in (x_first, y_first, gain):
-        out_main(p, 4)
-    tokens_output()
-    for p in (gain, x_first, y_first):
-        take(p, 4)
+    for get in (get_left, get_right, *gets):
+        get.wait()
+    named = {"x": x_first, "y": y_first, "g": gain}
+    acts = {"v": out_via, "m": out_main, "t": take}
+    token_acts = {
+        "Tc": tokens_to_chips,
+        "T0": lambda: tokens_to_far(0),
+        "T1": lambda: tokens_to_far(1),
+        "Tg": tokens_gradient,
+        "To": tokens_output,
+    }
+    for word in ORDER:
+        if word[0] == "P":
+            products(int(word[1]))
+        elif word[0] == "T":
+            token_acts[word]()
+        else:
+            for name in word[:-2]:
+                acts[word[-2]](named[name], int(word[-1]))
     home = (y * 4 + x) * 160
     ghome = pl.ds(pl.multiple_of((y * 4 + x) * 64, 16), 64)
     theirs = pl.ds(pl.multiple_of(home + (1 - zl) * 80, 16), 80)
@@ -863,13 +884,13 @@
             jax.ShapeDtypeStruct(x.shape, low),
             jax.ShapeDtypeStruct(x.shape, low),
         ],
-        in_specs=[vmem] * 12,
+        in_specs=[HBM] * 10 + [vmem, HBM],
         out_specs=[vmem] * 4,
         scratch_shapes=[
-            pltpu.VMEM((2 * rows, width), low),
+            *buffers(xn, mixed, down, d_xn, x, mid, d_mid, order),
+            dma((8,)),
             pltpu.VMEM((2 * rows, d_q_kv.shape[1]), low),
             pltpu.VMEM((2 * rows, width), low),
-            pltpu.VMEM((2 * rows, mixed.shape[1]), low),
             pltpu.VMEM((2560, 2 * ATTN), low),
             pltpu.VMEM((2, 5, 2, 80, ATTN), low),
             pltpu.VMEM((2, 5, 2, 160, ATTN), low),
@@ -889,9 +910,9 @@
             pltpu.VMEM((rows, width), low),
             pltpu.VMEM((rows, width), low),
             pltpu.VMEM((rows, width), low),
-            dma((5,)),
-            dma((4,)),
-            dma((4,)),
+            dma((3,)),
+            dma((2,)),
+            dma((2,)),
             dma((60,)),
             dma((60,)),
             dma((3,)),
@@ -903,52 +924,383 @@
             dma((3,)),
         ],
         compiler_params=pltpu.CompilerParams(
-            collective_id=cid, has_side_effects=True, vmem_limit_bytes=52 * 2**20
+            collective_id=cid, has_side_effects=True, vmem_limit_bytes=60 * 2**20
         ),
     )(xn, d_q_kv, d_low, mixed, gains, down, d_xn, x, mid, d_mid, gain, order)
 
 
-def grads_kernel(dy_ref, xn_ref, h_ref, d_ref, o_ref):
-    def product(left, right):
-        o_ref[...] = lax.dot_general(
-            left[...], right[...], (((0,), (0,)), ((), ())), preferred_element_type=jnp.float32
-        ).astype(o_ref.dtype)
-
-    pl.when(pl.program_id(0) < 4)(lambda: product(dy_ref, h_ref))
-    pl.when(pl.program_id(0) >= 4)(lambda: product(xn_ref, d_ref))
-
-
-def feed_grads(dy, xn, hidden, d_gate_up):
-    depth, rows = dy.shape
-    tile = 256
+GELU_IN, GELU_CUBE = math.sqrt(2.0 / math.pi), 0.044715
+
+
+def feed_kernel(
+    xn_in, dy_ref, g_ref, d_ref, h_out, dg_out, o_ref,
+    xn_ref, h_ref, dg_ref, in_sem, h_sem, dy, wg, wd, dy_turned, xn_turned, back, out, load_sem, out_sem,
+):
+    f32, low = jnp.float32, jnp.bfloat16
+    units, tile, lines = h_ref.shape[1], 256, out.shape[1]
+    get_xn = fetch([(xn_in, xn_ref)], in_sem)[0]
+    get_dy = pltpu.make_async_copy(dy_ref, dy, load_sem.at[0])
+    get_dy.start()
+    loads = []
+    for source, target in ((d_ref, wd), (g_ref, wg)):
+        for n in range(4):
+            some = pl.ds(n * 640, 640)
+            loads.append(pltpu.make_async_copy(source.at[some], target.at[some], load_sem.at[1 + len(loads)]))
+            loads[-1].start()
+    get_xn.wait()
+    xn_turned[...] = xn_ref[...].T
+    get_dy.wait()
+    dy_turned[...] = dy[...].T
+    for n in range(4):
+        loads[n].wait()
+    for k in range(units // tile):
+        at = pl.ds(k * tile, tile)
+        back[:, at] = jnp.dot(dy[...], wd[:, at], preferred_element_type=f32)
+    for n in range(4, 8):
+        loads[n].wait()
+    for k in range(units // tile):
+        at, beside = pl.ds(k * tile, tile), pl.ds(units + k * tile, tile)
+        gate = jnp.dot(xn_ref[...], wg[:, at], preferred_element_type=f32)
+        up = jnp.dot(xn_ref[...], wg[:, beside], preferred_element_type=f32)
+        d = back[:, at]
+        square = gate * gate
+        t = jnp.tanh(GELU_IN * (gate + GELU_CUBE * gate * square))
+        cdf = 0.5 * (1.0 + t)
+        slope = cdf + 0.5 * gate * (1.0 - t * t) * (GELU_IN * (1.0 + 3.0 * GELU_CUBE * square))
+        gelu = gate * cdf
+        h_ref[:, at] = (gelu * up).astype(low)
+        dg_ref[:, at] = (d * up * slope).astype(low)
+        dg_ref[:, beside] = (d * gelu).astype(low)
+
+    puts = fetch([(h_ref, h_out), (dg_ref, dg_out)], h_sem)
+
+    def put(i):
+        slot = lax.rem(i, 2)
+        rows = pl.ds(pl.multiple_of(i * lines, lines), lines)
+        return pltpu.make_async_copy(out.at[slot], o_ref.at[rows], out_sem.at[slot])
+
+    steps = o_ref.shape[0] // lines
+
+    @pl.loop(0, steps)
+    def _(i):
+        slot = lax.rem(i, 2)
+        pl.when(i >= 2)(lambda: put(i - 2).wait())
+        rows = pl.ds(pl.multiple_of(i * lines, lines), lines)
+        for left, right, count, first in ((dy_turned, h_ref, 2, 0), (xn_turned, dg_ref, 4, units)):
+            for k in range(count):
+                out[slot, :, pl.ds(first + k * 512, 512)] = jnp.dot(
+                    left[rows], right[:, pl.ds(k * 512, 512)], preferred_element_type=f32
+                ).astype(low)
+        put(i).start()
+
+    put(steps - 2).wait()
+    put(steps - 1).wait()
+    for copy in puts:
+        copy.wait()
+
+
+def feed(xn, dy, w_gate_up, w_down):
+    depth, width = xn.shape
+    units = w_down.shape[1]
+    low, dma = jnp.bfloat16, pltpu.SemaphoreType.DMA
+    shapes = [
+        jax.ShapeDtypeStruct((depth, units), low),
+        jax.ShapeDtypeStruct((depth, 2 * units), low),
+        jax.ShapeDtypeStruct((width, 3 * units), low),
+    ]
     return pl.pallas_call(
-        grads_kernel,
-        grid=(12,),
-        out_shape=jax.ShapeDtypeStruct((rows, 12 * tile), jnp.bfloat16),
-        in_specs=[
-            pl.BlockSpec((depth, rows), lambda j: (0, 0)),
-            pl.BlockSpec((depth, rows), lambda j: (0, 0)),
-            pl.BlockSpec((depth, tile), lambda j: (0, jnp.minimum(j, 3))),
-            pl.BlockSpec((depth, tile), lambda j: (0, jnp.maximum(j - 4, 0))),
+        feed_kernel,
+        out_shape=shapes,
+        in_specs=[HBM] * 4,
+        out_specs=[HBM] * 3,
+        scratch_shapes=[
+            *buffers(xn, *shapes[:2]),
+            dma((1,)),
+            dma((2,)),
+            pltpu.VMEM((depth, width), low),
+            pltpu.VMEM((width, 2 * units), low),
+            pltpu.VMEM((width, units), low),
+            pltpu.VMEM((width, depth), low),
+            pltpu.VMEM((width, depth), low),
+            pltpu.VMEM((depth, units), jnp.float32),
+            pltpu.VMEM((2, 320, 3 * units), low),
+            dma((9,)),
+            dma((2,)),
         ],
-        out_specs=pl.BlockSpec((rows, tile), lambda j: (0, j)),
-        compiler_params=pltpu.CompilerParams(vmem_limit_bytes=40 * 2**20),
+        compiler_params=pltpu.CompilerParams(vmem_limit_bytes=60 * 2**20),
         cost_estimate=pl.CostEstimate(
-            flops=2 * depth * rows * 12 * tile,
-            bytes_accessed=4 * depth * rows + 2 * rows * 12 * tile,
-            transcendentals=0,
+            flops=12 * depth * width * units,
+            bytes_accessed=4 * depth * width + 12 * width * units + 6 * depth * units,
+            transcendentals=depth * units,
         ),
-    )(dy, xn, hidden, d_gate_up)
-
-
-def rms_norm(values, gain_row):
-    return (
-        values * lax.rsqrt(jnp.mean(values * values, axis=-1, keepdims=True) + norm_eps) * gain_row
+    )(xn, dy, w_gate_up, w_down)
+
+
+def back_kernel(
+    dg_in, h_in, w_ref, d_ref, wo_ref, wq_ref,
+    x_in, mid_in, dy_in, g2_ref, soft_in, q_in, kv_in, cos_ref, sin_ref,
+    down_out, dmid_out, dl_out, dq_out, dx_out, gains_out,
+    dg_ref, h_ref, x_ref, mid_ref, dy_ref, soft_ref, q_ref, kv_ref,
+    down_ref, dmid_ref, dl_ref, dq_ref, dx_ref, gains_ref, in_sem, out_sem,
+    w, wd, wo, part, from_core, other, from_chips, own, from_far, grad, kv_part, kv_far, halved, sums,
+    wsem, send, recv, osem, qsem, fsend, frecv,
+):
+    zl, c, zh = lax.axis_index("zl"), lax.axis_index("c"), lax.axis_index("zh")
+    core, far = {"c": 1 - c}, {"zh": 1 - zh}
+    chips = [{"zl": 1 - zl, "zh": k} for k in range(2)]
+    f32, low = jnp.float32, jnp.bfloat16
+    parts, width = w_ref.shape[0] // 640, 640
+    rows = x_ref.shape[0]
+    half, step = rows // 2, 16
+    heads = soft_ref.shape[0]
+    get_dg, get_h, *gets = fetch(
+        [
+            (dg_in, dg_ref), (h_in, h_ref), (x_in, x_ref), (mid_in, mid_ref), (dy_in, dy_ref),
+            (soft_in, soft_ref), (q_in, q_ref), (kv_in, kv_ref),
+        ],
+        in_sem,
     )
-
-
-def geglu(gate_part, up_part):
-    return jax.nn.gelu(gate_part) * up_part
+    loads = []
+    for source, target, first in ((w_ref, w, 0), (d_ref, wd, parts)):
+        for n in range(parts):
+            some = pl.ds(n * width, width)
+            loads.append(pltpu.make_async_copy(source.at[some], target.at[some], wsem.at[first + n]))
+            loads[-1].start()
+    get_wo = pltpu.make_async_copy(wo_ref, wo, osem)
+    get_wo.start()
+    wq = w.at[:, pl.ds(0, wq_ref.shape[1])]
+    get_wq = pltpu.make_async_copy(wq_ref, wq, qsem)
+    greet([core, far, *chips])
+    order = [1 - zl, zl]
+    started = []
+
+    def go(src, dst, n, out_slot, in_slot, peer):
+        copy = remote(src, dst, send.at[n * 6 + out_slot], recv.at[n * 6 + in_slot], peer)
+        copy.start()
+        started.append(copy)
+
+    def arrived(dst, n, slot):
+        remote(dst, dst, send.at[n * 6 + slot], recv.at[n * 6 + slot], core).wait_recv()
+
+    def columns(n):
+        return pl.ds(n * width, width)
+
+    def product(left, right, n, target):
+        some = pl.ds(n * width, width)
+        v = lax.dot_general(
+            left[...], right[some], (((1,), (1,)), ((), ())), preferred_element_type=f32
+        ).astype(low)
+        for t in range(4):
+            target[t, :, some] = v[t * rows : (t + 1) * rows]
+
+    def multiply(n):
+        loads[n].wait()
+        product(dg_ref, w, n, part)
+        for i, z in enumerate(order):
+            go(part.at[z * 2 + 1 - c, :, columns(n)], from_core.at[i, :, columns(n)], n, i, i, core)
+
+    def down(n):
+        loads[parts + n].wait()
+        product(h_ref, wd, n, down_ref)
+
+    def to_chips(n):
+        arrived(from_core.at[0, :, columns(n)], n, 0)
+
+        @pl.loop(0, rows // step)
+        def _(i):
+            at = pl.ds(pl.multiple_of(i * step, step), step)
+            total = part[(1 - zl) * 2 + c, at, columns(n)].astype(f32) + from_core[0, at, columns(n)].astype(f32)
+            other[at, columns(n)] = total.astype(low)
+
+        for k in range(2):
+            go(other.at[pl.ds(k * half, half), columns(n)], from_chips.at[zh, :, columns(n)], n, 2 + k, 2 + zh, chips[k])
+
+    def to_far(n, k):
+        piece = (1 - zh) if k == 0 else zh
+        if k == 0:
+            arrived(from_core.at[1, :, columns(n)], n, 1)
+        else:
+            for i in range(2):
+                arrived(from_chips.at[i, :, columns(n)], n, 2 + i)
+
+        @pl.loop(0, half // step)
+        def _(i):
+            at = pl.ds(pl.multiple_of(piece * half + i * step, step), step)
+            total = part[zl * 2 + c, at, columns(n)].astype(f32) + from_core[1, at, columns(n)].astype(f32)
+            if k == 1:
+                there = pl.ds(pl.multiple_of(i * step, step), step)
+                total += from_chips[0, there, columns(n)].astype(f32) + from_chips[1, there, columns(n)].astype(f32)
+            own[at, columns(n)] = total.astype(low)
+
+        at = pl.ds(pl.multiple_of(piece * half, half), half)
+        go(own.at[at, columns(n)], from_far.at[at, columns(n)], n, 4 + k, 4 + k, far)
+
+    def finish(n):
+        for k in range(2):
+            arrived(from_far.at[pl.ds(k * half, half), columns(n)], n, 4 + k)
+
+        @pl.loop(0, rows // step)
+        def _(i):
+            at = pl.ds(pl.multiple_of(i * step, step), step)
+            grad[at, columns(n)] = own[at, columns(n)].astype(f32) + from_far[at, columns(n)].astype(f32)
+
+    get_dg.wait()
+    multiply(0)
+    multiply(1)
+    to_chips(0)
+    to_far(0, 0)
+    multiply(2)
+    to_chips(1)
+    to_far(1, 0)
+    multiply(3)
+    get_wq.start()
+    to_chips(2)
+    to_far(2, 0)
+    to_far(0, 1)
+    get_h.wait()
+    down(0)
+    to_chips(3)
+    to_far(3, 0)
+    to_far(1, 1)
+    down(1)
+    to_far(2, 1)
+    down(2)
+    to_far(3, 1)
+    down(3)
+    for n in range(parts):
+        finish(n)
+    sums[...] = jnp.zeros_like(sums)
+    puts = fetch([(down_ref, down_out)], out_sem)
+    for get in gets:
+        get.wait()
+
+    @pl.loop(0, rows // step)
+    def _(i):
+        at = pl.ds(pl.multiple_of(i * step, step), step)
+        v, d = mid_ref[at], grad[at]
+        r = lax.rsqrt(jnp.mean(v * v, axis=-1, keepdims=True) + norm_eps)
+        n = v * r
+        sums[1:2] += jnp.sum(d * n, axis=0, keepdims=True) * 0.5
+        d = d * g2_ref[...]
+        d = dy_ref[at].astype(f32) + r * (d - n * jnp.mean(d * n, axis=-1, keepdims=True))
+        dmid_ref[at] = d
+        dl_ref[at] = d.astype(low)
+
+    def across(left, right, left_dim, right_dim):
+        return lax.dot_general(
+            left, right, (((left_dim,), (right_dim,)), ((), ())), preferred_element_type=f32
+        )
+
+    def turned_back(u):
+        turn = u[:, :ROT]
+        turn = turn * cos_ref[...] - pltpu.roll(turn, ROT // 2, 1) * sin_ref[...]
+        return jnp.concatenate([turn, u[:, ROT:]], axis=1).astype(low)
+
+    get_wo.wait()
+    puts += fetch([(dmid_ref, dmid_out), (dl_ref, dl_out)], out_sem.at[pl.ds(1, 2)])
+    keys, values = kv_ref[:, :HEAD_DIM], kv_ref[:, HEAD_DIM:]
+    scale = HEAD_DIM**-0.5
+    d_keys = jnp.zeros((rows, HEAD_DIM), f32)
+    d_values = jnp.zeros((rows, HEAD_DIM), f32)
+    for h in range(heads):
+        at = pl.ds(h * HEAD_DIM, HEAD_DIM)
+        d_mixed = jnp.dot(dl_ref[...], wo[:, at], preferred_element_type=f32).astype(low)
+        soft = soft_ref[h]
+        d_probs = across(d_mixed, values, 1, 1)
+        d_scores = (soft * (d_probs - jnp.sum(soft * d_probs, axis=-1, keepdims=True))).astype(low)
+        dq_ref[:, at] = turned_back(jnp.dot(d_scores, keys, preferred_element_type=f32) * scale)
+        d_keys += across(d_scores, q_ref[:, at], 0, 0)
+        d_values += across(soft.astype(low), d_mixed, 0, 0)
+    kv_part[:, :HEAD_DIM] = turned_back(d_keys * scale)
+    kv_part[:, HEAD_DIM:] = d_values.astype(low)
+    pair = remote(kv_part, kv_far, fsend, frecv, far)
+    pair.start()
+    pair.wait()
+    first_kv = heads * HEAD_DIM
+    kv = kv_part[...].astype(f32) + kv_far[...].astype(f32)
+    kv = kv.astype(low)
+    dq_ref[:, first_kv:] = kv
+    halved[:, :first_kv] = dq_ref[:, :first_kv]
+    halved[:, first_kv:] = kv * 0.5
+    get_wq.wait()
+    for k in range(5):
+        some = pl.ds(k * 512, 512)
+        d = across(halved[...], w[some, : wq_ref.shape[1]], 1, 1)
+        grad[:, some] = d
+        dx_ref[:, some] = d.astype(low)
+
+    @pl.loop(0, rows // step)
+    def _(i):
+        at = pl.ds(pl.multiple_of(i * step, step), step)
+        v = x_ref[at]
+        r = lax.rsqrt(jnp.mean(v * v, axis=-1, keepdims=True) + norm_eps)
+        sums[0:1] += jnp.sum(grad[at] * (v * r), axis=0, keepdims=True)
+
+    both = jnp.concatenate([sums[...], jnp.zeros((8, sums.shape[1]), f32)], axis=0)
+    for k in range(64):
+        tile = jnp.concatenate([both[:, k * 40 : (k + 1) * 40], jnp.zeros((16, 88), f32)], axis=1)
+        gains_ref[k * 16 : (k + 1) * 16] = tile.astype(low)
+    puts += fetch([(dq_ref, dq_out), (dx_ref, dx_out), (gains_ref, gains_out)], out_sem.at[pl.ds(3, 3)])
+    for copy in started:
+        copy.wait_send()
+    for copy in puts:
+        copy.wait()
+
+
+def feed_back(
+    d_gate_up, hidden, w_gate_up, w_down, w_out, w_q_kv,
+    x, mid, dy, gain, soft, queries, keys_values, cosine, sine, cid,
+):
+    dma, low, f32 = pltpu.SemaphoreType.DMA, jnp.bfloat16, jnp.float32
+    vmem = pl.BlockSpec(memory_space=pltpu.VMEM)
+    rows, width = x.shape
+    wide = w_q_kv.shape[1]
+    shapes = [
+        jax.ShapeDtypeStruct((4, rows, width), low),
+        jax.ShapeDtypeStruct((rows, width), f32),
+        jax.ShapeDtypeStruct((rows, width), low),
+        jax.ShapeDtypeStruct((rows, wide), low),
+        jax.ShapeDtypeStruct((rows, width), low),
+        jax.ShapeDtypeStruct((1024, 128), low),
+    ]
+    return pl.pallas_call(
+        back_kernel,
+        out_shape=shapes,
+        in_specs=[HBM] * 9 + [vmem] + [HBM] * 3 + [vmem] * 2,
+        out_specs=[HBM] * 6,
+        scratch_shapes=[
+            *buffers(d_gate_up, hidden, x, mid, dy, soft, queries, keys_values, *shapes),
+            dma((8,)),
+            dma((6,)),
+            pltpu.VMEM(w_gate_up.shape, low),
+            pltpu.VMEM(w_down.shape, low),
+            pltpu.VMEM(w_out.shape, low),
+            pltpu.VMEM((4, rows, width), low),
+            pltpu.VMEM((2, rows, width), low),
+            pltpu.VMEM((rows, width), low),
+            pltpu.VMEM((2, rows // 2, width), low),
+            pltpu.VMEM((rows, width), low),
+            pltpu.VMEM((rows, width), low),
+            pltpu.VMEM((rows, width), f32),
+            pltpu.VMEM(keys_values.shape, low),
+            pltpu.VMEM(keys_values.shape, low),
+            pltpu.VMEM((rows, wide), low),
+            pltpu.VMEM((8, width), f32),
+            dma((8,)),
+            dma((24,)),
+            dma((24,)),
+            dma,
+            dma,
+            dma,
+            dma,
+        ],
+        compiler_params=pltpu.CompilerParams(
+            collective_id=cid, has_side_effects=True, vmem_limit_bytes=60 * 2**20
+        ),
+    )(
+        d_gate_up, hidden, w_gate_up, w_down, w_out, w_q_kv,
+        x, mid, dy, gain, soft, queries, keys_values, cosine, sine,
+    )
 
 
 def tables():
@@ -956,21 +1308,6 @@
     rates = jnp.exp(jnp.arange(half_rot, dtype=jnp.float32) * (-2.0 * math.log(10000.0) / ROT))
     angles = jnp.arange(SEQ_LEN, dtype=jnp.float32)[:, None] * rates[None, :]
     return (jnp.cos(angles), jnp.sin(angles))
-
-
-def rotate(field, cosine, sine):
-    half_rot = ROT // 2
-    first = field[..., :half_rot]
-    second = field[..., half_rot:ROT]
-    return jnp.concatenate(
-        [first * cosine - second * sine, second * cosine + first * sine, field[..., ROT:]], axis=-1
-    )
-
-
-def contract(left, right, left_dim, right_dim):
-    return lax.dot_general(
-        left, right, (((left_dim,), (right_dim,)), ((), ())), preferred_element_type=jnp.float32
-    )
 
 
 def padded(weight):
@@ -991,15 +1328,8 @@
 ):
     low = jnp.bfloat16
     rows = tokens.shape[0]
-    seqs = rows // SEQ_LEN
-    heads_here = query_weight.shape[1] // HEAD_DIM
-    wide = heads_here * HEAD_DIM
-    scale = HEAD_DIM ** (-0.5)
+    wide = query_weight.shape[1]
     cosine, sine = tables()
-    positions = jnp.arange(SEQ_LEN)
-    keep_mask = (positions[:, None] >= positions[None, :]) & (
-        positions[:, None] - positions[None, :] < WINDOW
-    )
     attn = jnp.concatenate([query_weight, kv_weight, out_weight.T], axis=1)
     attn = attn.reshape(40, 2, 2, ATTN).transpose(1, 2, 0, 3)
     attn = jnp.broadcast_to(attn, (2, *attn.shape)).reshape(4, 2, 40, ATTN)
@@ -1011,105 +1341,51 @@
     second = second.transpose(2, 0, 1, 3).reshape(4, 80, 2 * FEED)
     order = jnp.asarray(feature_order(), low)
     first, gains, second, x_in, dy_here = group_exchange(
-        [first, gains, second], tokens, cotangent, order, 5
+        first, gains, second, tokens, cotangent, order, 5
     )
-    second = second.reshape(4, 2, 40, 2 * FEED).transpose(0, 2, 1, 3).reshape(160, 4 * FEED)
     w_gate_up = lax.all_gather(second, PLANE, axis=0, tiled=True)
-    first = first.reshape(4, 2, 40, ATTN).transpose(1, 0, 2, 3).reshape(2, 160, ATTN)
     w_q_kv, w_out_t, gains, dy, down = attention_gather(first, gains.reshape(64, 128), dy_here, down, 6)
     gains = gains.reshape(64, 16, 128)[:, :2, :40].transpose(1, 0, 2).reshape(2, 2560).astype(jnp.float32)
-    down = down.reshape(4, 2, 40, FEED).transpose(1, 0, 2, 3).reshape(2, 160, FEED)
     dy = dy.reshape(4 * rows, -1)
-    gain_one, gain_two = gains[0], gains[1]
-
-    xn_one = rms_norm(x_in, gain_one).astype(low)
-    q_kv_pre = jnp.dot(xn_one, w_q_kv, preferred_element_type=jnp.float32)
-    q_pre, kv_pre = q_kv_pre[:, :wide], q_kv_pre[:, wide:]
-    queries = rotate(
-        q_pre.reshape(seqs, SEQ_LEN, heads_here, HEAD_DIM), cosine[:, None, :], sine[:, None, :]
-    ).astype(low)
-    key_rot = rotate(kv_pre[:, :HEAD_DIM].reshape(seqs, SEQ_LEN, HEAD_DIM), cosine, sine).astype(low)
-    value_rows = kv_pre[:, HEAD_DIM:].reshape(seqs, SEQ_LEN, HEAD_DIM).astype(low)
-
-    def score_rows():
-        raw = (
-            jnp.einsum("sqhd,skd->shqk", queries, key_rot, preferred_element_type=jnp.float32)
-            * scale
-        )
-        return jnp.where(keep_mask, raw, -1e30)
-
-    scores = score_rows()
-    row_max = jnp.max(scores, axis=-1, keepdims=True)
-    log_total = row_max + jnp.log(jnp.sum(jnp.exp(scores - row_max), axis=-1, keepdims=True))
-    attn_probs = jnp.exp(scores - log_total).astype(low)
-    mixed_heads = jnp.einsum(
-        "shqk,skd->sqhd", attn_probs, value_rows, preferred_element_type=jnp.float32
+    gain_one, gain_two = gains[0][None, :], gains[1][None, :]
+    cosine = jnp.concatenate([cosine, cosine], axis=1)
+    sine = jnp.concatenate([-sine, sine], axis=1)
+    x_mid, xn_all, w_down_t, xn_one, mixed_heads, queries, keys_values, soft_rows = middle(
+        x_in, gain_one, gain_two, cosine, sine, w_q_kv, w_out_t, down, 2
     )
-    mixed_heads = mixed_heads.reshape(rows, wide).astype(low)
-    attn_part = contract(mixed_heads, w_out_t, 1, 1).astype(low)
-    x_mid, xn_all, w_down_t = middle(attn_part, x_in, gain_two[None, :], down, 2)
     xn_all = xn_all.reshape(4 * rows, -1)
-    gate_up = jnp.dot(xn_all, w_gate_up, preferred_element_type=jnp.float32)
-    gate_pre, up_pre = gate_up[:, : 2 * FEED], gate_up[:, 2 * FEED :]
-    hidden = geglu(gate_pre, up_pre).astype(low)
-    down_part = contract(hidden, w_down_t, 1, 1).astype(low)
-    d_hidden = jnp.dot(dy, w_down_t, preferred_element_type=jnp.float32)
-    geglu_pull = jax.vjp(geglu, gate_pre, up_pre)[1]
-    d_gate_pre, d_up_pre = geglu_pull(d_hidden)
-    d_gate_low = d_gate_pre.astype(low)
-    d_up_low = d_up_pre.astype(low)
-    d_gate_up = jnp.concatenate([d_gate_low, d_up_low], axis=1)
-    sent = feed_grads(dy, xn_all, hidden, d_gate_up)
+    hidden, d_gate_up, sent = feed(xn_all, dy, w_gate_up, w_down_t)
     sent = lax.psum_scatter(sent, PLANE, scatter_dimension=0, tiled=True)
-    sent = sent.reshape(4, 40, 3, 2, FEED).transpose(0, 2, 3, 1, 4).reshape(4, 240, FEED)
-    d_xn_two_part = contract(d_gate_up, w_gate_up, 1, 1)
-    d_xn_two = token_sum(d_xn_two_part.astype(low).reshape(4, rows, -1), 3)
-
-    norm_two_pull = jax.vjp(rms_norm, x_mid, gain_two)[1]
-    d_mid_norm, d_gain_two = norm_two_pull(d_xn_two)
-    d_mid = dy_here.astype(jnp.float32) + d_mid_norm
-    d_mid_low = d_mid.astype(low)
-    d_mixed = (
-        jnp.dot(d_mid_low, w_out_t, preferred_element_type=jnp.float32)
-        .astype(low)
-        .reshape(seqs, SEQ_LEN, heads_here, HEAD_DIM)
+    down_part, d_mid, d_mid_low, d_q_kv, d_xn_one, d_gains = feed_back(
+        d_gate_up,
+        hidden,
+        w_gate_up,
+        w_down_t,
+        w_out_t,
+        w_q_kv,
+        x_in,
+        x_mid,
+        dy_here,
+        gain_two,
+        soft_rows,
+        queries,
+        keys_values,
+        cosine,
+        sine,
+        3,
     )
-    soft_rows = jnp.exp(score_rows() - log_total)
-    d_probs = jnp.einsum("sqhd,skd->shqk", d_mixed, value_rows, preferred_element_type=jnp.float32)
-    d_scores = (
-        soft_rows * (d_probs - jnp.sum(soft_rows * d_probs, axis=-1, keepdims=True))
-    ).astype(low)
-    d_queries = (
-        jnp.einsum("shqk,skd->sqhd", d_scores, key_rot, preferred_element_type=jnp.float32) * scale
-    )
-    d_keys = (
-        jnp.einsum("shqk,sqhd->skd", d_scores, queries, preferred_element_type=jnp.float32) * scale
-    )
-    d_values = jnp.einsum("shqk,sqhd->skd", attn_probs, d_mixed, preferred_element_type=jnp.float32)
-    d_q_pre = (
-        rotate(d_queries, cosine[:, None, :], -sine[:, None, :]).reshape(rows, wide).astype(low)
-    )
-    d_k_pre = rotate(d_keys, cosine, -sine).reshape(rows, HEAD_DIM)
-    d_kv_part = jnp.concatenate([d_k_pre, d_values.reshape(rows, HEAD_DIM)], axis=-1)
-    d_kv_low = pair_sum(d_kv_part.astype(low), 4).astype(low)
-    d_xn_one = contract(jnp.concatenate([d_q_pre, d_kv_low * 0.5], axis=1), w_q_kv, 1, 1)
-    norm_one_pull = jax.vjp(lambda g: rms_norm(x_in, g), gain_one)[1]
-    d_gain_one = norm_one_pull(d_xn_one)[0]
-    d_gains = jnp.stack([d_gain_one, 0.5 * d_gain_two], axis=0).astype(low)
-    d_gains = d_gains.reshape(2, 64, 40).transpose(1, 0, 2)
-    d_gains = jnp.pad(d_gains, ((0, 0), (0, 14), (0, 88))).reshape(1024, 128)
     attn_out, gain_out, block_out, tokens_grad = plane_sum(
-        xn_one,
-        jnp.concatenate([d_q_pre, d_kv_low], axis=1),
+        xn_one.reshape(2 * rows, -1),
+        d_q_kv,
         d_mid_low,
-        mixed_heads,
+        mixed_heads.reshape(2 * rows, -1),
         d_gains,
-        down_part.reshape(4, rows, -1),
-        d_xn_one.astype(low),
+        down_part,
+        d_xn_one,
         x_in,
         x_mid,
         d_mid,
-        gain_one[None, :],
+        gain_one,
         order,
         7,
     )

time: 409 us -> 378 us (0.924)
  matrix products: 56.6 us -> 0 us
  Pallas kernels: 287 us -> 337 us
  local copies, waits for them, and re-layouts: 35.5 us -> 17.8 us
  other arithmetic: 7.78 us -> 2.97 us
    dot_general x14 -> x0, matrix products: 56.6 us -> none  [the longest x4 29.3 us: contract(): lax.dot_general(left, right, (((left_dim,), (right_dim,)), ((), ())), pre...]
    pallas_call x5 -> x4, Pallas kernels: 99.9 us -> 145 us  [the longest x1 50.4 us: middle(): pl.pallas_call(middle_kernel, out_shape=shapes, in_specs=[HBM] + [vmem] *...]
    unnamed x94 -> x21, local copies, waits for them, and re-layouts: 16.8 us -> 5.43 us
    reshape x6 -> x0, local copies, waits for them, and re-layouts: 5.68 us -> none  [the longest x2 3.18 us: local(): sent.reshape(4, 40, 3, 2, FEED).transpose(0, 2, 3, 1, 4)]
  transfers between devices with their start and end apart: 2 -> 2, of which waited for: 0 -> 0; matrix products, arithmetic and copies ran while one was open for 16% -> 3% of each run, Pallas kernels for 60% -> 74%
where the time goes in v4:
time: 378 us; the launch traced here: 373 us
  Pallas kernels  337 us (89%)
  local copies, waits for them, and re-layouts  17.8 us (5%)
  between operations  14.8 us (4%)
    pallas_call x1, Pallas kernels, plane_sum(): pl.pallas_call(plane_sum_kernel, out_shape=[jax.ShapeDtypeStruct((40, 4 *...  96.8 us
    pallas_call x1, Pallas kernels, attention_gather(): pl.pallas_call(attention_gather_kernel, out_shape=[jax.ShapeDtypeStruct((...  80 us
    pallas_call x1, Pallas kernels, middle(): pl.pallas_call(middle_kernel, out_shape=shapes, in_specs=[HBM] + [vmem] *...  50.4 us
    pallas_call x1, Pallas kernels, feed_back(): pl.pallas_call(back_kernel, out_shape=shapes, in_specs=[HBM] * 9 + [vmem]...  46.8 us
    pallas_call x1, Pallas kernels, feed(): pl.pallas_call(feed_kernel, out_shape=shapes, in_specs=[HBM] * 4, out_spe...  28.6 us
    pallas_call x1, Pallas kernels, group_exchange(): pl.pallas_call(exchange_kernel, out_shape=shapes, in_specs=[anywhere] * 3...  19.6 us
    pallas_call x1, Pallas kernels, finish(): pl.pallas_call(finish_kernel, out_shape=[jax.ShapeDtypeStruct((40, 3840),...  14.6 us
  transfers between devices with their start and end apart: 2, of which 0 were waited for; matrix products, arithmetic and copies ran while one was open for 3% of the time, Pallas kernels for 74%

profile of v4, /device:TPU:1, one launch (start us, length us, event | category | flops | bytes accessed | tf_op | source)
XLA Modules:
  0.0 372.6 jit_solution(4663695102623385051)
XLA Ops:
  7.2 0.0 copy-start.4
  7.2 0.0 copy-start.6
  7.2 0.0 copy-start.7
  7.2 0.0 all-gather.2.cloned.1.call-start
  7.3 1.0 pad_maximum_fusion.1
  8.3 0.2 reshape.68
  8.5 1.4 reshape.69
  9.9 0.1 copy.26
  10.0 0.0 copy-done.4
  10.0 0.5 reshape.70
  10.5 0.1 copy.27
  10.6 0.0 copy-done.6
  10.6 0.0 copy-done.7
  10.7 0.1 pad_bitcast_fusion
  10.7 0.9 pad_maximum_fusion
  11.6 0.0 copy-start.5
  11.6 0.6 broadcast_in_dim.9.g_ref
  12.2 0.8 broadcast_in_dim.8
  13.0 19.6 %shard_map.186 = (bf16[2,160,768]{2,1,0:T(8,128)(2,1)}, bf16[4,16,128]{2,1,0:T(8,128)(2,1)}, bf16[160,2048]{1,0:T(8,128)(2,1)}, f32[128,2560]{1,0:T(8,128)}, bf16[128,2560]{1,0:T(8,128)(2,1)}) custom-call(bf16[4,80,768]{2,1,0:T(8,128)(2,1)} %bitcast.33, bf16[4,16,128]{2,1,0:T(8,128)(2,1)} %broadcast_in_dim.9.g_ref, bf16[4,80,1024]{2,1,0:T(8,128)(2,1)} %bitcast.32, ...), custom_call_target="tpu_custom_call" | custom-call | tf_op jit(solution)/shard_map/pallas_call | solution.py:143
  32.7 0.0 all-gather.2.cloned.1.call-update
  32.7 0.0 reduce-scatter.2.cloned.1.call-start
  32.7 0.0 copy-done.5
  32.7 0.5 reshape.73
  33.2 0.1 copy.28
  33.3 0.2 reshape.74
  33.6 0.8 copy.29
  34.3 80.0 %shard_map.187 = (bf16[2560,1792]{1,0:T(8,128)(2,1)}, bf16[2560,1280]{1,0:T(8,128)(2,1)}, bf16[1024,128]{1,0:T(8,128)(2,1)}, bf16[4,128,2560]{2,1,0:T(8,128)(2,1)}, bf16[2,160,512]{2,1,0:T(8,128)(2,1)}) custom-call(bf16[2,160,768]{2,1,0:T(8,128)(2,1)} %get-tuple-element.45.in_ref, bf16[64,128]{1,0:T(8,128)(2,1)} %bitcast.42, ...), custom_call_target="tpu_custom_call" | custom-call | tf_op jit(solution)/shard_map/pallas_call | solution.py:349
  114.3 0.9 slice.40
  115.3 0.7 slice.34.g2_ref
  116.0 0.7 slice.32.g1_ref.g_ref
  116.7 0.3 fusion.2
  117.0 0.8 pad_maximum_fusion.2
  117.7 50.4 %shard_map.188 = (f32[128,2560]{1,0:T(8,128)}, bf16[4,128,2560]{2,1,0:T(8,128)(2,1)}, bf16[2560,1024]{1,0:T(8,128)(2,1)}, bf16[2,128,2560]{2,1,0:T(8,128)(2,1)},...) custom-call(f32[128,2560]{1,0:T(8,128)} %get-tuple-element.44.x_in, ...), custom_call_target="tpu_custom_call" | custom-call | tf_op jit(solution)/shard_map/pallas_call | solution.py:533
  168.2 0.0 all-gather.2.cloned.1.call-done.g_ref.w_ref
  168.2 28.6 %shard_map.189 = (bf16[512,1024]{1,0:T(8,128)(2,1)}, bf16[512,2048]{1,0:T(8,128)(2,1)}, bf16[2560,3072]{1,0:T(8,128)(2,1)}) custom-call(bf16[512,2560]{1,0:T(8,128)(2,1)} %bitcast.47, bf16[512,2560]{1,0:T(8,128)(2,1)} %bitcast.46, bf16[2560,2048]{1,0:T(8,128)(2,1)} %all-gather.2.cloned.1.call-done.g_ref.w_ref, bf16[2560,1024]{1,0:T(8,128)(2,1)} %get-tuple-element.56.d_ref), custom_call_target="tpu_custom_call" | custom-call | flops 16106127360 | bytes 39845888 | tf_op jit(solution)/shard_map/pallas_call | solution.py:1011
  196.9 0.0 reduce-scatter.2.cloned.1.call-update
  196.9 46.8 %shard_map.190 = (bf16[4,128,2560]{2,1,0:T(8,128)(2,1)}, f32[128,2560]{1,0:T(8,128)}, bf16[128,2560]{1,0:T(8,128)(2,1)}, bf16[128,1792]{1,0:T(8,128)(2,1)}, bf16...) custom-call(bf16[512,2048]{1,0:T(8,128)(2,1)} %get-tuple-element.57.dg_in, bf16[512,1024]{1,0:T(8,128)(2,1)} %get-tuple-element.58.h_in, ...), custom_call_target="tpu_custom_call" | custom-call | tf_op jit(solution)/shard_map/pallas_call | solution.py:1266
  243.7 96.8 %shard_map.191 = (f32[40,3072]{1,0:T(8,128)}, f32[16,128]{1,0:T(8,128)}, bf16[128,2560]{1,0:T(8,128)(2,1)}, bf16[128,2560]{1,0:T(8,128)(2,1)}) custom-call(bf16[256,2560]{1,0:T(8,128)(2,1)} %bitcast.36, bf16[128,1792]{1,0:T(8,128)(2,1)} %get-tuple-element.63.dq_ref, bf16[128,2560]{1,0:T(8,128)(2,1)} %get-tuple-element.64.dl_ref, bf16[256,1280]{1,0:T(8,128)(2,1)} %bitcast.38, ...), custom_call_target="tpu_custom_call" | custom-call | tf_op jit(solution)/shard_map/pallas_call | solution.py:879
  340.5 0.0 copy-start
  340.5 1.6 slice.37
  342.1 1.3 slice_bitcast_fusion.1
  343.4 1.8 slice_bitcast_fusion
  345.2 0.0 reduce-scatter.2.cloned.1.call-done.s_in
  345.2 14.6 %shard_map.192 = (f32[40,3840]{1,0:T(8,128)}, f32[40,3840]{1,0:T(8,128)}, f32[40,3840]{1,0:T(8,128)}) custom-call(bf16[160,3072]{1,0:T(8,128)(2,1)} %reduce-scatter.2.cloned.1.call-done.s_in), custom_call_target="tpu_custom_call" | custom-call | tf_op jit(solution)/shard_map/pallas_call | solution.py:585
  359.8 0.0 copy-start.3
  359.8 0.0 copy-start.2
  359.8 0.0 copy-start.1
  359.8 2.1 copy.38
  361.9 0.0 copy-done
  361.9 0.8 copy.39
  362.7 0.0 copy-done.3
  362.7 0.8 copy.40
  363.6 0.0 copy-done.2
  363.6 0.8 copy.41
  364.4 0.0 copy-done.1
  364.4 0.8 copy.42
  (6 shorter events, 0.1 us)
Async XLA Ops:
  7.2 2.9 copy-start.4
  7.2 3.4 copy-start.6
  7.2 3.4 copy-start.7
  7.2 161.0 %all-gather.2.cloned.1.call-start = ((), (), s32[]{:S(2)}) async-start(), calls=%async_computation.1 | async-start | bytes 11141120 | tf_op jit(solution)/shard_map/all_gather | solution.py:1346
  11.6 21.1 %copy-start.5 = (bf16[3840,40]{0,1:T(8,128)(2,1)S(1)}, bf16[3840,40]{0,1:T(8,128)(2,1)}, u32[]{:S(2)}) copy-start(bf16[3840,40]{0,1:T(8,128)(2,1)} %param.19) | copy-start | bytes 921604
  32.7 312.5 %reduce-scatter.2.cloned.1.call-start = ((), (), s32[]{:S(2)}) async-start(), calls=%async_computation.2 | async-start | bytes 16711680 | tf_op jit(solution)/shard_map/reduce_scatter | solution.py:1358
  340.5 21.4 %copy-start = (bf16[128,2560]{1,0:T(8,128)(2,1)S(1)}, bf16[128,2560]{1,0:T(8,128)(2,1)}, u32[]{:S(2)}) copy-start(bf16[128,2560]{1,0:T(8,128)(2,1)} %get-tuple-element.102) | copy-start | bytes 1966084
  359.8 3.0 copy-start.3
  359.8 3.8 %copy-start.2 = (f32[40,3840]{1,0:T(8,128)S(1)}, f32[40,3840]{1,0:T(8,128)}, u32[]{:S(2)}) copy-start(f32[40,3840]{1,0:T(8,128)} %get-tuple-element.109) | copy-start | bytes 1843204
  359.8 4.6 %copy-start.1 = (f32[40,3840]{1,0:T(8,128)S(1)}, f32[40,3840]{1,0:T(8,128)}, u32[]{:S(2)}) copy-start(f32[40,3840]{1,0:T(8,128)} %get-tuple-element.77) | copy-start | bytes 1843204
Sparse Core Ops, SparseCore 0:
  32.8 118.3 all-gather.1
  197.0 133.6 reduce-scatter.1

commit v5 on v4

--- a/solution.py
+++ b/solution.py
@@ -49,6 +49,10 @@
     return pltpu.make_async_remote_copy(
         src_ref=src, dst_ref=dst, send_sem=send, recv_sem=recv, device_id=peer, device_id_type=MESH
     )
+
+
+ATTN, FEED = 768, 512
+MAIN, PACKED = 896, 1920
 
 
 def fetch(pairs, sems):
@@ -107,61 +111,76 @@
 
 
 def exchange_kernel(
-    a_ref, g_ref, s_ref, tok_ref, cot_ref, order_ref,
-    ao_out, go_ref, so_out, x_out, dy_out,
-    al, sl, ao_ref, so_ref, x_ref, dy_ref, here, send, recv, out_sem
+    q_ref, kv_ref, wo_ref, g_ref, u_ref, d_ref, gain_ref, tok_ref, cot_ref, order_ref,
+    ao_out, go_ref, so_out, do_out, x_out, dy_out,
+    a_block, g_block, s_block, d_block, al, sl, ao_ref, so_ref, x_ref, dy_ref, here, send, recv, out_sem,
 ):
+    f32, low = jnp.float32, jnp.bfloat16
+
+    def stacked(v):
+        half = v.shape[1] // 2
+        return jnp.concatenate([v[:, :half], v[:, half:]], axis=0).astype(low)
+
+    attn = jnp.concatenate([r[...].astype(f32) for r in (q_ref, kv_ref, wo_ref)], axis=1)
+    for k in range(2):
+        block = stacked(attn[:, k * 2 * ATTN : (k + 1) * 2 * ATTN])
+        a_block[k] = block
+        a_block[2 + k] = block
+    gate, up, down = (r[...].astype(f32) for r in (g_ref, u_ref, d_ref))
+    for t in range(4):
+        first, tail, end = t * 960, t * 960 + MAIN, (t + 1) * 960
+        packed = [gate[:, first:tail], up[:, first:tail], gate[:, tail:end], up[:, tail:end]]
+        s_block[t] = stacked(jnp.concatenate([*packed, jnp.zeros((40, 128), f32)], axis=1))
+        d_block[t] = stacked(jnp.concatenate([down[:, first:end], jnp.zeros((40, 64), f32)], axis=1))
+        g_block[t] = gain_ref[...]
     greet(group_peers())
-    finish = send_blocks([a_ref, g_ref, s_ref], [al, go_ref, sl], here, send, recv)
+    finish = send_blocks([a_block, g_block, s_block], [al, go_ref, sl], here, send, recv)
+    early = fetch([(d_block, do_out)], out_sem.at[pl.ds(4, 1)])
     reorder(tok_ref, order_ref, x_ref, False)
     reorder(cot_ref, order_ref, dy_ref, False)
     puts = fetch([(x_ref, x_out), (dy_ref, dy_out)], out_sem)
     finish()
-    f32, low = jnp.float32, jnp.bfloat16
     for h in range(2):
         parts = [al[t].astype(f32)[h * 40 : (h + 1) * 40] for t in range(4)]
         ao_ref[h] = jnp.concatenate(parts, axis=0).astype(low)
     for k in range(2):
         parts = [sl[t].astype(f32) for t in (2 * k, 2 * k + 1)]
-        parts = [jnp.concatenate([v[:40], v[40:]], axis=1) for v in parts]
+        parts = [jnp.concatenate([v[:40], v[40:, : PACKED - 2 * FEED]], axis=1) for v in parts]
         so_ref[pl.ds(k * 80, 80)] = jnp.concatenate(parts, axis=0).astype(low)
     last = fetch([(ao_ref, ao_out), (so_ref, so_out)], out_sem.at[pl.ds(2, 2)])
-    for put in (*puts, *last):
+    for put in (*early, *puts, *last):
         put.wait()
 
 
-def group_exchange(attn, gains, second, tokens, cotangent, order, cid):
+def group_exchange(weights, gains, tokens, cotangent, order, cid):
     low, dma = jnp.bfloat16, pltpu.SemaphoreType.DMA
-    anywhere, vmem = pl.BlockSpec(memory_space=pl.ANY), pl.BlockSpec(memory_space=pltpu.VMEM)
+    vmem = pl.BlockSpec(memory_space=pltpu.VMEM)
     shapes = [
-            jax.ShapeDtypeStruct((2, 160, attn.shape[2]), low),
-            jax.ShapeDtypeStruct(gains.shape, low),
-            jax.ShapeDtypeStruct((160, 2 * second.shape[2]), low),
-            jax.ShapeDtypeStruct(tokens.shape, jnp.float32),
-            jax.ShapeDtypeStruct(cotangent.shape, low),
-        ]
+        jax.ShapeDtypeStruct((2, 160, ATTN), low),
+        jax.ShapeDtypeStruct((4, 16, 128), low),
+        jax.ShapeDtypeStruct((160, PACKED), low),
+        jax.ShapeDtypeStruct((4, 80, FEED), low),
+        jax.ShapeDtypeStruct(tokens.shape, jnp.float32),
+        jax.ShapeDtypeStruct(cotangent.shape, low),
+    ]
+    attn, second = (jax.ShapeDtypeStruct((4, 80, n), low) for n in (ATTN, 2 * FEED))
     return pl.pallas_call(
         exchange_kernel,
         out_shape=shapes,
-        in_specs=[anywhere] * 3 + [vmem] * 3,
-        out_specs=[HBM] * 5,
+        in_specs=[vmem] * 10,
+        out_specs=[HBM] * 6,
         scratch_shapes=[
-            pltpu.VMEM(attn.shape, low),
-            pltpu.VMEM(second.shape, low),
-            *buffers(shapes[0], *shapes[2:]),
+            *buffers(attn, shapes[1], second, shapes[3], attn, second),
+            *buffers(shapes[0], shapes[2], *shapes[4:]),
             dma((3,)),
             dma((9,)),
             dma((9,)),
-            dma((4,)),
+            dma((5,)),
         ],
         compiler_params=pltpu.CompilerParams(
-            collective_id=cid, has_side_effects=True, vmem_limit_bytes=60 * 2**20
+            collective_id=cid, has_side_effects=True, vmem_limit_bytes=54 * 2**20
         ),
-    )(attn, gains, second, tokens, cotangent, order)
-
-
-ATTN, FEED = 768, 512
-WIDE = ATTN + FEED
+    )(*weights, gains, tokens, cotangent, order)
 
 
 def shift(i, by):
@@ -211,7 +230,7 @@
         for n, p, i1, _, i2, (back2, ahead2) in each:
             go(p.own(), p.at(i1, i2), n, 1, 0, ahead2)
             go(p.own(), p.at(i1, i2), n, 1, 1, back2)
-            cross(n, p.own(), p.at(i1, i2))
+            cross(n, p.own(), p.at(i1, i2), None)
 
     def first_axis():
         for n, p, i1, (back1, ahead1), i2, (back2, ahead2) in each:
@@ -225,7 +244,7 @@
             for ring, ref in ((2, left), (3, right)):
                 go(ref, ref, n, ring, 0, ahead2)
                 go(ref, ref, n, ring, 1, back2)
-                cross(n, ref, ref)
+                cross(n, ref, ref, (shift(i1, 3 if ring == 2 else 1), i2))
         for n, p, i1, _, i2, (back2, ahead2) in each:
             far = shift(i1, 2)
             arrived(p.at(far, i2, 0), n, 0, 2)
@@ -233,7 +252,7 @@
             ref = p.at(far, i2)
             go(ref, ref, n, 4, 0, ahead2)
             go(ref, ref, n, 4, 1, back2)
-            cross(n, ref, ref)
+            cross(n, ref, ref, (far, i2))
 
     def second_axis():
         for ring, by in firsts:
@@ -243,11 +262,11 @@
                 arrived(left, n, ring, 0)
                 low = p.at(j, shift(i2, 3), 0)
                 go(low, low, n, ring, 2, ahead2)
-                cross(n, left, left)
+                cross(n, left, left, (j, shift(i2, 3)))
                 arrived(right, n, ring, 1)
                 high = p.at(j, shift(i2, 1), 1)
                 go(high, high, n, ring, 3, back2)
-                cross(n, right, right)
+                cross(n, right, right, (j, shift(i2, 1)))
 
     def last():
         for ring, by in firsts:
@@ -255,59 +274,84 @@
                 j, far = shift(i1, by), shift(i2, 2)
                 arrived(p.at(j, far, 0), n, ring, 2)
                 arrived(p.at(j, far, 1), n, ring, 3)
-                cross(n, p.at(j, far), p.at(j, far))
+                cross(n, p.at(j, far), p.at(j, far), (j, far))
+
+    def finish():
         for copy in started:
             copy.wait_send()
 
-    return own_blocks, first_axis, second_axis, last
+    return own_blocks, first_axis, second_axis, last, finish
 
 
 def attention_gather_kernel(
-    in_ref, g_ref, dy_ref, d_ref, a_ref, o_ref, go_ref, all_ref, do_out,
-    dl, do_ref, do_sem, here, send, recv, csend, crecv, dsend, drecv, xhere, xsend, xrecv,
+    in_hbm, g_hbm, dy_hbm, d_hbm, a_ref, o_ref, go_ref, all_ref, do_out,
+    in_ref, g_ref, dy_ref, d_ref, in_sem, dl, do_ref, do_sem, here, send, recv, csend, crecv, zsend, zrecv, dsend, drecv, xhere, xsend, xrecv,
 ):
     y, x, c = lax.axis_index("y"), lax.axis_index("x"), lax.axis_index("c")
     zl, zh = lax.axis_index("zl"), lax.axis_index("zh")
     core = {"c": 1 - c}
+    gets = fetch([(in_hbm, in_ref), (g_hbm, g_ref), (dy_hbm, dy_ref), (d_hbm, d_ref)], in_sem)
     chips = [{"zl": 1 - zl, "zh": k} for k in range(2)]
     greet([*ring_of("x", x), *ring_of("y", y), core, *chips, {"zl": 1 - zl, "c": 1 - c}])
     whole = pl.ds(0, 160)
-
+    for get in gets:
+        get.wait()
+
+    chip = {"zl": 1 - zl}
     for side in range(2):
 
         @pl.when(c == side)
         def _(side=side):
-            sources = [
-                in_ref.at[0, whole, pl.ds(0, 256)],
-                in_ref.at[0, whole, pl.ds(256, 512)],
-                in_ref.at[1, whole, pl.ds(0, 768)],
-                g_ref,
-            ]
             if side == 0:
-                targets = [(a_ref, 0, 256), (a_ref, 256, 512), (a_ref, 768, 768)]
+                starts = [(a_ref, 0), (a_ref, 256), (a_ref, 512), (a_ref, 768), (a_ref, 1280)]
             else:
-                targets = [(a_ref, 1536, 256), (o_ref, 0, 512), (o_ref, 512, 768)]
-            targets.append((go_ref, 0, 128))
-            pieces = [
-                Piece(h, source, ref, pl.ds(first, width), rows)
-                for h, source, (ref, first, width), rows in zip((0, 0, 1, 0), sources, targets, (160, 160, 160, 64))
-            ]
-            crossed = []
-
-            def cross(n, src, dst):
-                if n < 3:
-                    k = len(crossed)
-                    copy = remote(src, dst, csend.at[k], crecv.at[k], core)
+                starts = [(a_ref, 1536), (o_ref, 0), (o_ref, 256), (o_ref, 512), (o_ref, 1024)]
+            segments = ((0, 0, 256, False), (0, 256, 256, False), (0, 512, 128, True), (1, 0, 512, False), (1, 512, 128, True))
+            pieces, others = [], {}
+            for n, ((h, source, width, shared), (ref, first)) in enumerate(zip(segments, starts)):
+                for part in range(2 if shared else 1):
+                    off = pl.multiple_of((zl if part == 0 else 1 - zl) * width, 128) if shared else 0
+                    piece = Piece(
+                        h, in_ref.at[h, whole, pl.ds(source + off, width)], ref, pl.ds(first + off, width)
+                    )
+                    if part == 0:
+                        pieces.append(piece)
+                    else:
+                        others[n] = piece
+            pieces.append(Piece(0, g_ref, go_ref, pl.ds(0, 128), 64))
+            crossed, passed_on, drained = [], [], []
+
+            def to_core(src, dst):
+                k = len(crossed)
+                copy = remote(src, dst, csend.at[k], crecv.at[k], core)
+                copy.start()
+                crossed.append(copy)
+
+            def cross(n, src, dst, place):
+                if n < 5:
+                    to_core(src, dst)
+                if n in others and place is not None:
+                    k = len(passed_on)
+                    copy = remote(dst, dst, zsend.at[k], zrecv.at[k], chip)
                     copy.start()
-                    crossed.append(copy)
-
-            own_blocks, first_axis, second_axis, last = gather_steps(y, x, pieces, send, recv, cross)
+                    passed_on.append((copy, others[n].at(*place)))
+
+            def drain(count):
+                for k in range(len(drained), count):
+                    ref = passed_on[k][1]
+                    remote(ref, ref, zsend.at[k], zrecv.at[k], chip).wait_recv()
+                    to_core(ref, ref)
+                    drained.append(k)
+
+            own_blocks, first_axis, second_axis, last, sent = gather_steps(y, x, pieces, send, recv, cross)
             own_blocks()
             keeps = []
-            for n, p in enumerate(pieces):
+            for n, p in enumerate([*pieces, *others.values()]):
                 i1, _, i2, _ = around(p.h, y, x)
                 keeps.append(pltpu.make_async_copy(p.own(), p.at(i1, i2), here.at[n]))
                 keeps[-1].start()
+                if n >= len(pieces):
+                    to_core(p.own(), p.at(i1, i2))
             finish = send_blocks([d_ref], [dl], xhere, xsend, xrecv)
             half = dy_ref.shape[0] // 2
             mine, other = zl * 2 + c, (1 - zl) * 2 + c
@@ -319,7 +363,7 @@
             across = remote(dy_ref, all_ref.at[mine], dsend.at[2], drecv.at[2], core)
             for copy in (*away, across):
                 copy.start()
-            keeps.append(pltpu.make_async_copy(dy_ref, all_ref.at[mine], here.at[4]))
+            keeps.append(pltpu.make_async_copy(dy_ref, all_ref.at[mine], here.at[8]))
             keeps[-1].start()
             first_axis()
             finish()
@@ -328,6 +372,7 @@
                 do_ref[h] = jnp.concatenate(parts, axis=0).astype(jnp.bfloat16)
             puts = fetch([(do_ref, do_out)], do_sem)
             second_axis()
+            drain(6)
             passed = []
             for k in range(2):
                 rows = pl.ds(k * half, half)
@@ -336,6 +381,10 @@
                 passed.append(remote(there, there, dsend.at[3 + k], drecv.at[3 + k], core))
                 passed[-1].start()
             last()
+            drain(30)
+            sent()
+            for copy, _ in passed_on:
+                copy.wait_send()
             for copy in (*crossed, *passed, across):
                 copy.wait()
             for copy in away:
@@ -358,14 +407,18 @@
         in_specs=[HBM] * 4,
         out_specs=[HBM] * 5,
         scratch_shapes=[
+            *buffers(own, gains, dy, down),
+            dma((4,)),
             pltpu.VMEM(down.shape, kind),
             pltpu.VMEM((2, 160, down.shape[2]), kind),
             dma((1,)),
-            dma((5,)),
-            dma((80,)),
-            dma((80,)),
-            dma((48,)),
-            dma((48,)),
+            dma((9,)),
+            dma((120,)),
+            dma((120,)),
+            dma((112,)),
+            dma((112,)),
+            dma((30,)),
+            dma((30,)),
             dma((5,)),
             dma((5,)),
             dma((1,)),
@@ -377,9 +430,9 @@
 
 
 def middle_kernel(
-    x_in, g1_ref, g2_ref, cos_ref, sin_ref, wq_ref, wo_ref, d_ref,
-    mid_out, all_out, w_ref, xn_out, mixed_out, q_out, kv_out, soft_out,
-    x_ref, mid_ref, all_ref, xn_ref, mixed_ref, q_ref, kv_ref, soft_ref, in_sem, out_sem,
+    x_in, g_in, cos_ref, sin_ref, wq_ref, wo_ref, d_in,
+    mid_out, all_out, w_ref, xn_out, mixed_out, q_out, kv_out, soft_out, rows_out,
+    x_ref, g_ref, d_ref, mid_ref, all_ref, xn_ref, mixed_ref, q_ref, kv_ref, soft_ref, rows_ref, in_sem, out_sem,
     wq, wo, p_ref, landed, here, wsem, psend, precv, gsend, grecv, send, recv, csend, crecv,
 ):
     y, x, c = lax.axis_index("y"), lax.axis_index("x"), lax.axis_index("c")
@@ -388,7 +441,7 @@
     chips = [{"zl": 1 - zl, "zh": k} for k in range(2)]
     f32, low = jnp.float32, jnp.bfloat16
     heads = soft_ref.shape[0]
-    get_x = fetch([(x_in, x_ref)], in_sem)[0]
+    *gets, get_d = fetch([(x_in, x_ref), (g_in, g_ref), (d_in, d_ref)], in_sem)
     loads = []
     for k in range(heads + 2):
         columns = pl.ds(k * HEAD_DIM, HEAD_DIM)
@@ -402,9 +455,10 @@
     pieces = [
         Piece(h, d_ref.at[h, pl.ds(0, 160)], w_ref, pl.ds(h * FEED, FEED)) for h in range(2)
     ]
-    own_blocks, first_axis, second_axis, last = gather_steps(
-        y, x, pieces, send, recv, lambda n, src, dst: None
+    own_blocks, first_axis, second_axis, last, sent = gather_steps(
+        y, x, pieces, send, recv, lambda n, src, dst, place: None
     )
+    get_d.wait()
     own_blocks()
     keeps = []
     for n, p in enumerate(pieces):
@@ -412,14 +466,17 @@
         keeps.append(pltpu.make_async_copy(p.own(), p.at(i1, i2), here.at[n]))
         keeps[-1].start()
     half, step = x_ref.shape[0] // 2, 16
-    get_x.wait()
+    for get in gets:
+        get.wait()
+    tiles = [g_ref[k * 16 : (k + 1) * 16].astype(f32)[:8, :40] for k in range(64)]
+    rows_ref[...] = jnp.concatenate(tiles, axis=1)
 
     @pl.loop(0, 2 * half // step)
     def _(i):
         at = pl.ds(pl.multiple_of(i * step, step), step)
         v = x_ref[at]
         r = lax.rsqrt(jnp.mean(v * v, axis=-1, keepdims=True) + norm_eps)
-        xn_ref[c, at] = (v * r * g1_ref[...]).astype(low)
+        xn_ref[c, at] = (v * r * rows_ref[0:1]).astype(low)
 
     shared = [remote(xn_ref.at[c], xn_ref.at[c], csend.at[0], crecv.at[0], core)]
     shared[0].start()
@@ -455,7 +512,7 @@
         ).astype(low)
     shared.append(remote(mixed_ref.at[c], mixed_ref.at[c], csend.at[1], crecv.at[1], core))
     shared[1].start()
-    puts = fetch([(q_ref, q_out), (kv_ref, kv_out), (soft_ref, soft_out)], out_sem)
+    puts = fetch([(q_ref, q_out), (kv_ref, kv_out), (soft_ref, soft_out), (rows_ref, rows_out)], out_sem)
     for k in range(5):
         loads[heads + 2 + k].wait()
         some = pl.ds(k * 512, 512)
@@ -484,7 +541,7 @@
             v = x_ref[at] + branch
             mid_ref[at] = v
             r = lax.rsqrt(jnp.mean(v * v, axis=-1, keepdims=True) + norm_eps)
-            all_ref[mine, at] = (v * r * g2_ref[...]).astype(low)
+            all_ref[mine, at] = (v * r * rows_ref[1:2]).astype(low)
 
         ready = all_ref.at[mine, part]
         if k == 0:
@@ -502,11 +559,12 @@
         passed.append(remote(there, there, gsend.at[4 + k], grecv.at[4 + k], core))
         passed[-1].start()
     last()
+    sent()
     for copy in (*across, *passed, *shared):
         copy.wait()
     puts += fetch(
         [(mid_ref, mid_out), (all_ref, all_out), (xn_ref, xn_out), (mixed_ref, mixed_out)],
-        out_sem.at[pl.ds(3, 4)],
+        out_sem.at[pl.ds(4, 4)],
     )
     for copy in (*away, *pair):
         copy.wait_send()
@@ -514,7 +572,7 @@
         keep.wait()
 
 
-def middle(x, gain_one, gain_two, cosine, sine, w_q_kv, w_out_t, down, cid):
+def middle(x, gains, cosine, sine, w_q_kv, w_out_t, down, cid):
     dma, f32, low = pltpu.SemaphoreType.DMA, jnp.float32, jnp.bfloat16
     vmem = pl.BlockSpec(memory_space=pltpu.VMEM)
     rows, width = x.shape
@@ -529,16 +587,17 @@
         jax.ShapeDtypeStruct((rows, wide), low),
         jax.ShapeDtypeStruct((rows, 2 * HEAD_DIM), low),
         jax.ShapeDtypeStruct((heads, rows, rows), f32),
+        jax.ShapeDtypeStruct((8, width), f32),
     ]
     return pl.pallas_call(
         middle_kernel,
         out_shape=shapes,
-        in_specs=[HBM] + [vmem] * 4 + [HBM] * 3,
-        out_specs=[HBM] * 8,
+        in_specs=[HBM] * 2 + [vmem] * 2 + [HBM] * 3,
+        out_specs=[HBM] * 9,
         scratch_shapes=[
-            *buffers(x, *shapes[:2], *shapes[3:]),
-            dma((1,)),
-            dma((7,)),
+            *buffers(x, gains, down, *shapes[:2], *shapes[3:]),
+            dma((3,)),
+            dma((8,)),
             pltpu.VMEM(w_q_kv.shape, low),
             pltpu.VMEM(w_out_t.shape, low),
             pltpu.VMEM(x.shape, low),
@@ -557,41 +616,76 @@
         compiler_params=pltpu.CompilerParams(
             collective_id=cid, has_side_effects=True, vmem_limit_bytes=60 * 2**20
         ),
-    )(x, gain_one, gain_two, cosine, sine, w_q_kv, w_out_t, down)
-
-
-def finish_kernel(s_in, down_ref, gate_ref, up_ref, s_ref, in_sem, blocks, landed, here, send, recv):
+    )(x, gains, cosine, sine, w_q_kv, w_out_t, down)
+
+
+def finish_kernel(s_in, o_ref, s_ref, in_sem, blocks, here, send, recv):
     get = fetch([(s_in, s_ref)], in_sem)[0]
     greet(group_peers())
     get.wait()
-    wide = s_ref.shape[1] // 2
+    wide = blocks.shape[2]
     for t in range(4):
         first = t * 40 // 16 * 16
         size = (t * 40 + 40 + 15) // 16 * 16 - first
         v = s_ref[pl.ds(first, size)].astype(jnp.float32)[t * 40 - first : t * 40 - first + 40]
-        blocks[t] = jnp.concatenate([v[:, :wide], v[:, wide:]], axis=0).astype(jnp.bfloat16)
-    send_blocks([blocks], [landed], here, send, recv)()
-    for t in range(4):
-        v = landed[t].astype(jnp.float32)
-        v = jnp.concatenate([v[:40], v[40:]], axis=1)
-        for k, out in enumerate((down_ref, gate_ref, up_ref)):
-            out[:, t * 960 : (t + 1) * 960] = v[:, k * 2 * FEED : k * 2 * FEED + 960]
+        rest = jnp.concatenate([v[:, wide:], jnp.zeros((40, 2 * wide - v.shape[1]), jnp.float32)], axis=1)
+        blocks[t] = jnp.concatenate([v[:, :wide], rest], axis=0).astype(jnp.bfloat16)
+    send_blocks([blocks], [o_ref], here, send, recv)()
 
 
 def finish(sent, cid):
     dma = pltpu.SemaphoreType.DMA
-    vmem = pl.BlockSpec(memory_space=pltpu.VMEM)
-    buffer = pltpu.VMEM((4, 80, sent.shape[1] // 2), sent.dtype)
+    buffer = jax.ShapeDtypeStruct((4, 80, 3 * FEED), sent.dtype)
     return pl.pallas_call(
         finish_kernel,
-        out_shape=[jax.ShapeDtypeStruct((40, 3840), jnp.float32)] * 3,
+        out_shape=buffer,
         in_specs=[HBM],
-        out_specs=[vmem] * 3,
-        scratch_shapes=[*buffers(sent), dma((1,)), buffer, buffer, dma((1,)), dma((3,)), dma((3,))],
+        out_specs=HBM,
+        scratch_shapes=[*buffers(sent), dma((1,)), *buffers(buffer), dma((1,)), dma((3,)), dma((3,))],
         compiler_params=pltpu.CompilerParams(
             collective_id=cid, has_side_effects=True, vmem_limit_bytes=60 * 2**20
         ),
     )(sent)
+
+
+def write_kernel(
+    l_in, block_in, grad_in, q_in, kv_in, o_in, g_in,
+    block, grad, q, kv, o, g, down_ref, gate_ref, up_ref,
+    landed, b1, b2, b3, b4, b5, b6, sem, load_sem,
+):
+    held = (b1, b2, b3, b4, b5, b6)
+    get, *gets = fetch(list(zip((l_in, block_in, grad_in, q_in, kv_in, o_in, g_in), (landed, *held))), load_sem)
+    for one in gets:
+        one.wait()
+    copies = fetch(list(zip(held, (block, grad, q, kv, o, g))), sem)
+    get.wait()
+    for t in range(4):
+        v = landed[t].astype(jnp.float32)
+        v = jnp.concatenate([v[:40], v[40:]], axis=1)
+        first, tail = t * 960, t * 960 + MAIN
+        gate_ref[:, first:tail] = v[:, :MAIN]
+        gate_ref[:, tail : tail + 64] = v[:, 2 * MAIN : 2 * MAIN + 64]
+        up_ref[:, first:tail] = v[:, MAIN : 2 * MAIN]
+        up_ref[:, tail : tail + 64] = v[:, 2 * MAIN + 64 : PACKED]
+        down_ref[:, first : first + 960] = v[:, PACKED : PACKED + 960]
+    for copy in copies:
+        copy.wait()
+
+
+def written(landed, arrays):
+    dma = pltpu.SemaphoreType.DMA
+    vmem = pl.BlockSpec(memory_space=pltpu.VMEM)
+    return pl.pallas_call(
+        write_kernel,
+        out_shape=[
+            *(jax.ShapeDtypeStruct(a.shape, a.dtype) for a in arrays),
+            *[jax.ShapeDtypeStruct((40, 3840), jnp.float32)] * 3,
+        ],
+        in_specs=[HBM] * 7,
+        out_specs=[HBM] * 6 + [vmem] * 3,
+        scratch_shapes=[*buffers(landed, *arrays), dma((6,)), dma((7,))],
+        compiler_params=pltpu.CompilerParams(vmem_limit_bytes=56 * 2**20),
+    )(landed, *arrays)
 
 
 class SumPiece:
@@ -618,9 +712,9 @@
 
 
 def plane_sum_kernel(
-    left_in, dq_ref, dl_ref, right_in, gi_ref, p_in, t_in, x_in, mid_in, dmid_in, g_ref, order_in,
-    attn_ref, go_ref, block_ref, grad_ref,
-    left, right_o, p_ref, t_ref, x_ref, mid_ref, dmid_ref, order_ref, in_sem,
+    left_in, dq_ref, dl_ref, right_in, gi_ref, p_in, t_in, x_in, mid_in, dmid_in, g_in, order_in,
+    q_out, kv_out, wo_out, go_ref, block_ref, grad_ref,
+    left, right_o, p_ref, t_ref, x_ref, mid_ref, dmid_ref, g_ref, order_ref, attn_ref, in_sem,
     right, left_o, sums, via, main, gsums, gvia, gmain, from_chip, attn_low, gfar, gsum, gall,
     t_core, t_other, t_chips, t_own, t_far, landed, block_low, grad_low,
     here, csend, crecv, send, recv, esend, erecv, tsend, trecv, shere, ssend, srecv,
@@ -631,7 +725,7 @@
     get_p, get_t, get_left, get_right, *gets = fetch(
         [
             (p_in, p_ref), (t_in, t_ref), (left_in, left), (right_in, right_o), (x_in, x_ref),
-            (mid_in, mid_ref), (dmid_in, dmid_ref), (order_in, order_ref),
+            (mid_in, mid_ref), (dmid_in, dmid_ref), (g_in, g_ref), (order_in, order_ref),
         ],
         in_sem,
     )
@@ -709,7 +803,7 @@
         @pl.loop(0, tokens // step)
         def _(i):
             at = pl.ds(pl.multiple_of(i * step, step), step)
-            d = (t_ref[at].astype(f32) + landed[at].astype(f32)) * g_ref[...]
+            d = (t_ref[at].astype(f32) + landed[at].astype(f32)) * g_ref[0:1]
             v = x_ref[at]
             r = lax.rsqrt(jnp.mean(v * v, axis=-1, keepdims=True) + norm_eps)
             n = v * r
@@ -868,27 +962,32 @@
     )
     last.wait()
     keep.wait()
+    first = 0
+    for out in (q_out, kv_out, wo_out):
+        out[...] = attn_ref[:, first : first + out.shape[1]]
+        first += out.shape[1]
     for copy in (*started, *shared, pair, *t_cores, *t_sent):
         copy.wait_send()
 
 
-def plane_sum(xn, d_q_kv, d_low, mixed, gains, down, d_xn, x, mid, d_mid, gain, order, cid):
+def plane_sum(xn, d_q_kv, d_low, mixed, gains, down, d_xn, x, mid, d_mid, gains_row, order, cid):
     low, dma, f32 = jnp.bfloat16, pltpu.SemaphoreType.DMA, jnp.float32
     rows, width = x.shape
     vmem = pl.BlockSpec(memory_space=pltpu.VMEM)
     return pl.pallas_call(
         plane_sum_kernel,
         out_shape=[
-            jax.ShapeDtypeStruct((40, 4 * ATTN), f32),
+            *(jax.ShapeDtypeStruct((40, n), f32) for n in (1280, 512, 1280)),
             jax.ShapeDtypeStruct((16, 128), f32),
             jax.ShapeDtypeStruct(x.shape, low),
             jax.ShapeDtypeStruct(x.shape, low),
         ],
-        in_specs=[HBM] * 10 + [vmem, HBM],
-        out_specs=[vmem] * 4,
+        in_specs=[HBM] * 12,
+        out_specs=[vmem] * 6,
         scratch_shapes=[
-            *buffers(xn, mixed, down, d_xn, x, mid, d_mid, order),
-            dma((8,)),
+            *buffers(xn, mixed, down, d_xn, x, mid, d_mid, gains_row, order),
+            pltpu.VMEM((40, 4 * ATTN), f32),
+            dma((9,)),
             pltpu.VMEM((2 * rows, d_q_kv.shape[1]), low),
             pltpu.VMEM((2 * rows, width), low),
             pltpu.VMEM((2560, 2 * ATTN), low),
@@ -926,7 +1025,7 @@
         compiler_params=pltpu.CompilerParams(
             collective_id=cid, has_side_effects=True, vmem_limit_bytes=60 * 2**20
         ),
-    )(xn, d_q_kv, d_low, mixed, gains, down, d_xn, x, mid, d_mid, gain, order)
+    )(xn, d_q_kv, d_low, mixed, gains, down, d_xn, x, mid, d_mid, gains_row, order)
 
 
 GELU_IN, GELU_CUBE = math.sqrt(2.0 / math.pi), 0.044715
@@ -937,7 +1036,8 @@
     xn_ref, h_ref, dg_ref, in_sem, h_sem, dy, wg, wd, dy_turned, xn_turned, back, out, load_sem, out_sem,
 ):
     f32, low = jnp.float32, jnp.bfloat16
-    units, tile, lines = h_ref.shape[1], 256, out.shape[1]
+    units, lines = h_ref.shape[1], out.shape[1]
+    lanes = lax.broadcasted_iota(jnp.int32, (1, 128), 1)
     get_xn = fetch([(xn_in, xn_ref)], in_sem)[0]
     get_dy = pltpu.make_async_copy(dy_ref, dy, load_sem.at[0])
     get_dy.start()
@@ -953,25 +1053,32 @@
     dy_turned[...] = dy[...].T
     for n in range(4):
         loads[n].wait()
-    for k in range(units // tile):
-        at = pl.ds(k * tile, tile)
+    for k in range(units // 256):
+        at = pl.ds(k * 256, 256)
         back[:, at] = jnp.dot(dy[...], wd[:, at], preferred_element_type=f32)
     for n in range(4, 8):
         loads[n].wait()
-    for k in range(units // tile):
-        at, beside = pl.ds(k * tile, tile), pl.ds(units + k * tile, tile)
-        gate = jnp.dot(xn_ref[...], wg[:, at], preferred_element_type=f32)
-        up = jnp.dot(xn_ref[...], wg[:, beside], preferred_element_type=f32)
-        d = back[:, at]
+    def act(gate, up, d):
         square = gate * gate
         t = jnp.tanh(GELU_IN * (gate + GELU_CUBE * gate * square))
         cdf = 0.5 * (1.0 + t)
         slope = cdf + 0.5 * gate * (1.0 - t * t) * (GELU_IN * (1.0 + 3.0 * GELU_CUBE * square))
         gelu = gate * cdf
-        h_ref[:, at] = (gelu * up).astype(low)
-        dg_ref[:, at] = (d * up * slope).astype(low)
-        dg_ref[:, beside] = (d * gelu).astype(low)
-
+        return gelu * up, d * up * slope, d * gelu
+
+    for first, size in ((0, 256), (256, 256), (512, 256), (768, 128)):
+        at, beside = pl.ds(first, size), pl.ds(MAIN + first, size)
+        gate = jnp.dot(xn_ref[...], wg[:, at], preferred_element_type=f32)
+        up = jnp.dot(xn_ref[...], wg[:, beside], preferred_element_type=f32)
+        hidden, d_gate, d_up = act(gate, up, back[:, at])
+        h_ref[:, at] = hidden.astype(low)
+        dg_ref[:, at] = d_gate.astype(low)
+        dg_ref[:, beside] = d_up.astype(low)
+    at, both = pl.ds(MAIN, 128), pl.ds(2 * MAIN, 128)
+    gate = jnp.dot(xn_ref[...], wg[:, both], preferred_element_type=f32)
+    hidden, d_gate, d_up = act(gate, pltpu.roll(gate, 64, 1), back[:, at])
+    h_ref[:, at] = jnp.where(lanes < 64, hidden, 0.0).astype(low)
+    dg_ref[:, both] = jnp.where(lanes < 64, d_gate, pltpu.roll(d_up, 64, 1)).astype(low)
     puts = fetch([(h_ref, h_out), (dg_ref, dg_out)], h_sem)
 
     def put(i):
@@ -986,11 +1093,12 @@
         slot = lax.rem(i, 2)
         pl.when(i >= 2)(lambda: put(i - 2).wait())
         rows = pl.ds(pl.multiple_of(i * lines, lines), lines)
-        for left, right, count, first in ((dy_turned, h_ref, 2, 0), (xn_turned, dg_ref, 4, units)):
-            for k in range(count):
-                out[slot, :, pl.ds(first + k * 512, 512)] = jnp.dot(
-                    left[rows], right[:, pl.ds(k * 512, 512)], preferred_element_type=f32
-                ).astype(low)
+        for left, right, first, total in ((xn_turned, dg_ref, 0, PACKED), (dy_turned, h_ref, PACKED, 960)):
+            for k in range(0, total, 512):
+                size = min(512, right.shape[1] - k)
+                kept = min(size, total - k)
+                v = jnp.dot(left[rows], right[:, pl.ds(k, size)], preferred_element_type=f32)
+                out[slot, :, pl.ds(first + k, kept)] = v[:, :kept].astype(low)
         put(i).start()
 
     put(steps - 2).wait()
@@ -1005,8 +1113,8 @@
     low, dma = jnp.bfloat16, pltpu.SemaphoreType.DMA
     shapes = [
         jax.ShapeDtypeStruct((depth, units), low),
-        jax.ShapeDtypeStruct((depth, 2 * units), low),
-        jax.ShapeDtypeStruct((width, 3 * units), low),
+        jax.ShapeDtypeStruct((depth, PACKED), low),
+        jax.ShapeDtypeStruct((width, PACKED + 960), low),
     ]
     return pl.pallas_call(
         feed_kernel,
@@ -1018,12 +1126,12 @@
             dma((1,)),
             dma((2,)),
             pltpu.VMEM((depth, width), low),
-            pltpu.VMEM((width, 2 * units), low),
+            pltpu.VMEM((width, PACKED), low),
             pltpu.VMEM((width, units), low),
             pltpu.VMEM((width, depth), low),
             pltpu.VMEM((width, depth), low),
             pltpu.VMEM((depth, units), jnp.float32),
-            pltpu.VMEM((2, 320, 3 * units), low),
+            pltpu.VMEM((2, 640, PACKED + 960), low),
             dma((9,)),
             dma((2,)),
         ],
@@ -1038,9 +1146,9 @@
 
 def back_kernel(
     dg_in, h_in, w_ref, d_ref, wo_ref, wq_ref,
-    x_in, mid_in, dy_in, g2_ref, soft_in, q_in, kv_in, cos_ref, sin_ref,
+    x_in, mid_in, dy_in, g_in, soft_in, q_in, kv_in, cos_ref, sin_ref,
     down_out, dmid_out, dl_out, dq_out, dx_out, gains_out,
-    dg_ref, h_ref, x_ref, mid_ref, dy_ref, soft_ref, q_ref, kv_ref,
+    dg_ref, h_ref, x_ref, mid_ref, dy_ref, g_ref, soft_ref, q_ref, kv_ref,
     down_ref, dmid_ref, dl_ref, dq_ref, dx_ref, gains_ref, in_sem, out_sem,
     w, wd, wo, part, from_core, other, from_chips, own, from_far, grad, kv_part, kv_far, halved, sums,
     wsem, send, recv, osem, qsem, fsend, frecv,
@@ -1056,7 +1164,7 @@
     get_dg, get_h, *gets = fetch(
         [
             (dg_in, dg_ref), (h_in, h_ref), (x_in, x_ref), (mid_in, mid_ref), (dy_in, dy_ref),
-            (soft_in, soft_ref), (q_in, q_ref), (kv_in, kv_ref),
+            (g_in, g_ref), (soft_in, soft_ref), (q_in, q_ref), (kv_in, kv_ref),
         ],
         in_sem,
     )
@@ -1181,7 +1289,7 @@
         r = lax.rsqrt(jnp.mean(v * v, axis=-1, keepdims=True) + norm_eps)
         n = v * r
         sums[1:2] += jnp.sum(d * n, axis=0, keepdims=True) * 0.5
-        d = d * g2_ref[...]
+        d = d * g_ref[1:2]
         d = dy_ref[at].astype(f32) + r * (d - n * jnp.mean(d * n, axis=-1, keepdims=True))
         dmid_ref[at] = d
         dl_ref[at] = d.astype(low)
@@ -1249,7 +1357,7 @@
 
 def feed_back(
     d_gate_up, hidden, w_gate_up, w_down, w_out, w_q_kv,
-    x, mid, dy, gain, soft, queries, keys_values, cosine, sine, cid,
+    x, mid, dy, gains, soft, queries, keys_values, cosine, sine, cid,
 ):
     dma, low, f32 = pltpu.SemaphoreType.DMA, jnp.bfloat16, jnp.float32
     vmem = pl.BlockSpec(memory_space=pltpu.VMEM)
@@ -1266,11 +1374,11 @@
     return pl.pallas_call(
         back_kernel,
         out_shape=shapes,
-        in_specs=[HBM] * 9 + [vmem] + [HBM] * 3 + [vmem] * 2,
+        in_specs=[HBM] * 13 + [vmem] * 2,
         out_specs=[HBM] * 6,
         scratch_shapes=[
-            *buffers(d_gate_up, hidden, x, mid, dy, soft, queries, keys_values, *shapes),
-            dma((8,)),
+            *buffers(d_gate_up, hidden, x, mid, dy, gains, soft, queries, keys_values, *shapes),
+            dma((9,)),
             dma((6,)),
             pltpu.VMEM(w_gate_up.shape, low),
             pltpu.VMEM(w_down.shape, low),
@@ -1299,19 +1407,16 @@
         ),
     )(
         d_gate_up, hidden, w_gate_up, w_down, w_out, w_q_kv,
-        x, mid, dy, gain, soft, queries, keys_values, cosine, sine,
+        x, mid, dy, gains, soft, queries, keys_values, cosine, sine,
     )
 
 
 def tables():
-    half_rot = ROT // 2
-    rates = jnp.exp(jnp.arange(half_rot, dtype=jnp.float32) * (-2.0 * math.log(10000.0) / ROT))
-    angles = jnp.arange(SEQ_LEN, dtype=jnp.float32)[:, None] * rates[None, :]
-    return (jnp.cos(angles), jnp.sin(angles))
-
-
-def padded(weight):
-    return jnp.pad(weight.reshape(40, 4, 960), ((0, 0), (0, 0), (0, 64)))
+    half = ROT // 2
+    rates = np.exp(np.arange(half, dtype=np.float32) * np.float32(-2.0 * math.log(10000.0) / ROT))
+    angles = np.arange(SEQ_LEN, dtype=np.float32)[:, None] * rates[None, :]
+    cosine, sine = np.cos(angles), np.sin(angles)
+    return np.concatenate([cosine, cosine], axis=1), np.concatenate([-sine, sine], axis=1)
 
 
 def local(
@@ -1328,30 +1433,18 @@
 ):
     low = jnp.bfloat16
     rows = tokens.shape[0]
-    wide = query_weight.shape[1]
-    cosine, sine = tables()
-    attn = jnp.concatenate([query_weight, kv_weight, out_weight.T], axis=1)
-    attn = attn.reshape(40, 2, 2, ATTN).transpose(1, 2, 0, 3)
-    attn = jnp.broadcast_to(attn, (2, *attn.shape)).reshape(4, 2, 40, ATTN)
-    first = attn.reshape(4, 80, ATTN)
     gains = jnp.pad(jnp.stack([attn_gain, mlp_gain], axis=0), ((0, 14), (0, 88)))
-    gains = jnp.broadcast_to(gains, (4, 16, 128))
-    down = padded(down_weight.T).reshape(40, 4, 2, FEED).transpose(1, 2, 0, 3).reshape(4, 80, FEED)
-    second = jnp.stack([padded(gate_weight), padded(up_weight)], axis=0)
-    second = second.transpose(2, 0, 1, 3).reshape(4, 80, 2 * FEED)
     order = jnp.asarray(feature_order(), low)
-    first, gains, second, x_in, dy_here = group_exchange(
-        first, gains, second, tokens, cotangent, order, 5
+    weights = (query_weight, kv_weight, out_weight.T, gate_weight, up_weight, down_weight.T)
+    first, gains, second, down, x_in, dy_here = group_exchange(
+        weights, gains, tokens, cotangent, order, 5
     )
     w_gate_up = lax.all_gather(second, PLANE, axis=0, tiled=True)
     w_q_kv, w_out_t, gains, dy, down = attention_gather(first, gains.reshape(64, 128), dy_here, down, 6)
-    gains = gains.reshape(64, 16, 128)[:, :2, :40].transpose(1, 0, 2).reshape(2, 2560).astype(jnp.float32)
     dy = dy.reshape(4 * rows, -1)
-    gain_one, gain_two = gains[0][None, :], gains[1][None, :]
-    cosine = jnp.concatenate([cosine, cosine], axis=1)
-    sine = jnp.concatenate([-sine, sine], axis=1)
-    x_mid, xn_all, w_down_t, xn_one, mixed_heads, queries, keys_values, soft_rows = middle(
-        x_in, gain_one, gain_two, cosine, sine, w_q_kv, w_out_t, down, 2
+    cosine, sine = (jnp.asarray(t) for t in tables())
+    x_mid, xn_all, w_down_t, xn_one, mixed_heads, queries, keys_values, soft_rows, gains = middle(
+        x_in, gains, cosine, sine, w_q_kv, w_out_t, down, 2
     )
     xn_all = xn_all.reshape(4 * rows, -1)
     hidden, d_gate_up, sent = feed(xn_all, dy, w_gate_up, w_down_t)
@@ -1366,7 +1459,7 @@
         x_in,
         x_mid,
         dy_here,
-        gain_two,
+        gains,
         soft_rows,
         queries,
         keys_values,
@@ -1374,7 +1467,7 @@
         sine,
         3,
     )
-    attn_out, gain_out, block_out, tokens_grad = plane_sum(
+    query_out, kv_out, out_out, gain_out, block_out, tokens_grad = plane_sum(
         xn_one.reshape(2 * rows, -1),
         d_q_kv,
         d_mid_low,
@@ -1385,18 +1478,20 @@
         x_in,
         x_mid,
         d_mid,
-        gain_one,
+        gains,
         order,
         7,
     )
-    down_out, gate_out, up_out = finish(sent, 8)
+    block_out, tokens_grad, query_out, kv_out, out_out, gain_out, down_out, gate_out, up_out = written(
+        finish(sent, 8), (block_out, tokens_grad, query_out, kv_out, out_out, gain_out)
+    )
     return (
         block_out,
         tokens_grad,
         gain_out[0, :40],
-        attn_out[:, :wide],
-        attn_out[:, wide : wide + 2 * HEAD_DIM],
-        attn_out[:, wide + 2 * HEAD_DIM :].T,
+        query_out,
+        kv_out,
+        out_out.T,
         gain_out[1, :40],
         gate_out,
         up_out,

time: 378 us -> 357 us (0.944)
  local copies, waits for them, and re-layouts: 17.8 us -> 1.27 us
    pallas_call x1, Pallas kernels: 80 us -> 67.6 us  [attention_gather(): pl.pallas_call(attention_gather_kernel, out_shape=[jax.ShapeDtypeStruct((...]
    pallas_call x5 -> x6, Pallas kernels: 228 us -> 237 us  [the longest x1 95.2 us: plane_sum(): pl.pallas_call(plane_sum_kernel, out_shape=[*(jax.ShapeDtypeStruct((40, n...]
    unnamed x21 -> x0, local copies, waits for them, and re-layouts: 5.43 us -> none
    slice x5 -> x0, local copies, waits for them, and re-layouts: 3.92 us -> none  [the longest x1 1.59 us: local(): attn_out[:, wide:wide + 2 * HEAD_DIM]]
  transfers between devices with their start and end apart: 2 -> 2, of which waited for: 0 -> 0; matrix products, arithmetic and copies ran while one was open for 3% -> 0% of each run, Pallas kernels for 74% -> 76%
where the time goes in v5:
time: 357 us; the launch traced here: 351 us
  Pallas kernels  334 us (94%)
  between operations  14.6 us (4%)
    pallas_call x1, Pallas kernels, plane_sum(): pl.pallas_call(plane_sum_kernel, out_shape=[*(jax.ShapeDtypeStruct((40, n...  95.2 us
    pallas_call x1, Pallas kernels, attention_gather(): pl.pallas_call(attention_gather_kernel, out_shape=[jax.ShapeDtypeStruct((...  67.6 us
    pallas_call x1, Pallas kernels, middle(): pl.pallas_call(middle_kernel, out_shape=shapes, in_specs=[HBM] * 2 + [vme...  56.7 us
    pallas_call x1, Pallas kernels, feed_back(): pl.pallas_call(back_kernel, out_shape=shapes, in_specs=[HBM] * 13 + [vmem...  46.8 us
    pallas_call x1, Pallas kernels, feed(): pl.pallas_call(feed_kernel, out_shape=shapes, in_specs=[HBM] * 4, out_spe...  29.6 us
    pallas_call x1, Pallas kernels, group_exchange(): pl.pallas_call(exchange_kernel, out_shape=shapes, in_specs=[vmem] * 10, o...  20 us
    pallas_call x1, Pallas kernels, finish(): pl.pallas_call(finish_kernel, out_shape=buffer, in_specs=[HBM], out_specs...  13.6 us
  transfers between devices with their start and end apart: 2, of which 0 were waited for; matrix products, arithmetic and copies ran while one was open for 0% of the time, Pallas kernels for 76%

profile of v5, /device:TPU:1, one launch (start us, length us, event | category | flops | bytes accessed | tf_op | source)
XLA Modules:
  0.0 351.0 jit_solution(2865435338341232206)
XLA Ops:
  7.2 0.0 all-gather.2.cloned.1.call-start
  7.2 1.3 fusion.5.gain_ref
  8.5 20.0 %shard_map.204 = (bf16[2,160,768]{2,1,0:T(8,128)(2,1)}, bf16[4,16,128]{2,1,0:T(8,128)(2,1)}, bf16[160,1920]{1,0:T(8,128)(2,1)}, bf16[4,80,512]{2,1,0:T(8,128)(2,...) custom-call(bf16[40,1280]{1,0:T(8,128)(2,1)} %q_ref.1, bf16[40,512]{1,0:T(8,128)(2,1)} %kv_ref.1, ...), custom_call_target="tpu_custom_call" | custom-call | tf_op jit(solution)/shard_map/pallas_call | solution.py:167
  28.5 0.0 all-gather.2.cloned.1.call-update
  28.5 0.0 reduce-scatter.2.cloned.1.call-start
  28.6 67.6 %shard_map.205 = (bf16[2560,1792]{1,0:T(8,128)(2,1)}, bf16[2560,1280]{1,0:T(8,128)(2,1)}, bf16[1024,128]{1,0:T(8,128)(2,1)}, bf16[4,128,2560]{2,1,0:T(8,128)(2,1)}, bf16[2,160,512]{2,1,0:T(8,128)(2,1)}) custom-call(bf16[2,160,768]{2,1,0:T(8,128)(2,1)} %get-tuple-element.55.in_hbm, bf16[64,128]{1,0:T(8,128)(2,1)} %bitcast.19, ...), custom_call_target="tpu_custom_call" | custom-call | tf_op jit(solution)/shard_map/pallas_call | solution.py:398
  96.2 56.7 %shard_map.206 = (f32[128,2560]{1,0:T(8,128)}, bf16[4,128,2560]{2,1,0:T(8,128)(2,1)}, bf16[2560,1024]{1,0:T(8,128)(2,1)}, bf16[2,128,2560]{2,1,0:T(8,128)(2,1)},...) custom-call(f32[128,2560]{1,0:T(8,128)} %get-tuple-element.54.x_in, ...), custom_call_target="tpu_custom_call" | custom-call | tf_op jit(solution)/shard_map/pallas_call | solution.py:592
  152.9 0.0 all-gather.2.cloned.1.call-done.g_ref.w_ref
  152.9 29.6 %shard_map.207 = (bf16[512,1024]{1,0:T(8,128)(2,1)}, bf16[512,1920]{1,0:T(8,128)(2,1)}, bf16[2560,2880]{1,0:T(8,128)(2,1)}) custom-call(bf16[512,2560]{1,0:T(8,128)(2,1)} %bitcast.23, bf16[512,2560]{1,0:T(8,128)(2,1)} %bitcast.22, bf16[2560,1920]{1,0:T(8,128)(2,1)} %all-gather.2.cloned.1.call-done.g_ref.w_ref, bf16[2560,1024]{1,0:T(8,128)(2,1)} %get-tuple-element.66.d_ref), custom_call_target="tpu_custom_call" | custom-call | flops 16106127360 | bytes 39845888 | tf_op jit(solution)/shard_map/pallas_call | solution.py:1119
  182.6 0.0 reduce-scatter.2.cloned.1.call-update
  182.6 46.8 %shard_map.209 = (bf16[4,128,2560]{2,1,0:T(8,128)(2,1)}, f32[128,2560]{1,0:T(8,128)}, bf16[128,2560]{1,0:T(8,128)(2,1)}, bf16[128,1792]{1,0:T(8,128)(2,1)}, bf16...) custom-call(bf16[512,1920]{1,0:T(8,128)(2,1)} %get-tuple-element.69.dg_in, bf16[512,1024]{1,0:T(8,128)(2,1)} %get-tuple-element.70.h_in, ...), custom_call_target="tpu_custom_call" | custom-call | tf_op jit(solution)/shard_map/pallas_call | solution.py:1374
  229.4 95.2 %shard_map.210 = (f32[40,1280]{1,0:T(8,128)}, f32[40,512]{1,0:T(8,128)}, f32[40,1280]{1,0:T(8,128)}, f32[16,128]{1,0:T(8,128)}, bf16[128,2560]{1,0:T(8,128)(2,1)}, /*index=5*/bf16[128,2560]{1,0:T(8,128)(2,1)}) custom-call(bf16[256,2560]{1,0:T(8,128)(2,1)} %bitcast.15, bf16[128,1792]{1,0:T(8,128)(2,1)} %get-tuple-element.76.dq_ref, ...), custom_call_target="tpu_custom_call" | custom-call | tf_op jit(solution)/shard_map/pallas_call | solution.py:977
  324.6 0.0 reduce-scatter.2.cloned.1.call-done.s_in
  324.6 13.6 %shard_map.208.l_in = bf16[4,80,1536]{2,1,0:T(8,128)(2,1)} custom-call(bf16[160,2880]{1,0:T(8,128)(2,1)} %reduce-scatter.2.cloned.1.call-done.s_in), custom_call_target="tpu_custom_call" | custom-call | tf_op jit(solution)/shard_map/pallas_call | solution.py:639
  338.2 4.3 %shard_map.211 = (bf16[128,2560]{1,0:T(8,128)(2,1)}, bf16[128,2560]{1,0:T(8,128)(2,1)}, f32[40,1280]{1,0:T(8,128)}, f32[40,512]{1,0:T(8,128)}, f32[40,1280]{1,0:...) custom-call(bf16[4,80,1536]{2,1,0:T(8,128)(2,1)} %shard_map.208.l_in, ...), custom_call_target="tpu_custom_call" | custom-call | tf_op jit(solution)/shard_map/pallas_call | solution.py:678
  342.5 1.3 slice_bitcast_fusion
Async XLA Ops:
  7.2 145.7 %all-gather.2.cloned.1.call-start = ((), (), s32[]{:S(2)}) async-start(), calls=%async_computation.1 | async-start | bytes 10444800 | tf_op jit(solution)/shard_map/all_gather | solution.py:1442
  28.5 296.1 %reduce-scatter.2.cloned.1.call-start = ((), (), s32[]{:S(2)}) async-start(), calls=%async_computation.2 | async-start | bytes 16015360 | tf_op jit(solution)/shard_map/reduce_scatter | solution.py:1451
Sparse Core Ops, SparseCore 0:
  28.6 105.9 all-gather.1
  182.7 130.4 reduce-scatter.1

commit v6 on v5

--- a/solution.py
+++ b/solution.py
@@ -303,10 +303,10 @@
         @pl.when(c == side)
         def _(side=side):
             if side == 0:
-                starts = [(a_ref, 0), (a_ref, 256), (a_ref, 512), (a_ref, 768), (a_ref, 1280)]
+                starts = [(a_ref, 512), (a_ref, 1024), (a_ref, 0), (a_ref, 256), (a_ref, 768)]
             else:
-                starts = [(a_ref, 1536), (o_ref, 0), (o_ref, 256), (o_ref, 512), (o_ref, 1024)]
-            segments = ((0, 0, 256, False), (0, 256, 256, False), (0, 512, 128, True), (1, 0, 512, False), (1, 512, 128, True))
+                starts = [(o_ref, 256), (o_ref, 768), (a_ref, 1536), (o_ref, 0), (o_ref, 512)]
+            segments = ((0, 512, 128, True), (1, 256, 256, True), (0, 0, 256, False), (0, 256, 256, False), (1, 0, 256, False))
             pieces, others = [], {}
             for n, ((h, source, width, shared), (ref, first)) in enumerate(zip(segments, starts)):
                 for part in range(2 if shared else 1):
@@ -513,25 +513,30 @@
     shared.append(remote(mixed_ref.at[c], mixed_ref.at[c], csend.at[1], crecv.at[1], core))
     shared[1].start()
     puts = fetch([(q_ref, q_out), (kv_ref, kv_out), (soft_ref, soft_out), (rows_ref, rows_out)], out_sem)
-    for k in range(5):
-        loads[heads + 2 + k].wait()
-        some = pl.ds(k * 512, 512)
+    mine, other = zl * 2 + c, (1 - zl) * 2 + c
+    parts = [pl.ds(pl.multiple_of(k * half, half), half) for k in (1 - zh, zh)]
+    chunks = [pl.ds(k * 512, 512) for k in range(5)]
+    pair = [
+        [
+            remote(p_ref.at[part, some], landed.at[part, some], psend.at[5 * k + n], precv.at[5 * k + n], far)
+            for n, some in enumerate(chunks)
+        ]
+        for k, part in enumerate(parts)
+    ]
+    for n, some in enumerate(chunks):
+        loads[heads + 2 + n].wait()
         p_ref[:, some] = lax.dot_general(
             mixed_ref[c], wo[some], (((1,), (1,)), ((), ())), preferred_element_type=f32
         ).astype(low)
-    mine, other = zl * 2 + c, (1 - zl) * 2 + c
-    parts = [pl.ds(pl.multiple_of(k * half, half), half) for k in (1 - zh, zh)]
-    pair = [
-        remote(p_ref.at[part], landed.at[part], psend.at[k], precv.at[k], far)
-        for k, part in enumerate(parts)
-    ]
-    for copy in pair:
+        pair[0][n].start()
+    for copy in pair[1]:
         copy.start()
     first_axis()
     away, across = [], []
     for k in range(2):
         part = parts[1 - k]
-        pair[k].wait_recv()
+        for copy in pair[k]:
+            copy.wait_recv()
         first = (zh if k == 0 else 1 - zh) * half
 
         @pl.loop(0, half // step)
@@ -566,7 +571,7 @@
         [(mid_ref, mid_out), (all_ref, all_out), (xn_ref, xn_out), (mixed_ref, mixed_out)],
         out_sem.at[pl.ds(4, 4)],
     )
-    for copy in (*away, *pair):
+    for copy in (*away, *pair[0], *pair[1]):
         copy.wait_send()
     for keep in (*keeps, *puts):
         keep.wait()
@@ -604,8 +609,8 @@
             pltpu.VMEM(x.shape, low),
             dma((2,)),
             dma((heads + 7,)),
-            dma((2,)),
-            dma((2,)),
+            dma((10,)),
+            dma((10,)),
             dma((6,)),
             dma((6,)),
             dma((40,)),
@@ -704,10 +709,10 @@
 
 
 ORDER = (
-    "P0", "yv0", "yv1", "yv2", "xv0", "P1", "xv1", "P2", "xv2", "P3", "yxm0", "yxv3", "Tc", "yxm1",
-    "T0", "xyt0", "xyv4", "xym2", "gv0", "gv1", "gv2", "gv3", "xyt1", "T1", "xym3", "xyt2", "gm0",
-    "gm1", "gm2", "gm3", "xym4", "xyt3", "gt0", "gt1", "gt2", "gt3", "gv4", "Tg", "gm4", "xyt4",
-    "gt4", "To",
+    "P0", "yv0", "xv0", "yv2", "P1", "P2", "xv2", "Tc", "gv0", "gv1", "gv2", "gv3", "xm0", "T0",
+    "yv1", "gm0", "gm1", "gm2", "gm3", "xv1", "ym0", "P3", "ym2", "xv3", "xm1", "xt0", "yv3", "xm2",
+    "ym1", "yt2", "gt0", "gt1", "gt2", "gt3", "gv4", "gm4", "yt0", "xt1", "xm3", "gt4", "ym3",
+    "xv4", "yv4", "T1", "xt2", "Tg", "yt1", "xm4", "ym4", "To", "yt3", "xt3", "yt4", "xt4",
 )
 
 
@@ -1046,13 +1051,16 @@
         for n in range(4):
             some = pl.ds(n * 640, 640)
             loads.append(pltpu.make_async_copy(source.at[some], target.at[some], load_sem.at[1 + len(loads)]))
-            loads[-1].start()
+    for n in range(4):
+        loads[n].start()
     get_xn.wait()
     xn_turned[...] = xn_ref[...].T
     get_dy.wait()
     dy_turned[...] = dy[...].T
     for n in range(4):
         loads[n].wait()
+    for n in range(4, 8):
+        loads[n].start()
     for k in range(units // 256):
         at = pl.ds(k * 256, 256)
         back[:, at] = jnp.dot(dy[...], wd[:, at], preferred_element_type=f32)
@@ -1161,21 +1169,15 @@
     rows = x_ref.shape[0]
     half, step = rows // 2, 16
     heads = soft_ref.shape[0]
-    get_dg, get_h, *gets = fetch(
-        [
-            (dg_in, dg_ref), (h_in, h_ref), (x_in, x_ref), (mid_in, mid_ref), (dy_in, dy_ref),
-            (g_in, g_ref), (soft_in, soft_ref), (q_in, q_ref), (kv_in, kv_ref),
-        ],
-        in_sem,
-    )
+    get_dg = fetch([(dg_in, dg_ref)], in_sem)[0]
     loads = []
     for source, target, first in ((w_ref, w, 0), (d_ref, wd, parts)):
         for n in range(parts):
             some = pl.ds(n * width, width)
             loads.append(pltpu.make_async_copy(source.at[some], target.at[some], wsem.at[first + n]))
-            loads[-1].start()
+    for n in range(2):
+        loads[n].start()
     get_wo = pltpu.make_async_copy(wo_ref, wo, osem)
-    get_wo.start()
     wq = w.at[:, pl.ds(0, wq_ref.shape[1])]
     get_wq = pltpu.make_async_copy(wq_ref, wq, qsem)
     greet([core, far, *chips])
@@ -1253,14 +1255,26 @@
             grad[at, columns(n)] = own[at, columns(n)].astype(f32) + from_far[at, columns(n)].astype(f32)
 
     get_dg.wait()
+    loads[2].start()
     multiply(0)
+    loads[3].start()
     multiply(1)
+    get_h, *gets = fetch(
+        [
+            (h_in, h_ref), (x_in, x_ref), (mid_in, mid_ref), (dy_in, dy_ref),
+            (g_in, g_ref), (soft_in, soft_ref), (q_in, q_ref), (kv_in, kv_ref),
+        ],
+        in_sem.at[pl.ds(1, 8)],
+    )
+    for n in range(parts, 2 * parts):
+        loads[n].start()
     to_chips(0)
     to_far(0, 0)
     multiply(2)
     to_chips(1)
     to_far(1, 0)
     multiply(3)
+    get_wo.start()
     get_wq.start()
     to_chips(2)
     to_far(2, 0)
@@ -1323,17 +1337,19 @@
     kv_part[:, HEAD_DIM:] = d_values.astype(low)
     pair = remote(kv_part, kv_far, fsend, frecv, far)
     pair.start()
+    first_kv = heads * HEAD_DIM
+    get_wq.wait()
+    for k in range(5):
+        some = pl.ds(k * 512, 512)
+        grad[:, some] = across(dq_ref[:, :first_kv], w[some, :first_kv], 1, 1)
     pair.wait()
-    first_kv = heads * HEAD_DIM
     kv = kv_part[...].astype(f32) + kv_far[...].astype(f32)
     kv = kv.astype(low)
     dq_ref[:, first_kv:] = kv
-    halved[:, :first_kv] = dq_ref[:, :first_kv]
-    halved[:, first_kv:] = kv * 0.5
-    get_wq.wait()
+    halved[...] = kv * 0.5
     for k in range(5):
         some = pl.ds(k * 512, 512)
-        d = across(halved[...], w[some, : wq_ref.shape[1]], 1, 1)
+        d = grad[:, some] + across(halved[...], w[some, first_kv : wq_ref.shape[1]], 1, 1)
         grad[:, some] = d
         dx_ref[:, some] = d.astype(low)
 
@@ -1392,7 +1408,7 @@
             pltpu.VMEM((rows, width), f32),
             pltpu.VMEM(keys_values.shape, low),
             pltpu.VMEM(keys_values.shape, low),
-            pltpu.VMEM((rows, wide), low),
+            pltpu.VMEM(keys_values.shape, low),
             pltpu.VMEM((8, width), f32),
             dma((8,)),
             dma((24,)),

time: 357 us -> 355 us (level)
    pallas_call x1, Pallas kernels: 56.7 us -> 48.6 us  [middle(): pl.pallas_call(middle_kernel, out_shape=shapes, in_specs=[HBM] * 2 + [vme...]
    pallas_call x1, Pallas kernels: 67.6 us -> 74.5 us  [attention_gather(): pl.pallas_call(attention_gather_kernel, out_shape=[jax.ShapeDtypeStruct((...]
where the time goes in v6:
time: 355 us; the launch traced here: 348 us
  Pallas kernels  331 us (93%)
  between operations  14.6 us (4%)
    pallas_call x1, Pallas kernels, plane_sum(): pl.pallas_call(plane_sum_kernel, out_shape=[*(jax.ShapeDtypeStruct((40, n...  98.3 us
    pallas_call x1, Pallas kernels, attention_gather(): pl.pallas_call(attention_gather_kernel, out_shape=[jax.ShapeDtypeStruct((...  74.5 us
    pallas_call x1, Pallas kernels, middle(): pl.pallas_call(middle_kernel, out_shape=shapes, in_specs=[HBM] * 2 + [vme...  48.6 us
    pallas_call x1, Pallas kernels, feed_back(): pl.pallas_call(back_kernel, out_shape=shapes, in_specs=[HBM] * 13 + [vmem...  44.4 us
    pallas_call x1, Pallas kernels, feed(): pl.pallas_call(feed_kernel, out_shape=shapes, in_specs=[HBM] * 4, out_spe...  27.5 us
    pallas_call x1, Pallas kernels, group_exchange(): pl.pallas_call(exchange_kernel, out_shape=shapes, in_specs=[vmem] * 10, o...  20 us
    pallas_call x1, Pallas kernels, finish(): pl.pallas_call(finish_kernel, out_shape=buffer, in_specs=[HBM], out_specs...  13.4 us
  transfers between devices with their start and end apart: 2, of which 0 were waited for; matrix products, arithmetic and copies ran while one was open for 0% of the time, Pallas kernels for 76%

profile of v6, /device:TPU:1, one launch (start us, length us, event | category | flops | bytes accessed | tf_op | source)
XLA Modules:
  0.0 348.2 jit_solution(9802754571843169505)
XLA Ops:
  7.2 0.0 all-gather.2.cloned.1.call-start
  7.2 1.3 fusion.5.gain_ref
  8.5 20.0 %shard_map.204 = (bf16[2,160,768]{2,1,0:T(8,128)(2,1)}, bf16[4,16,128]{2,1,0:T(8,128)(2,1)}, bf16[160,1920]{1,0:T(8,128)(2,1)}, bf16[4,80,512]{2,1,0:T(8,128)(2,...) custom-call(bf16[40,1280]{1,0:T(8,128)(2,1)} %q_ref.1, bf16[40,512]{1,0:T(8,128)(2,1)} %kv_ref.1, ...), custom_call_target="tpu_custom_call" | custom-call | tf_op jit(solution)/shard_map/pallas_call | solution.py:167
  28.5 0.0 all-gather.2.cloned.1.call-update
  28.5 0.0 reduce-scatter.2.cloned.1.call-start
  28.6 74.5 %shard_map.205 = (bf16[2560,1792]{1,0:T(8,128)(2,1)}, bf16[2560,1280]{1,0:T(8,128)(2,1)}, bf16[1024,128]{1,0:T(8,128)(2,1)}, bf16[4,128,2560]{2,1,0:T(8,128)(2,1)}, bf16[2,160,512]{2,1,0:T(8,128)(2,1)}) custom-call(bf16[2,160,768]{2,1,0:T(8,128)(2,1)} %get-tuple-element.55.in_hbm, bf16[64,128]{1,0:T(8,128)(2,1)} %bitcast.19, ...), custom_call_target="tpu_custom_call" | custom-call | tf_op jit(solution)/shard_map/pallas_call | solution.py:398
  103.0 48.6 %shard_map.206 = (f32[128,2560]{1,0:T(8,128)}, bf16[4,128,2560]{2,1,0:T(8,128)(2,1)}, bf16[2560,1024]{1,0:T(8,128)(2,1)}, bf16[2,128,2560]{2,1,0:T(8,128)(2,1)},...) custom-call(f32[128,2560]{1,0:T(8,128)} %get-tuple-element.54.x_in, ...), custom_call_target="tpu_custom_call" | custom-call | tf_op jit(solution)/shard_map/pallas_call | solution.py:597
  151.7 0.0 all-gather.2.cloned.1.call-done.g_ref.w_ref
  151.7 27.5 %shard_map.207 = (bf16[512,1024]{1,0:T(8,128)(2,1)}, bf16[512,1920]{1,0:T(8,128)(2,1)}, bf16[2560,2880]{1,0:T(8,128)(2,1)}) custom-call(bf16[512,2560]{1,0:T(8,128)(2,1)} %bitcast.23, bf16[512,2560]{1,0:T(8,128)(2,1)} %bitcast.22, bf16[2560,1920]{1,0:T(8,128)(2,1)} %all-gather.2.cloned.1.call-done.g_ref.w_ref, bf16[2560,1024]{1,0:T(8,128)(2,1)} %get-tuple-element.66.d_ref), custom_call_target="tpu_custom_call" | custom-call | flops 16106127360 | bytes 39845888 | tf_op jit(solution)/shard_map/pallas_call | solution.py:1127
  179.2 0.0 reduce-scatter.2.cloned.1.call-update
  179.2 44.4 %shard_map.209 = (bf16[4,128,2560]{2,1,0:T(8,128)(2,1)}, f32[128,2560]{1,0:T(8,128)}, bf16[128,2560]{1,0:T(8,128)(2,1)}, bf16[128,1792]{1,0:T(8,128)(2,1)}, bf16...) custom-call(bf16[512,1920]{1,0:T(8,128)(2,1)} %get-tuple-element.69.dg_in, bf16[512,1024]{1,0:T(8,128)(2,1)} %get-tuple-element.70.h_in, ...), custom_call_target="tpu_custom_call" | custom-call | tf_op jit(solution)/shard_map/pallas_call | solution.py:1390
  223.7 98.3 %shard_map.210 = (f32[40,1280]{1,0:T(8,128)}, f32[40,512]{1,0:T(8,128)}, f32[40,1280]{1,0:T(8,128)}, f32[16,128]{1,0:T(8,128)}, bf16[128,2560]{1,0:T(8,128)(2,1)}, /*index=5*/bf16[128,2560]{1,0:T(8,128)(2,1)}) custom-call(bf16[256,2560]{1,0:T(8,128)(2,1)} %bitcast.15, bf16[128,1792]{1,0:T(8,128)(2,1)} %get-tuple-element.76.dq_ref, ...), custom_call_target="tpu_custom_call" | custom-call | tf_op jit(solution)/shard_map/pallas_call | solution.py:982
  322.0 0.0 reduce-scatter.2.cloned.1.call-done.s_in
  322.0 13.4 %shard_map.208.l_in = bf16[4,80,1536]{2,1,0:T(8,128)(2,1)} custom-call(bf16[160,2880]{1,0:T(8,128)(2,1)} %reduce-scatter.2.cloned.1.call-done.s_in), custom_call_target="tpu_custom_call" | custom-call | tf_op jit(solution)/shard_map/pallas_call | solution.py:644
  335.4 4.3 %shard_map.211 = (bf16[128,2560]{1,0:T(8,128)(2,1)}, bf16[128,2560]{1,0:T(8,128)(2,1)}, f32[40,1280]{1,0:T(8,128)}, f32[40,512]{1,0:T(8,128)}, f32[40,1280]{1,0:...) custom-call(bf16[4,80,1536]{2,1,0:T(8,128)(2,1)} %shard_map.208.l_in, ...), custom_call_target="tpu_custom_call" | custom-call | tf_op jit(solution)/shard_map/pallas_call | solution.py:683
  339.7 1.3 slice_bitcast_fusion
Async XLA Ops:
  7.2 144.5 %all-gather.2.cloned.1.call-start = ((), (), s32[]{:S(2)}) async-start(), calls=%async_computation.1 | async-start | bytes 10444800 | tf_op jit(solution)/shard_map/all_gather | solution.py:1458
  28.5 293.5 %reduce-scatter.2.cloned.1.call-start = ((), (), s32[]{:S(2)}) async-start(), calls=%async_computation.2 | async-start | bytes 16015360 | tf_op jit(solution)/shard_map/reduce_scatter | solution.py:1467
Sparse Core Ops, SparseCore 0:
  28.6 95.9 all-gather.1
  179.4 128.6 reduce-scatter.1

commit v7 on v6

--- a/solution.py
+++ b/solution.py
@@ -727,9 +727,9 @@
     y, x, c, zl, zh = (lax.axis_index(k) for k in ("y", "x", "c", "zl", "zh"))
     core, chip, far_peer = {"c": 1 - c}, {"zl": 1 - zl}, {"zh": 1 - zh}
     chips = [{"zl": 1 - zl, "zh": k} for k in range(2)]
-    get_p, get_t, get_left, get_right, *gets = fetch(
+    get_left, get_right, get_p, get_t, *gets = fetch(
         [
-            (p_in, p_ref), (t_in, t_ref), (left_in, left), (right_in, right_o), (x_in, x_ref),
+            (left_in, left), (right_in, right_o), (p_in, p_ref), (t_in, t_ref), (x_in, x_ref),
             (mid_in, mid_ref), (dmid_in, dmid_ref), (g_in, g_ref), (order_in, order_ref),
         ],
         in_sem,
@@ -915,8 +915,8 @@
         copy.wait()
     for copy in shared:
         copy.wait_recv()
-    for get in (get_left, get_right, *gets):
-        get.wait()
+    get_left.wait()
+    get_right.wait()
     named = {"x": x_first, "y": y_first, "g": gain}
     acts = {"v": out_via, "m": out_main, "t": take}
     token_acts = {
@@ -930,6 +930,8 @@
         if word[0] == "P":
             products(int(word[1]))
         elif word[0] == "T":
+            while gets:
+                gets.pop().wait()
             token_acts[word]()
         else:
             for name in word[:-2]:

time: 355 us -> 355 us (level)
  no operation moved by 1% of the time
where the time goes in v7:
time: 355 us; the launch traced here: 349 us
  Pallas kernels  331 us (93%)
  between operations  14.6 us (4%)
    pallas_call x1, Pallas kernels, plane_sum(): pl.pallas_call(plane_sum_kernel, out_shape=[*(jax.ShapeDtypeStruct((40, n...  98.8 us
    pallas_call x1, Pallas kernels, attention_gather(): pl.pallas_call(attention_gather_kernel, out_shape=[jax.ShapeDtypeStruct((...  74.5 us
    pallas_call x1, Pallas kernels, middle(): pl.pallas_call(middle_kernel, out_shape=shapes, in_specs=[HBM] * 2 + [vme...  48.6 us
    pallas_call x1, Pallas kernels, feed_back(): pl.pallas_call(back_kernel, out_shape=shapes, in_specs=[HBM] * 13 + [vmem...  44.4 us
    pallas_call x1, Pallas kernels, feed(): pl.pallas_call(feed_kernel, out_shape=shapes, in_specs=[HBM] * 4, out_spe...  27.5 us
    pallas_call x1, Pallas kernels, group_exchange(): pl.pallas_call(exchange_kernel, out_shape=shapes, in_specs=[vmem] * 10, o...  20 us
    pallas_call x1, Pallas kernels, finish(): pl.pallas_call(finish_kernel, out_shape=buffer, in_specs=[HBM], out_specs...  13.4 us
  transfers between devices with their start and end apart: 2, of which 0 were waited for; matrix products, arithmetic and copies ran while one was open for 0% of the time, Pallas kernels for 76%

profile of v7, /device:TPU:1, one launch (start us, length us, event | category | flops | bytes accessed | tf_op | source)
XLA Modules:
  0.0 348.7 jit_solution(3969306465443412661)
XLA Ops:
  7.2 0.0 all-gather.2.cloned.1.call-start
  7.2 1.3 fusion.5.gain_ref
  8.5 20.0 %shard_map.204 = (bf16[2,160,768]{2,1,0:T(8,128)(2,1)}, bf16[4,16,128]{2,1,0:T(8,128)(2,1)}, bf16[160,1920]{1,0:T(8,128)(2,1)}, bf16[4,80,512]{2,1,0:T(8,128)(2,...) custom-call(bf16[40,1280]{1,0:T(8,128)(2,1)} %q_ref.1, bf16[40,512]{1,0:T(8,128)(2,1)} %kv_ref.1, ...), custom_call_target="tpu_custom_call" | custom-call | tf_op jit(solution)/shard_map/pallas_call | solution.py:167
  28.5 0.0 all-gather.2.cloned.1.call-update
  28.5 0.0 reduce-scatter.2.cloned.1.call-start
  28.6 74.5 %shard_map.205 = (bf16[2560,1792]{1,0:T(8,128)(2,1)}, bf16[2560,1280]{1,0:T(8,128)(2,1)}, bf16[1024,128]{1,0:T(8,128)(2,1)}, bf16[4,128,2560]{2,1,0:T(8,128)(2,1)}, bf16[2,160,512]{2,1,0:T(8,128)(2,1)}) custom-call(bf16[2,160,768]{2,1,0:T(8,128)(2,1)} %get-tuple-element.55.in_hbm, bf16[64,128]{1,0:T(8,128)(2,1)} %bitcast.19, ...), custom_call_target="tpu_custom_call" | custom-call | tf_op jit(solution)/shard_map/pallas_call | solution.py:398
  103.0 48.6 %shard_map.206 = (f32[128,2560]{1,0:T(8,128)}, bf16[4,128,2560]{2,1,0:T(8,128)(2,1)}, bf16[2560,1024]{1,0:T(8,128)(2,1)}, bf16[2,128,2560]{2,1,0:T(8,128)(2,1)},...) custom-call(f32[128,2560]{1,0:T(8,128)} %get-tuple-element.54.x_in, ...), custom_call_target="tpu_custom_call" | custom-call | tf_op jit(solution)/shard_map/pallas_call | solution.py:597
  151.7 0.0 all-gather.2.cloned.1.call-done.g_ref.w_ref
  151.7 27.5 %shard_map.207 = (bf16[512,1024]{1,0:T(8,128)(2,1)}, bf16[512,1920]{1,0:T(8,128)(2,1)}, bf16[2560,2880]{1,0:T(8,128)(2,1)}) custom-call(bf16[512,2560]{1,0:T(8,128)(2,1)} %bitcast.23, bf16[512,2560]{1,0:T(8,128)(2,1)} %bitcast.22, bf16[2560,1920]{1,0:T(8,128)(2,1)} %all-gather.2.cloned.1.call-done.g_ref.w_ref, bf16[2560,1024]{1,0:T(8,128)(2,1)} %get-tuple-element.66.d_ref), custom_call_target="tpu_custom_call" | custom-call | flops 16106127360 | bytes 39845888 | tf_op jit(solution)/shard_map/pallas_call | solution.py:1129
  179.2 0.0 reduce-scatter.2.cloned.1.call-update
  179.2 44.4 %shard_map.209 = (bf16[4,128,2560]{2,1,0:T(8,128)(2,1)}, f32[128,2560]{1,0:T(8,128)}, bf16[128,2560]{1,0:T(8,128)(2,1)}, bf16[128,1792]{1,0:T(8,128)(2,1)}, bf16...) custom-call(bf16[512,1920]{1,0:T(8,128)(2,1)} %get-tuple-element.69.dg_in, bf16[512,1024]{1,0:T(8,128)(2,1)} %get-tuple-element.70.h_in, ...), custom_call_target="tpu_custom_call" | custom-call | tf_op jit(solution)/shard_map/pallas_call | solution.py:1392
  223.7 98.8 %shard_map.210 = (f32[40,1280]{1,0:T(8,128)}, f32[40,512]{1,0:T(8,128)}, f32[40,1280]{1,0:T(8,128)}, f32[16,128]{1,0:T(8,128)}, bf16[128,2560]{1,0:T(8,128)(2,1)}, /*index=5*/bf16[128,2560]{1,0:T(8,128)(2,1)}) custom-call(bf16[256,2560]{1,0:T(8,128)(2,1)} %bitcast.15, bf16[128,1792]{1,0:T(8,128)(2,1)} %get-tuple-element.76.dq_ref, ...), custom_call_target="tpu_custom_call" | custom-call | tf_op jit(solution)/shard_map/pallas_call | solution.py:984
  322.5 0.0 reduce-scatter.2.cloned.1.call-done.s_in
  322.5 13.4 %shard_map.208.l_in = bf16[4,80,1536]{2,1,0:T(8,128)(2,1)} custom-call(bf16[160,2880]{1,0:T(8,128)(2,1)} %reduce-scatter.2.cloned.1.call-done.s_in), custom_call_target="tpu_custom_call" | custom-call | tf_op jit(solution)/shard_map/pallas_call | solution.py:644
  335.9 4.3 %shard_map.211 = (bf16[128,2560]{1,0:T(8,128)(2,1)}, bf16[128,2560]{1,0:T(8,128)(2,1)}, f32[40,1280]{1,0:T(8,128)}, f32[40,512]{1,0:T(8,128)}, f32[40,1280]{1,0:...) custom-call(bf16[4,80,1536]{2,1,0:T(8,128)(2,1)} %shard_map.208.l_in, ...), custom_call_target="tpu_custom_call" | custom-call | tf_op jit(solution)/shard_map/pallas_call | solution.py:683
  340.1 1.3 slice_bitcast_fusion
Async XLA Ops:
  7.2 144.5 %all-gather.2.cloned.1.call-start = ((), (), s32[]{:S(2)}) async-start(), calls=%async_computation.1 | async-start | bytes 10444800 | tf_op jit(solution)/shard_map/all_gather | solution.py:1460
  28.5 294.0 %reduce-scatter.2.cloned.1.call-start = ((), (), s32[]{:S(2)}) async-start(), calls=%async_computation.2 | async-start | bytes 16015360 | tf_op jit(solution)/shard_map/reduce_scatter | solution.py:1469
Sparse Core Ops, SparseCore 0:
  28.6 95.9 all-gather.1
  179.4 130.3 reduce-scatter.1
